TPU v7x, 32 devices: a whole 2x2x4 slice. The times are simulated.
32 devices in a mesh: ens: 2 (over y), lon: 16 (over z, x, core).
Axes of the slice: x: 2, y: 2, z: 4, core: 2. Of those that a mesh axis runs over, the one named last changes fastest.
Arguments:
- final_cot: float32 [10, 256, 2048], P('ens', 'lon'), parts along dimension 0, may hold values from -6 to 6
- strains: bfloat16 [16, 3, 256, 2048], P('ens', None, 'lon'), parts along dimension 0, may hold values from -6 to 6
- strength: float32 [256, 2048], P('lon'), may hold values from 0.25 to 1
- mass: float32 [256, 2048], P('lon'), may hold values from 1 to 4
- ice_mask: int32 [256, 2048], P('lon'), may hold values 0 or 1
- partner: int32 [256], P('lon'), may hold values from 0 to 255, as said below
Outputs:
- initial_cot: float32 [10, 256, 2048], P('ens', 'lon'), parts along dimension 0
There are 2 independent parts, one for each index of `ens`. A program takes and returns all parts, laid end to end along the dimension named above; an argument that names none is the same for every part. Nothing has to cross between parts.
Inputs may be any that keep to these rules, and one draw needn't show every extreme that they name: Columns form 256 // 16 aligned blocks of 16; the partners of the columns of block b are exactly the columns of block 15 - b, and the partner of a column's partner is the column itself.
All inputs are finite; a program needn't handle non-finite values. No bound on the sum of `ice_mask` on one device may be relied on, other than what follows from the above.
Results may differ from a plain program's by a relative error of at most 0.0003.
Values may be sent and summed in bfloat16 or wider, within the bound.
No kernel may reach another device: no remote copies, remote signals or barrier semaphores. Data moves between devices by JAX's collectives and lax.ppermute only.
A program may use at most 64 MiB of HBM per device.

v0:
```python
import jax
import jax.numpy as jnp
from jax import lax
from jax.sharding import PartitionSpec as P

relax_keep = 5.0 / 6.0
relax_take = 1.0 / 6.0
inertia = 5.0
coriolis = 0.5
delta_floor = 0.5
ellipse_inv = 0.25


def passed_along(value, axis, steps):
    count = lax.axis_size(axis)
    pairs = [(source, (source + steps) % count) for source in range(count)]
    return lax.ppermute(value, axis, pairs)


def viscosity(saved, strength):
    rates = saved.astype(jnp.float32)
    delta = jnp.sqrt(
        rates[0] * rates[0] + ellipse_inv * (rates[1] * rates[1] + rates[2] * rates[2])
    )
    zeta = strength / (2.0 * jnp.maximum(delta, delta_floor))
    return (zeta, ellipse_inv * zeta)


def below(field):
    return jnp.concatenate([jnp.zeros_like(field[:, :1]), field[:, :-1]], axis=1)


def stresses(vel_u, vel_v, sig_one, sig_two, sig_shear, next_cols, zeta, eta):
    grad_ux = jnp.concatenate([vel_u[1:], next_cols[0]], 0) - vel_u
    grad_vx = jnp.concatenate([vel_v[1:], next_cols[1]], 0) - vel_v
    grad_uy = vel_u - below(vel_u)
    grad_vy = vel_v - below(vel_v)
    new_one = relax_keep * sig_one + relax_take * zeta * (grad_ux + grad_vy)
    new_two = relax_keep * sig_two + relax_take * eta * (grad_ux - grad_vy)
    new_shear = relax_keep * sig_shear + relax_take * eta * (grad_uy + grad_vx)
    return (new_one, new_two, new_shear)


def momentum(vel_u, vel_v, new_one, new_two, new_shear, prev_cols, fold_rows, wet, mass):
    total = new_one + new_two
    differ = new_one - new_two
    prev_total = prev_cols[0] + prev_cols[1]
    fold_differ = fold_rows[0] - fold_rows[1]
    fold_shear = -fold_rows[2]
    force_x = 0.5 * (total - jnp.concatenate([prev_total, total[:-1]], 0)) + (
        jnp.concatenate([new_shear[:, 1:], fold_shear[:, None]], 1) - new_shear
    )
    force_y = 0.5 * (jnp.concatenate([differ[:, 1:], fold_differ[:, None]], 1) - differ) + (
        new_shear - jnp.concatenate([prev_cols[2], new_shear[:-1]], 0)
    )
    out_u = wet * (inertia * vel_u + force_x / mass + coriolis * vel_v) / (1.0 + inertia)
    out_v = wet * (inertia * vel_v + force_y / mass - coriolis * vel_u) / (1.0 + inertia)
    return (out_u, out_v)


def pull_momentum(adjoint, wet, mass):
    columns = adjoint.shape[1]
    rows_lat = adjoint.shape[2]
    flat = jnp.zeros((columns, rows_lat), jnp.float32)
    edge_zero = jnp.zeros((3, 1, rows_lat), jnp.float32)
    fold_zero = jnp.zeros((3, columns), jnp.float32)
    _, pull_force = jax.vjp(
        lambda a, b, c, d, e, f, g: momentum(a, b, c, d, e, f, g, wet, mass),
        flat,
        flat,
        flat,
        flat,
        flat,
        edge_zero,
        fold_zero,
    )
    return pull_force((adjoint[0], adjoint[1]))


def pull_stresses(stress_cot, zeta, eta):
    columns = stress_cot.shape[1]
    rows_lat = stress_cot.shape[2]
    flat = jnp.zeros((columns, rows_lat), jnp.float32)
    next_zero = jnp.zeros((2, 1, rows_lat), jnp.float32)
    _, pull_stress = jax.vjp(
        lambda a, b, c, d, e, f: stresses(a, b, c, d, e, f, zeta, eta),
        flat,
        flat,
        flat,
        flat,
        flat,
        next_zero,
    )
    return pull_stress((stress_cot[0], stress_cot[1], stress_cot[2]))


def on_device(final_cot, strains, strength, mass, ice_mask, partner):
    wet = ice_mask.astype(jnp.float32)
    count = strains.shape[0]
    adjoint = final_cot
    for cycle_at in reversed(range(count)):
        zeta, eta = viscosity(strains[cycle_at], strength)
        back = pull_momentum(adjoint, wet, mass)
        from_east = passed_along(back[5], "lon", -1)
        whole_row = lax.all_gather(back[6], "lon", axis=1, tiled=True)
        fold_add = jnp.take(whole_row, partner, axis=1)
        stress_cot = jnp.stack([adjoint[2] + back[2], adjoint[3] + back[3], adjoint[4] + back[4]])
        stress_cot = stress_cot.at[:, -1:, :].add(from_east)
        stress_cot = stress_cot.at[:, :, -1].add(fold_add)
        front = pull_stresses(stress_cot, zeta, eta)
        from_west = passed_along(front[5], "lon", 1)
        velocity_cot = (
            jnp.stack([back[0] + front[0], back[1] + front[1]]).at[:, :1, :].add(from_west)
        )
        adjoint = jnp.concatenate([velocity_cot, jnp.stack([front[2], front[3], front[4]])], 0)
    return adjoint


def solution(mesh):
    return jax.shard_map(
        on_device,
        mesh=mesh,
        in_specs=(
            P("ens", "lon", None),
            P("ens", None, "lon", None),
            P("lon", None),
            P("lon", None),
            P("lon", None),
            P("lon"),
        ),
        out_specs=P("ens", "lon", None),
        check_vma=False,
    )
```

profile of v0, /device:TPU:0, one launch (start us, length us, event | category | flops | bytes accessed | tf_op | source)
XLA Modules:
  0.0 325.0 jit_solution(10606465573201489993)
XLA Ops:
  1.8 5.4 %collective-permute-start = (f32[3,1,2048]{2,1,0:T(1,128)}, f32[3,1,2048]{2,1,0:T(1,128)}, u32[]{:S(2)}, u32[]{:S(2)}) collective-permute-start(f32[3,1,2048]{2,1,0:T(1,128)} %pad_add_fusion.23), channel_id=1, source_target_pairs={{0,15},{1,0},{2,1},{3,2},{4,3},{5,4},{6,5},{7,6},{8,7},{9,8},{10,9... | collective-permute-start | bytes 73736 | tf_op jit(solution)/shard_map/ppermute | solution.py:17
  8.8 17.7 %all-gather = f32[16,16,3]{1,2,0:T(4,128)S(1)} all-gather(f32[1,16,3]{1,2,0:T(4,128)S(1)} %add_bitcast_fusion.44), channel_id=1, replica_groups=mesh['ens'=2,'lon'=16] {'lon'}, dimensions={0}, use_global_device_ids=true | all-gather | bytes 3264 | tf_op jit(solution)/shard_map/all_gather | solution.py:105
  27.4 2.6 slice_convert_fusion
  38.2 3.6 %collective-permute-done.1 = f32[2,1,2048]{2,0,1:T(2,128)S(1)} collective-permute-done((f32[2,1,2048]{2,0,1:T(2,128)S(1)}, f32[2,1,2048]{2,0,1:T(2,128)S(1)}, u32[]{:S(2)}, u32[]{:S(2)}) %collective-permute-start.1) | collective-permute-done | bytes 16416 | tf_op jit(solution)/shard_map/ppermute | solution.py:17
  46.7 18.6 %all-gather.1 = f32[16,16,3]{1,2,0:T(4,128)} all-gather(f32[1,16,3]{1,2,0:T(4,128)S(1)} %add_bitcast_fusion.43), channel_id=1, replica_groups=mesh['ens'=2,'lon'=16] {'lon'}, dimensions={0}, use_global_device_ids=true | all-gather | bytes 3264 | tf_op jit(solution)/shard_map/all_gather | solution.py:105
  66.9 2.2 gather_fusion.1
  70.4 1.9 collective-permute-start.2
  75.7 1.7 scatter-add.85
  84.0 3.9 %collective-permute-done.3 = f32[2,1,2048]{2,0,1:T(2,128)S(1)} collective-permute-done((f32[2,1,2048]{2,0,1:T(2,128)S(1)}, f32[2,1,2048]{2,0,1:T(2,128)S(1)}, u32[]{:S(2)}, u32[]{:S(2)}) %collective-permute-start.3) | collective-permute-done | bytes 16416 | tf_op jit(solution)/shard_map/ppermute | solution.py:17
  91.6 18.9 %all-gather.2 = f32[16,16,3]{1,2,0:T(4,128)} all-gather(f32[1,16,3]{1,2,0:T(4,128)S(1)} %add_bitcast_fusion.42), channel_id=1, replica_groups=mesh['ens'=2,'lon'=16] {'lon'}, dimensions={0}, use_global_device_ids=true | all-gather | bytes 3264 | tf_op jit(solution)/shard_map/all_gather | solution.py:105
  113.4 1.7 collective-permute-start.4
  118.3 1.7 scatter-add.90
  126.6 3.9 %collective-permute-done.5 = f32[2,1,2048]{2,0,1:T(2,128)S(1)} collective-permute-done((f32[2,1,2048]{2,0,1:T(2,128)S(1)}, f32[2,1,2048]{2,0,1:T(2,128)S(1)}, u32[]{:S(2)}, u32[]{:S(2)}) %collective-permute-start.5) | collective-permute-done | bytes 16416 | tf_op jit(solution)/shard_map/ppermute | solution.py:17
  133.6 17.3 %all-gather.3 = f32[16,16,3]{1,2,0:T(4,128)S(1)} all-gather(f32[1,16,3]{1,2,0:T(4,128)S(1)} %add_bitcast_fusion.41), channel_id=1, replica_groups=mesh['ens'=2,'lon'=16] {'lon'}, dimensions={0}, use_global_device_ids=true | all-gather | bytes 3264 | tf_op jit(solution)/shard_map/all_gather | solution.py:105
  151.8 1.9 collective-permute-start.6
  156.9 1.7 scatter-add.95
  165.2 3.9 %collective-permute-done.7 = f32[2,1,2048]{2,0,1:T(2,128)S(1)} collective-permute-done((f32[2,1,2048]{2,0,1:T(2,128)S(1)}, f32[2,1,2048]{2,0,1:T(2,128)S(1)}, u32[]{:S(2)}, u32[]{:S(2)}) %collective-permute-start.7) | collective-permute-done | bytes 16416 | tf_op jit(solution)/shard_map/ppermute | solution.py:17
  172.2 17.3 %all-gather.4 = f32[16,16,3]{1,2,0:T(4,128)S(1)} all-gather(f32[1,16,3]{1,2,0:T(4,128)S(1)} %add_bitcast_fusion.40), channel_id=1, replica_groups=mesh['ens'=2,'lon'=16] {'lon'}, dimensions={0}, use_global_device_ids=true | all-gather | bytes 3264 | tf_op jit(solution)/shard_map/all_gather | solution.py:105
  190.4 1.9 collective-permute-start.8
  195.5 1.7 scatter-add.100
  203.8 3.9 %collective-permute-done.9 = f32[2,1,2048]{2,0,1:T(2,128)S(1)} collective-permute-done((f32[2,1,2048]{2,0,1:T(2,128)S(1)}, f32[2,1,2048]{2,0,1:T(2,128)S(1)}, u32[]{:S(2)}, u32[]{:S(2)}) %collective-permute-start.9) | collective-permute-done | bytes 16416 | tf_op jit(solution)/shard_map/ppermute | solution.py:17
  210.8 17.3 %all-gather.5 = f32[16,16,3]{1,2,0:T(4,128)S(1)} all-gather(f32[1,16,3]{1,2,0:T(4,128)S(1)} %add_bitcast_fusion.39), channel_id=1, replica_groups=mesh['ens'=2,'lon'=16] {'lon'}, dimensions={0}, use_global_device_ids=true | all-gather | bytes 3264 | tf_op jit(solution)/shard_map/all_gather | solution.py:105
  229.0 1.9 collective-permute-start.10
  234.1 1.7 scatter-add.105
  242.4 3.9 %collective-permute-done.11 = f32[2,1,2048]{2,0,1:T(2,128)S(1)} collective-permute-done((f32[2,1,2048]{2,0,1:T(2,128)S(1)}, f32[2,1,2048]{2,0,1:T(2,128)S(1)}, u32[]{:S(2)}, u32[]{:S(2)}) %collective-permute-start.11) | collective-permute-done | bytes 16416 | tf_op jit(solution)/shard_map/ppermute | solution.py:17
  249.4 17.3 %all-gather.6 = f32[16,16,3]{1,2,0:T(4,128)S(1)} all-gather(f32[1,16,3]{1,2,0:T(4,128)S(1)} %add_bitcast_fusion.38), channel_id=1, replica_groups=mesh['ens'=2,'lon'=16] {'lon'}, dimensions={0}, use_global_device_ids=true | all-gather | bytes 3264 | tf_op jit(solution)/shard_map/all_gather | solution.py:105
  267.6 2.1 collective-permute-start.12
  272.9 1.7 scatter-add.110
  281.1 3.9 %collective-permute-done.13 = f32[2,1,2048]{2,0,1:T(2,128)S(1)} collective-permute-done((f32[2,1,2048]{2,0,1:T(2,128)S(1)}, f32[2,1,2048]{2,0,1:T(2,128)S(1)}, u32[]{:S(2)}, u32[]{:S(2)}) %collective-permute-start.13) | collective-permute-done | bytes 16416 | tf_op jit(solution)/shard_map/ppermute | solution.py:17
  288.2 17.3 %all-gather.7 = f32[16,16,3]{1,2,0:T(4,128)S(1)} all-gather(f32[1,16,3]{1,2,0:T(4,128)S(1)} %add_bitcast_fusion.37), channel_id=1, replica_groups=mesh['ens'=2,'lon'=16] {'lon'}, dimensions={0}, use_global_device_ids=true | all-gather | bytes 3264 | tf_op jit(solution)/shard_map/all_gather | solution.py:105
  306.4 1.9 collective-permute-start.14
  318.3 5.6 %collective-permute-done.15 = f32[2,1,2048]{2,0,1:T(2,128)S(1)} collective-permute-done((f32[2,1,2048]{2,0,1:T(2,128)S(1)}, f32[2,1,2048]{2,0,1:T(2,128)S(1)}, u32[]{:S(2)}, u32[]{:S(2)}) %collective-permute-start.15) | collective-permute-done | bytes 16416 | tf_op jit(solution)/shard_map/ppermute | solution.py:17
  (294 shorter events, 115.8 us)
Async XLA Ops:
  1.8 31.2 %collective-permute-start = (f32[3,1,2048]{2,1,0:T(1,128)}, f32[3,1,2048]{2,1,0:T(1,128)}, u32[]{:S(2)}, u32[]{:S(2)}) collective-permute-start(f32[3,1,2048]{2,1,0:T(1,128)} %pad_add_fusion.23), channel_id=1, source_target_pairs={{0,15},{1,0},{2,1},{3,2},{4,3},{5,4},{6,5},{7,6},{8,7},{9,8},{10,9... | collective-permute-start | bytes 73736 | tf_op jit(solution)/shard_map/ppermute | solution.py:17
  8.6 21.4 %copy-start.6 = (s32[1024]{0:T(1024)}, s32[1024]{0:T(1024)S(1)}, u32[]{:S(2)}) copy-start(s32[1024]{0:T(1024)S(1)} %pad_clamp_fusion) | copy-start | bytes 12292
  29.9 4.4 %copy-start.2 = (f32[16,2048]{1,0:T(8,128)S(1)}, f32[16,2048]{1,0:T(8,128)}, u32[]{:S(2)}) copy-start(f32[16,2048]{1,0:T(8,128)} %param.58) | copy-start | bytes 393220
  32.6 3.7 %copy-start = (s32[16,2048]{1,0:T(8,128)S(1)}, s32[16,2048]{1,0:T(8,128)}, u32[]{:S(2)}) copy-start(s32[16,2048]{1,0:T(8,128)} %param.60) | copy-start | bytes 393220
  34.3 3.1 copy-start.4
  35.7 7.6 %copy-start.1 = (f32[16,2048]{1,0:T(8,128)S(1)}, f32[16,2048]{1,0:T(8,128)}, u32[]{:S(2)}) copy-start(f32[16,2048]{1,0:T(8,128)} %param.59) | copy-start | bytes 393220
  35.8 5.9 %collective-permute-start.1 = (f32[2,1,2048]{2,0,1:T(2,128)S(1)}, f32[2,1,2048]{2,0,1:T(2,128)S(1)}, u32[]{:S(2)}, u32[]{:S(2)}) collective-permute-start(f32[2,1,2048]{2,0,1:T(2,128)S(1)} %copy.522), channel_id=1, source_target_pairs={{0,1},{1,2},{2,3},{3,4},{4,5},{5,6},{6,7},{7,8},{8,9},{9,10},{10,1... | collective-permute-start | bytes 49160 | tf_op jit(solution)/shard_map/ppermute | solution.py:17
  69.1 5.3 %copy-start.7 = (f32[16,3]{1,0:T(8,128)S(1)}, f32[16,3]{1,0:T(8,128)}, u32[]{:S(2)}) copy-start(f32[16,3]{1,0:T(8,128)} %gather_fusion.1) | copy-start | bytes 580
  70.4 4.3 %collective-permute-start.2 = (f32[3,1,2048]{2,1,0:T(1,128)}, f32[3,1,2048]{2,1,0:T(1,128)}, u32[]{:S(2)}, u32[]{:S(2)}) collective-permute-start(f32[3,1,2048]{2,1,0:T(1,128)} %pad_add_fusion.22), channel_id=1, source_target_pairs={{0,15},{1,0},{2,1},{3,2},{4,3},{5,4},{6,5},{7,6},{8,7},{9,8},{10,9... | collective-permute-start | bytes 73736 | tf_op jit(solution)/shard_map/ppermute | solution.py:17
  82.0 5.9 %collective-permute-start.3 = (f32[2,1,2048]{2,0,1:T(2,128)S(1)}, f32[2,1,2048]{2,0,1:T(2,128)S(1)}, u32[]{:S(2)}, u32[]{:S(2)}) collective-permute-start(f32[2,1,2048]{2,0,1:T(2,128)S(1)} %copy.527), channel_id=1, source_target_pairs={{0,1},{1,2},{2,3},{3,4},{4,5},{5,6},{6,7},{7,8},{8,9},{9,10},{10,1... | collective-permute-start | bytes 49160 | tf_op jit(solution)/shard_map/ppermute | solution.py:17
  112.7 4.4 %copy-start.8 = (f32[16,3]{1,0:T(8,128)S(1)}, f32[16,3]{1,0:T(8,128)}, u32[]{:S(2)}) copy-start(f32[16,3]{1,0:T(8,128)} %gather_fusion.2) | copy-start | bytes 580
  113.4 4.0 %collective-permute-start.4 = (f32[3,1,2048]{2,1,0:T(1,128)S(1)}, f32[3,1,2048]{2,1,0:T(1,128)S(1)}, u32[]{:S(2)}, u32[]{:S(2)}) collective-permute-start(f32[3,1,2048]{2,1,0:T(1,128)S(1)} %pad_add_fusion.21), channel_id=1, source_target_pairs={{0,15},{1,0},{2,1},{3,2},{4,3},{5,4},{6,5},{7,6},{8,7},{9,8},{10,9... | collective-permute-start | bytes 73736 | tf_op jit(solution)/shard_map/ppermute | solution.py:17
  124.6 5.9 %collective-permute-start.5 = (f32[2,1,2048]{2,0,1:T(2,128)S(1)}, f32[2,1,2048]{2,0,1:T(2,128)S(1)}, u32[]{:S(2)}, u32[]{:S(2)}) collective-permute-start(f32[2,1,2048]{2,0,1:T(2,128)S(1)} %copy.532), channel_id=1, source_target_pairs={{0,1},{1,2},{2,3},{3,4},{4,5},{5,6},{6,7},{7,8},{8,9},{9,10},{10,1... | collective-permute-start | bytes 49160 | tf_op jit(solution)/shard_map/ppermute | solution.py:17
  151.8 4.1 %collective-permute-start.6 = (f32[3,1,2048]{2,1,0:T(1,128)S(1)}, f32[3,1,2048]{2,1,0:T(1,128)S(1)}, u32[]{:S(2)}, u32[]{:S(2)}) collective-permute-start(f32[3,1,2048]{2,1,0:T(1,128)S(1)} %pad_add_fusion.20), channel_id=1, source_target_pairs={{0,15},{1,0},{2,1},{3,2},{4,3},{5,4},{6,5},{7,6},{8,7},{9,8},{10,9... | collective-permute-start | bytes 73736 | tf_op jit(solution)/shard_map/ppermute | solution.py:17
  163.2 5.9 %collective-permute-start.7 = (f32[2,1,2048]{2,0,1:T(2,128)S(1)}, f32[2,1,2048]{2,0,1:T(2,128)S(1)}, u32[]{:S(2)}, u32[]{:S(2)}) collective-permute-start(f32[2,1,2048]{2,0,1:T(2,128)S(1)} %copy.537), channel_id=1, source_target_pairs={{0,1},{1,2},{2,3},{3,4},{4,5},{5,6},{6,7},{7,8},{8,9},{9,10},{10,1... | collective-permute-start | bytes 49160 | tf_op jit(solution)/shard_map/ppermute | solution.py:17
  190.4 4.1 %collective-permute-start.8 = (f32[3,1,2048]{2,1,0:T(1,128)S(1)}, f32[3,1,2048]{2,1,0:T(1,128)S(1)}, u32[]{:S(2)}, u32[]{:S(2)}) collective-permute-start(f32[3,1,2048]{2,1,0:T(1,128)S(1)} %pad_add_fusion.19), channel_id=1, source_target_pairs={{0,15},{1,0},{2,1},{3,2},{4,3},{5,4},{6,5},{7,6},{8,7},{9,8},{10,9... | collective-permute-start | bytes 73736 | tf_op jit(solution)/shard_map/ppermute | solution.py:17
  201.8 5.9 %collective-permute-start.9 = (f32[2,1,2048]{2,0,1:T(2,128)S(1)}, f32[2,1,2048]{2,0,1:T(2,128)S(1)}, u32[]{:S(2)}, u32[]{:S(2)}) collective-permute-start(f32[2,1,2048]{2,0,1:T(2,128)S(1)} %copy.542), channel_id=1, source_target_pairs={{0,1},{1,2},{2,3},{3,4},{4,5},{5,6},{6,7},{7,8},{8,9},{9,10},{10,1... | collective-permute-start | bytes 49160 | tf_op jit(solution)/shard_map/ppermute | solution.py:17
  229.0 4.1 %collective-permute-start.10 = (f32[3,1,2048]{2,1,0:T(1,128)S(1)}, f32[3,1,2048]{2,1,0:T(1,128)S(1)}, u32[]{:S(2)}, u32[]{:S(2)}) collective-permute-start(f32[3,1,2048]{2,1,0:T(1,128)S(1)} %pad_add_fusion.18), channel_id=1, source_target_pairs={{0,15},{1,0},{2,1},{3,2},{4,3},{5,4},{6,5},{7,6},{8,7},{9,8},{10,9... | collective-permute-start | bytes 73736 | tf_op jit(solution)/shard_map/ppermute | solution.py:17
  240.4 5.9 %collective-permute-start.11 = (f32[2,1,2048]{2,0,1:T(2,128)S(1)}, f32[2,1,2048]{2,0,1:T(2,128)S(1)}, u32[]{:S(2)}, u32[]{:S(2)}) collective-permute-start(f32[2,1,2048]{2,0,1:T(2,128)S(1)} %copy.547), channel_id=1, source_target_pairs={{0,1},{1,2},{2,3},{3,4},{4,5},{5,6},{6,7},{7,8},{8,9},{9,10},{10,1... | collective-permute-start | bytes 49160 | tf_op jit(solution)/shard_map/ppermute | solution.py:17
  267.6 4.3 %collective-permute-start.12 = (f32[3,1,2048]{2,1,0:T(1,128)S(1)}, f32[3,1,2048]{2,1,0:T(1,128)S(1)}, u32[]{:S(2)}, u32[]{:S(2)}) collective-permute-start(f32[3,1,2048]{2,1,0:T(1,128)S(1)} %pad_add_fusion.17), channel_id=1, source_target_pairs={{0,15},{1,0},{2,1},{3,2},{4,3},{5,4},{6,5},{7,6},{8,7},{9,8},{10,9... | collective-permute-start | bytes 73736 | tf_op jit(solution)/shard_map/ppermute | solution.py:17
  279.2 5.9 %collective-permute-start.13 = (f32[2,1,2048]{2,0,1:T(2,128)S(1)}, f32[2,1,2048]{2,0,1:T(2,128)S(1)}, u32[]{:S(2)}, u32[]{:S(2)}) collective-permute-start(f32[2,1,2048]{2,0,1:T(2,128)S(1)} %copy.552), channel_id=1, source_target_pairs={{0,1},{1,2},{2,3},{3,4},{4,5},{5,6},{6,7},{7,8},{8,9},{9,10},{10,1... | collective-permute-start | bytes 49160 | tf_op jit(solution)/shard_map/ppermute | solution.py:17
  306.4 4.1 %collective-permute-start.14 = (f32[3,1,2048]{2,1,0:T(1,128)S(1)}, f32[3,1,2048]{2,1,0:T(1,128)S(1)}, u32[]{:S(2)}, u32[]{:S(2)}) collective-permute-start(f32[3,1,2048]{2,1,0:T(1,128)S(1)} %pad_add_fusion.16), channel_id=1, source_target_pairs={{0,15},{1,0},{2,1},{3,2},{4,3},{5,4},{6,5},{7,6},{8,7},{9,8},{10,9... | collective-permute-start | bytes 73736 | tf_op jit(solution)/shard_map/ppermute | solution.py:17
  315.6 2.3 copy-start.3
  315.6 2.5 copy-start.5
  318.0 5.9 %collective-permute-start.15 = (f32[2,1,2048]{2,0,1:T(2,128)S(1)}, f32[2,1,2048]{2,0,1:T(2,128)S(1)}, u32[]{:S(2)}, u32[]{:S(2)}) collective-permute-start(f32[2,1,2048]{2,0,1:T(2,128)S(1)} %copy.557), channel_id=1, source_target_pairs={{0,1},{1,2},{2,3},{3,4},{4,5},{5,6},{6,7},{7,8},{8,9},{9,10},{10,1... | collective-permute-start | bytes 49160 | tf_op jit(solution)/shard_map/ppermute | solution.py:17
where the time goes:
time: 328 us; the launch traced here: 325 us
  blocking collectives  142 us (43%)
  other arithmetic  75.7 us (23%)
  local copies, waits for them, and re-layouts  54.1 us (16%)
  waiting for transfers between devices  32.8 us (10%)
  starting transfers between devices  19.4 us (6%)
    all_gather x8, blocking collectives, on_device(): whole_row = lax.all_gather(back[6], 'lon', axis=1, tiled=True)  142 us
    ppermute x16, waiting for transfers between devices, passed_along(): return lax.ppermute(value, axis, pairs)  32.8 us
    ppermute x16, starting transfers between devices, passed_along(): return lax.ppermute(value, axis, pairs)  19.4 us
    another operation x16, other arithmetic, on_device(): jnp.stack([adjoint[2] + back[2], adjoint[3] + back[3], adjoint[4] + back[...  15 us
    another operation x16, other arithmetic, on_device(): jnp.stack([back[0] + front[0], back[1] + front[1]]).at[:, :1, :]  12.8 us
    scatter-add x8, local copies, waits for them, and re-layouts, on_device(): stress_cot = stress_cot.at[:, -1:, :].add(from_east)  12.1 us
    scatter-add x8, local copies, waits for them, and re-layouts, on_device(): jnp.stack([back[0] + front[0], back[1] + front[1]]).at[:, :1, :]  11.5 us
    scatter-add x8, local copies, waits for them, and re-layouts, on_device(): stress_cot = stress_cot.at[:, :, -1].add(fold_add)  11.3 us
  transfers between devices with their start and end apart: 16, of which 8 were waited for; matrix products, arithmetic and copies ran while one was open for 11% of the time, Pallas kernels for 0%

commit v1 on v0

v1 whole, which is shorter than its diff:
```python
import functools

import jax
import jax.numpy as jnp
from jax import lax
from jax.experimental import pallas as pl
from jax.experimental.pallas import tpu as pltpu
from jax.sharding import PartitionSpec as P

COLS = 16
STEPS = 8
HALO = 8
TILE = 16
LANES = 128
GROUPS = 16
EXT = 40
UNROLL = 4

WEST_WIDTH = [STEPS + 1 - step for step in range(1, STEPS + 1)]
EAST_WIDTH = [STEPS - step for step in range(1, STEPS + 1)]
WEST_FIELD = [0, 8, 16, 24, 32]
WEST_COUNT = [8, 8, 8, 8, 8]
WEST_MASS = 40
WEST_ZETA = [48 + sum(WEST_WIDTH[:k]) for k in range(STEPS)]
WEST_SIZE = 48 + sum(WEST_WIDTH)
EAST_FIELD = [0, 8, 16, 23, 30]
EAST_COUNT = [8, 8, 7, 7, 7]
EAST_MASS = 37
EAST_ZETA = [45 + sum(EAST_WIDTH[:k]) for k in range(STEPS)]
EAST_SIZE = 45 + sum(EAST_WIDTH)
STRIP_FIELDS = 13
SHRINK = (5.0 / 6.0) ** STEPS


def as_rows(field):
    lead = field.shape[:-2]
    tiled = field.reshape(lead + (2, 8, GROUPS, LANES)).swapaxes(-3, -2)
    return tiled.reshape(lead + (2 * GROUPS * 8, LANES))


def from_rows(field):
    lead = field.shape[:-2]
    tiled = field.reshape(lead + (2, GROUPS, 8, LANES)).swapaxes(-3, -2)
    return tiled.reshape(lead + (COLS, GROUPS * LANES))


def column_slices(col):
    start = (col // 8) * 128 + col % 8
    return pl.ds(start, 8, 16), pl.ds(start + 8, 8, 16)


def column_tile(load, col):
    even, odd = column_slices(col)
    return jnp.concatenate([load(even), load(odd)], axis=0)


def pack_kernel(
    state, strains, strength, mass, ice_mask, partner,
    west_out, east_out, strip_out, zeta_out, mass_out, rows,
):
    lane = lax.broadcasted_iota(jnp.int32, (COLS, LANES), 1)
    strip = jnp.zeros((COLS, LANES), jnp.float32)

    def strip_field(strip, at, tile):
        moved = pltpu.roll(tile, (8 * at + 8) % LANES, 1)
        return jnp.where((lane >= 8 * at) & (lane < 8 * at + 8), moved, strip)

    for field in range(5):
        for col in range(COLS):
            tile = column_tile(lambda at: state[field, at, :], col).astype(jnp.bfloat16)
            if col >= 8:
                west_out[WEST_FIELD[field] + col - 8] = tile
            elif col < EAST_COUNT[field]:
                east_out[EAST_FIELD[field] + col] = tile
        last = jnp.concatenate([state[field, 120:128, :], state[field, 248:256, :]], 0)
        strip = strip_field(strip, field, last)

    for group in range(GROUPS):
        at = slice(128 * group, 128 * group + 128)
        weight = ice_mask[:, at].astype(jnp.float32) / (6.0 * mass[:, at])
        rows[8 * group : 8 * group + 8] = weight[:8]
        rows[128 + 8 * group : 136 + 8 * group] = weight[8:]
        if group == GROUPS - 1:
            strip = strip_field(strip, 5, weight)
    for col in range(COLS):
        tile = column_tile(lambda at: rows[at, :], col)
        mass_out[col] = tile
        if col >= 8:
            west_out[WEST_MASS + col - 8] = tile.astype(jnp.bfloat16)
        else:
            east_out[EAST_MASS + col] = tile.astype(jnp.bfloat16)

    for step in range(STEPS):
        cycle = STEPS - 1 - step
        for group in range(GROUPS):
            at = slice(128 * group, 128 * group + 128)
            div = strains[cycle, 0, :, at].astype(jnp.float32)
            ten = strains[cycle, 1, :, at].astype(jnp.float32)
            she = strains[cycle, 2, :, at].astype(jnp.float32)
            square = div * div + 0.25 * (ten * ten + she * she)
            zeta = (0.05 * strength[:, at]) * lax.rsqrt(jnp.maximum(square, 0.25))
            rows[8 * group : 8 * group + 8] = zeta[:8]
            rows[128 + 8 * group : 136 + 8 * group] = zeta[8:]
            if group == GROUPS - 1 and step < STEPS - 1:
                strip = strip_field(strip, 6 + step, zeta)
        for col in range(COLS):
            tile = column_tile(lambda at: rows[at, :], col)
            zeta_out[step, col] = tile
            if col >= COLS - WEST_WIDTH[step]:
                west_out[WEST_ZETA[step] + col - (COLS - WEST_WIDTH[step])] = tile.astype(jnp.bfloat16)
            if col < EAST_WIDTH[step]:
                east_out[EAST_ZETA[step] + col] = tile.astype(jnp.bfloat16)

    row_at = lax.broadcasted_iota(jnp.int32, (COLS, LANES), 0)
    place = jnp.zeros((COLS, LANES), jnp.int32)
    for col in range(COLS):
        place = jnp.where(row_at == col, lax.rem(partner[col], COLS), place)
    strip = jnp.where(lane == 8 * STRIP_FIELDS, place.astype(jnp.float32), strip)
    packed = strip.astype(jnp.bfloat16)
    for device in range(strip_out.shape[0]):
        strip_out[device] = packed


def fold_values(strips, folds):
    total = strips.shape[0]
    count = total // LANES
    lane = lax.broadcasted_iota(jnp.int32, (8, LANES), 1)
    sub = lax.broadcasted_iota(jnp.int32, (8, total), 0)
    turned = [strips[LANES * r : LANES * r + LANES, :].astype(jnp.float32).T for r in range(count)]

    def field(at):
        return jnp.concatenate([part[8 * at : 8 * at + 8] for part in turned], axis=1)

    places = [
        (7 - lane // COLS) * COLS
        + jnp.broadcast_to(part[8 * STRIP_FIELDS : 8 * STRIP_FIELDS + 1], (8, LANES)).astype(jnp.int32)
        for part in turned
    ]

    def by_partner(value):
        parts = [
            jnp.take_along_axis(
                value[:, LANES * (count - 1 - r) : LANES * (count - r)], places[r], axis=1,
                mode="promise_in_bounds",
            )
            for r in range(count)
        ]
        return jnp.concatenate(parts, axis=1)

    def next_col(value):
        return pltpu.roll(value, total - 1, 1)

    def prev_col(value):
        return pltpu.roll(value, 1, 1)

    def row_above(value):
        return jnp.where(sub == 7, 0.0, pltpu.roll(value, 7, 0))

    def row_below(value):
        return pltpu.roll(value, 1, 0)

    vel_u, vel_v, one, two, shear, weight = (field(at) for at in range(6))
    one = 2.0 * one
    two = 2.0 * two
    wet = weight != 0.0
    fold_p = jnp.zeros((8, total), jnp.float32)
    fold_q = jnp.zeros((8, total), jnp.float32)
    for step in range(STEPS):
        p = weight * vel_u
        q = weight * vel_v
        far_p = by_partner(p)
        far_q = by_partner(q)
        turn = (step + 1) % 8
        fold_p = jnp.where(sub == step, pltpu.roll(far_p, turn, 0) if turn else far_p, fold_p)
        fold_q = jnp.where(sub == step, pltpu.roll(far_q, turn, 0) if turn else far_q, fold_q)
        if step == STEPS - 1:
            break
        far_p = jnp.where(sub == 7, far_p, 0.0)
        far_q = jnp.where(sub == 7, far_q, 0.0)
        along = p - next_col(p)
        across = row_below(q) - q + far_q
        one = one + (along + across)
        two = two + (along - across)
        shear = shear + (row_below(p) - p - far_p) + (q - next_col(q))
        zeta = field(6 + step)
        first = zeta * one
        second = (0.25 * zeta) * two
        third = (0.5 * zeta) * shear
        x = first + second
        y = first - second
        wet_u = jnp.where(wet, vel_u, 0.0)
        wet_v = jnp.where(wet, vel_v, 0.0)
        vel_u = (wet_u - 0.1 * wet_v) + (prev_col(x) - x) + (third - row_above(third))
        vel_v = (wet_v + 0.1 * wet_u) + (prev_col(third) - third) + (y - row_above(y))

    me = lax.axis_index("lon")
    shift = lax.rem(2 * total + HALO - COLS * me, total)
    both = jnp.concatenate(
        [pltpu.roll(fold_p, shift, 1)[:, :LANES], pltpu.roll(fold_q, shift, 1)[:, :LANES]], axis=0
    )
    tall = jnp.concatenate([both, jnp.zeros((LANES - 16, LANES), jnp.float32)], axis=0).T
    for at in range(16):
        folds[at] = pltpu.roll(tall[:EXT], LANES - 1 - at, 1)


def main_kernel(
    state, zeta_in, mass_in, west, east, strips, out,
    vel_u, vel_v, one, two, shear, weight, zeta, folds,
):
    fields = (vel_u, vel_v, one, two, shear)
    scales = (1.0, 1.0, 2.0, 2.0, 1.0)
    fold_values(strips, folds)
    for field in range(5):
        for col in range(COLS):
            tile = column_tile(lambda at: state[field, at, :], col)
            fields[field][HALO + col] = scales[field] * tile
        for col in range(WEST_COUNT[field]):
            fields[field][col] = scales[field] * west[WEST_FIELD[field] + col].astype(jnp.float32)
        for col in range(EAST_COUNT[field]):
            fields[field][HALO + COLS + col] = scales[field] * east[EAST_FIELD[field] + col].astype(jnp.float32)
    for col in range(8):
        weight[col] = west[WEST_MASS + col].astype(jnp.float32)
        weight[HALO + COLS + col] = east[EAST_MASS + col].astype(jnp.float32)
    for col in range(COLS):
        weight[HALO + col] = mass_in[col]
    for step in range(STEPS):
        for col in range(COLS):
            zeta[step, HALO + col] = zeta_in[step, col]
        for col in range(WEST_WIDTH[step]):
            zeta[step, HALO - WEST_WIDTH[step] + col] = west[WEST_ZETA[step] + col].astype(jnp.float32)
        for col in range(EAST_WIDTH[step]):
            zeta[step, HALO + COLS + col] = east[EAST_ZETA[step] + col].astype(jnp.float32)

    lane = lax.broadcasted_iota(jnp.int32, (8, LANES), 1)
    sub = lax.broadcasted_iota(jnp.int32, (8, LANES), 0)
    first_lane = lane == 0
    last_lane = lane == LANES - 1
    top = sub == 0
    bottom = sub == 7
    corner = last_lane & bottom

    def row_above(value):
        turned = pltpu.roll(value, LANES - 1, 1)
        even, odd = turned[:8], turned[8:]
        carried = jnp.where(bottom, 0.0, pltpu.roll(even, 7, 0))
        return jnp.concatenate([jnp.where(last_lane, odd, even), jnp.where(last_lane, carried, odd)], 0)

    def row_below(value):
        turned = pltpu.roll(value, 1, 1)
        even, odd = turned[:8], turned[8:]
        carried = jnp.where(top, 0.0, pltpu.roll(odd, 1, 0))
        return jnp.concatenate([jnp.where(first_lane, carried, even), jnp.where(first_lane, even, odd)], 0)

    def at_fold(value, add):
        return jnp.concatenate([value[:8], value[8:] + jnp.where(corner, add, 0.0)], 0)

    def forces(col):
        u, v, w = vel_u[col], vel_v[col], weight[col]
        wet = w != 0.0
        wet_u = jnp.where(wet, u, 0.0)
        wet_v = jnp.where(wet, v, 0.0)
        return w * u, w * v, wet_u - 0.1 * wet_v, wet_v + 0.1 * wet_u

    blank = jnp.zeros((TILE, LANES), jnp.float32)

    @pl.loop(0, STEPS)
    def _(step):
        begin = step
        groups = (2 * STEPS + COLS - 1 - 2 * step + UNROLL - 1) // UNROLL

        def body(group, carry):
            p, q, keep_u, keep_v, west_x, west_c = carry
            for part in range(UNROLL):
                col = begin + group * UNROLL + part
                next_p, next_q, next_u, next_v = forces(col + 1)
                along = p - next_p
                across = at_fold(row_below(q) - q, folds[8 + step, pl.ds(col, 1), :])
                turn = at_fold(row_below(p) - p, -folds[step, pl.ds(col, 1), :])
                new_one = one[col] + (along + across)
                new_two = two[col] + (along - across)
                new_shear = shear[col] + turn + (q - next_q)
                one[col] = new_one
                two[col] = new_two
                shear[col] = new_shear
                z = zeta[step, col]
                first = z * new_one
                second = (0.25 * z) * new_two
                c = (0.5 * z) * new_shear
                x = first + second
                y = first - second
                vel_u[col] = keep_u + (west_x - x) + (c - row_above(c))
                vel_v[col] = keep_v + (west_c - c) + (y - row_above(y))
                p, q, keep_u, keep_v, west_x, west_c = next_p, next_q, next_u, next_v, x, c
            return p, q, keep_u, keep_v, west_x, west_c

        lax.fori_loop(0, groups, body, forces(begin) + (blank, blank))

    outs = (SHRINK, SHRINK, 0.5 * SHRINK, 0.5 * SHRINK, SHRINK)
    for field in range(5):
        for col in range(COLS):
            tile = outs[field] * fields[field][HALO + col]
            even, odd = column_slices(col)
            out[field, even, :] = tile[:8]
            out[field, odd, :] = tile[8:]


def on_device(final_cot, strains, strength, mass, ice_mask, partner):
    count = lax.axis_size("lon")
    state = as_rows(final_cot)
    whole = pl.BlockSpec(memory_space=pltpu.VMEM)
    f32 = jnp.float32
    bf16 = jnp.bfloat16
    params = pltpu.CompilerParams(vmem_limit_bytes=48 * 1024 * 1024)
    west_send, east_send, strip_send, zeta, weight = pl.pallas_call(
        pack_kernel,
        out_shape=(
            jax.ShapeDtypeStruct((WEST_SIZE, TILE, LANES), bf16),
            jax.ShapeDtypeStruct((EAST_SIZE, TILE, LANES), bf16),
            jax.ShapeDtypeStruct((count, COLS, LANES), bf16),
            jax.ShapeDtypeStruct((STEPS, COLS, TILE, LANES), f32),
            jax.ShapeDtypeStruct((COLS, TILE, LANES), f32),
        ),
        in_specs=[whole] * 5 + [pl.BlockSpec(memory_space=pltpu.SMEM)],
        out_specs=(whole,) * 5,
        scratch_shapes=[pltpu.VMEM((256, LANES), f32)],
        compiler_params=params,
    )(state, strains, strength, mass, ice_mask, partner)

    west = lax.ppermute(west_send, "lon", [(i, (i + 1) % count) for i in range(count)])
    east = lax.ppermute(east_send, "lon", [(i, (i - 1) % count) for i in range(count)])
    strips = lax.all_to_all(strip_send, "lon", 0, 0, tiled=True).reshape(count * COLS, LANES)

    out = pl.pallas_call(
        main_kernel,
        out_shape=jax.ShapeDtypeStruct(state.shape, f32),
        in_specs=[whole] * 6,
        out_specs=whole,
        scratch_shapes=[pltpu.VMEM((EXT, TILE, LANES), f32)] * 6
        + [pltpu.VMEM((STEPS, EXT, TILE, LANES), f32), pltpu.VMEM((16, EXT, LANES), f32)],
        compiler_params=params,
    )(state, zeta, weight, west, east, strips)
    return from_rows(out)


def solution(mesh):
    return jax.shard_map(
        on_device,
        mesh=mesh,
        in_specs=(
            P("ens", "lon", None),
            P("ens", None, "lon", None),
            P("lon", None),
            P("lon", None),
            P("lon", None),
            P("lon"),
        ),
        out_specs=P("ens", "lon", None),
        check_vma=False,
    )
```

time: 328 us -> 35.8 us (0.11)
  blocking collectives: 142 us -> 10.3 us
  other arithmetic: 75.7 us -> 0 us
  local copies, waits for them, and re-layouts: 54.1 us -> 5.86 us
  waiting for transfers between devices: 32.8 us -> 0.01 us
  starting transfers between devices: 19.4 us -> 5.53 us
  Pallas kernels: 0 us -> 13.8 us
    all_gather x8 -> x0, blocking collectives: 142 us -> none  [on_device(): whole_row = lax.all_gather(back[6], 'lon', axis=1, tiled=True)]
    scatter-add x24 -> x0, local copies, waits for them, and re-layouts: 34.9 us -> none  [the longest x8 12.1 us: on_device(): stress_cot = stress_cot.at[:, -1:, :].add(from_east)]
    ppermute x16 -> x2, waiting for transfers between devices: 32.8 us -> 0.01 us  [the longest x1 0.01 us: on_device(): lax.ppermute(east_send, 'lon', [(i, (i - 1) % count) for i in range(count)])]
    another operation x40 -> x0, other arithmetic: 28.4 us -> none  [the longest x16 15 us: on_device(): jnp.stack([adjoint[2] + back[2], adjoint[3] + back[3], adjoint[4] + back[...]
    ppermute x16 -> x2, starting transfers between devices: 19.4 us -> 5.53 us  [the longest x1 5.03 us: on_device(): lax.ppermute(east_send, 'lon', [(i, (i - 1) % count) for i in range(count)])]
    pallas_call x0 -> x2, Pallas kernels: none -> 13.8 us  [the longest x1 12.3 us: on_device(): pl.pallas_call(main_kernel, out_shape=jax.ShapeDtypeStruct(state.shape, f...]
    add x24 -> x0, other arithmetic: 13.6 us -> none  [the longest x8 7.56 us: on_device(): stress_cot = stress_cot.at[:, -1:, :].add(from_east)]
    neg x39 -> x0, other arithmetic: 10.5 us -> none  [the longest x8 8.3 us: stresses(): grad_uy = vel_u - below(vel_u)]
  transfers between devices with their start and end apart: 16 -> 2, of which waited for: 8 -> 0; matrix products, arithmetic and copies ran while one was open for 11% -> 0% of each run, Pallas kernels for 0% -> 0%
where the time goes in v1:
time: 35.8 us; the launch traced here: 35.5 us
  Pallas kernels  13.8 us (39%)
  blocking collectives  10.3 us (29%)
  local copies, waits for them, and re-layouts  5.86 us (16%)
  starting transfers between devices  5.53 us (15%)
    pallas_call x1, Pallas kernels, on_device(): pl.pallas_call(main_kernel, out_shape=jax.ShapeDtypeStruct(state.shape, f...  12.3 us
    all_to_all x1, blocking collectives, on_device(): lax.all_to_all(strip_send, 'lon', 0, 0, tiled=True)  10.3 us
    unnamed x12, local copies, waits for them, and re-layouts  5.86 us
    ppermute x1, starting transfers between devices, on_device(): lax.ppermute(east_send, 'lon', [(i, (i - 1) % count) for i in range(count)])  5.03 us
    pallas_call x1, Pallas kernels, on_device(): pl.pallas_call(pack_kernel, out_shape=(jax.ShapeDtypeStruct((WEST_SIZE, T...  1.49 us
  transfers between devices with their start and end apart: 2, of which 0 were waited for; matrix products, arithmetic and copies ran while one was open for 0% of the time, Pallas kernels for 0%

profile of v1, /device:TPU:0, one launch (start us, length us, event | category | flops | bytes accessed | tf_op | source)
XLA Modules:
  0.0 35.5 jit_solution(17981358845428744988)
XLA Ops:
  0.0 0.0 copy-start
  0.0 1.1 %copy-done = f32[5,16,2048]{2,1,0:T(8,128)S(1)} copy-done((f32[5,16,2048]{2,1,0:T(8,128)S(1)}, f32[5,16,2048]{2,1,0:T(8,128)}, u32[]{:S(2)}) %copy-start) | copy-done | bytes 655384
  1.1 0.0 copy-start.1
  1.1 1.4 %copy-done.1 = bf16[8,3,16,2048]{3,2,1,0:T(8,128)(2,1)S(1)} copy-done((bf16[8,3,16,2048]{3,2,1,0:T(8,128)(2,1)S(1)}, bf16[8,3,16,2048]{3,2,1,0:T(8,128)(2,1)}, u32[]{:S(2)}) %copy-start.1) | copy-done | bytes 1572888
  2.5 0.0 copy-start.2
  2.5 0.9 %copy-done.2 = f32[16,2048]{1,0:T(8,128)S(1)} copy-done((f32[16,2048]{1,0:T(8,128)S(1)}, f32[16,2048]{1,0:T(8,128)}, u32[]{:S(2)}) %copy-start.2) | copy-done | bytes 131096
  3.4 0.0 copy-start.3
  3.4 0.9 %copy-done.3 = f32[16,2048]{1,0:T(8,128)S(1)} copy-done((f32[16,2048]{1,0:T(8,128)S(1)}, f32[16,2048]{1,0:T(8,128)}, u32[]{:S(2)}) %copy-start.3) | copy-done | bytes 131096
  4.3 0.0 copy-start.4
  4.3 0.9 %copy-done.4 = s32[16,2048]{1,0:T(8,128)S(1)} copy-done((s32[16,2048]{1,0:T(8,128)S(1)}, s32[16,2048]{1,0:T(8,128)}, u32[]{:S(2)}) %copy-start.4) | copy-done | bytes 131096
  5.2 0.0 copy-start.5
  5.2 0.7 %copy-done.5 = s32[16]{0:T(128)S(1)} copy-done((s32[16]{0:T(128)S(1)}, s32[16]{0:T(128)}, u32[]{:S(2)}) %copy-start.5) | copy-done | bytes 88
  5.9 1.5 %shard_map.64 = (bf16[84,16,128]{2,1,0:T(8,128)(2,1)S(1)}, bf16[73,16,128]{2,1,0:T(8,128)(2,1)S(1)}, bf16[16,16,128]{2,1,0:T(8,128)(2,1)S(1)}, f32[8,16,16,128]{3,2,1,0:T(8,128)S(1)}, f32[16,16,128]{2,1,0:T(8,128)S(1)}) custom-call(f32[5,256,128]{2,1,0:T(8,128)S(1)} %bitcast.11, bf16[8,3,16,2048]{3,2,1,0:T(8,128)(2,1)S(1)} %copy-done.1, ...), custom_call_target="tpu_custom_call" | custom-call | tf_op jit(solution)/shard_map/pallas_call | solution.py:314
  7.4 0.5 %collective-permute-start = (bf16[84,16,128]{2,1,0:T(8,128)(2,1)S(1)}, bf16[84,16,128]{2,1,0:T(8,128)(2,1)S(1)}, u32[]{:S(2)}, u32[]{:S(2)}) collective-permute-start(bf16[84,16,128]{2,1,0:T(8,128)(2,1)S(1)} %get-tuple-element.12), channel_id=1, source_target_pairs={{0,1},{1,2},{2,3},{3,4},{4,5},{5,6},{6,7},{7,8},{8,9},{9,10},{10,1... | collective-permute-start | bytes 1032200 | tf_op jit(solution)/shard_map/ppermute | solution.py:329
  7.9 5.0 %collective-permute-start.1 = (bf16[73,16,128]{2,1,0:T(8,128)(2,1)S(1)}, bf16[73,16,128]{2,1,0:T(8,128)(2,1)S(1)}, u32[]{:S(2)}, u32[]{:S(2)}) collective-permute-start(bf16[73,16,128]{2,1,0:T(8,128)(2,1)S(1)} %get-tuple-element.13), channel_id=1, source_target_pairs={{0,15},{1,0},{2,1},{3,2},{4,3},{5,4},{6,5},{7,6},{8,7},{9,8},{10,9... | collective-permute-start | bytes 897032 | tf_op jit(solution)/shard_map/ppermute | solution.py:330
  12.9 10.3 %all_to_all.5 = bf16[16,16,128]{2,1,0:T(8,128)(2,1)S(1)} all-to-all(bf16[16,16,128]{2,1,0:T(8,128)(2,1)S(1)} %get-tuple-element.14), channel_id=1, replica_groups=mesh['ens'=2,'lon'=16] {'lon'}, dimensions={0} | all-to-all | bytes 131072 | tf_op jit(solution)/shard_map/all_to_all | solution.py:331
  23.2 0.0 collective-permute-done.1.east
  23.2 0.0 collective-permute-done.west
  23.2 12.3 %shard_map.65 = f32[5,256,128]{2,1,0:T(8,128)} custom-call(f32[5,256,128]{2,1,0:T(8,128)S(1)} %bitcast.12, f32[8,16,16,128]{3,2,1,0:T(8,128)S(1)} %get-tuple-element.10.zeta_in, f32[16,16,128]{2,1,0:T(8,128)S(1)} %get-tuple-element.11.mass_in, bf16[84,16,128]{2,1,0:T(8,128)(2,1)S(1)} %collective-permute-done.west, ...), custom_call_target="tpu_custom_call" | custom-call | tf_op jit(solution)/shard_map/pallas_call | solution.py:333
Async XLA Ops:
  0.0 1.1 %copy-start = (f32[5,16,2048]{2,1,0:T(8,128)S(1)}, f32[5,16,2048]{2,1,0:T(8,128)}, u32[]{:S(2)}) copy-start(f32[5,16,2048]{2,1,0:T(8,128)} %param.6) | copy-start | bytes 1966084
  1.1 1.4 %copy-start.1 = (bf16[8,3,16,2048]{3,2,1,0:T(8,128)(2,1)S(1)}, bf16[8,3,16,2048]{3,2,1,0:T(8,128)(2,1)}, u32[]{:S(2)}) copy-start(bf16[8,3,16,2048]{3,2,1,0:T(8,128)(2,1)} %strains.1) | copy-start | bytes 4718596
  2.5 0.9 %copy-start.2 = (f32[16,2048]{1,0:T(8,128)S(1)}, f32[16,2048]{1,0:T(8,128)}, u32[]{:S(2)}) copy-start(f32[16,2048]{1,0:T(8,128)} %strength.1) | copy-start | bytes 393220
  3.4 0.9 %copy-start.3 = (f32[16,2048]{1,0:T(8,128)S(1)}, f32[16,2048]{1,0:T(8,128)}, u32[]{:S(2)}) copy-start(f32[16,2048]{1,0:T(8,128)} %mass.1) | copy-start | bytes 393220
  4.3 0.9 %copy-start.4 = (s32[16,2048]{1,0:T(8,128)S(1)}, s32[16,2048]{1,0:T(8,128)}, u32[]{:S(2)}) copy-start(s32[16,2048]{1,0:T(8,128)} %ice_mask.1) | copy-start | bytes 393220
  5.2 0.7 %copy-start.5 = (s32[16]{0:T(128)S(1)}, s32[16]{0:T(128)}, u32[]{:S(2)}) copy-start(s32[16]{0:T(128)} %partner.1) | copy-start | bytes 196
  7.4 15.8 %collective-permute-start = (bf16[84,16,128]{2,1,0:T(8,128)(2,1)S(1)}, bf16[84,16,128]{2,1,0:T(8,128)(2,1)S(1)}, u32[]{:S(2)}, u32[]{:S(2)}) collective-permute-start(bf16[84,16,128]{2,1,0:T(8,128)(2,1)S(1)} %get-tuple-element.12), channel_id=1, source_target_pairs={{0,1},{1,2},{2,3},{3,4},{4,5},{5,6},{6,7},{7,8},{8,9},{9,10},{10,1... | collective-permute-start | bytes 1032200 | tf_op jit(solution)/shard_map/ppermute | solution.py:329
  7.9 15.3 %collective-permute-start.1 = (bf16[73,16,128]{2,1,0:T(8,128)(2,1)S(1)}, bf16[73,16,128]{2,1,0:T(8,128)(2,1)S(1)}, u32[]{:S(2)}, u32[]{:S(2)}) collective-permute-start(bf16[73,16,128]{2,1,0:T(8,128)(2,1)S(1)} %get-tuple-element.13), channel_id=1, source_target_pairs={{0,15},{1,0},{2,1},{3,2},{4,3},{5,4},{6,5},{7,6},{8,7},{9,8},{10,9... | collective-permute-start | bytes 897032 | tf_op jit(solution)/shard_map/ppermute | solution.py:330

commit v2 on v1

v2 whole, which is shorter than its diff:
```python
import functools

import jax
import jax.numpy as jnp
from jax import lax
from jax.experimental import pallas as pl
from jax.experimental.pallas import tpu as pltpu
from jax.sharding import PartitionSpec as P

COLS = 16
STEPS = 8
HALO = 8
TILE = 16
LANES = 128
GROUPS = 16
EXT = 40
UNROLL = 16

WEST_WIDTH = [STEPS + 1 - step for step in range(1, STEPS + 1)]
EAST_WIDTH = [STEPS - step for step in range(1, STEPS + 1)]
WEST_FIELD = [0, 8, 16, 24, 32]
WEST_COUNT = [8, 8, 8, 8, 8]
WEST_MASS = 40
WEST_ZETA = [48 + sum(WEST_WIDTH[:k]) for k in range(STEPS)]
WEST_SIZE = 48 + sum(WEST_WIDTH)
EAST_FIELD = [0, 8, 16, 23, 30]
EAST_COUNT = [8, 8, 7, 7, 7]
EAST_MASS = 37
EAST_ZETA = [45 + sum(EAST_WIDTH[:k]) for k in range(STEPS)]
EAST_SIZE = 45 + sum(EAST_WIDTH)
STRIP_FIELDS = 13
SHRINK = (5.0 / 6.0) ** STEPS


def as_rows(field):
    lead = field.shape[:-2]
    tiled = field.reshape(lead + (2, 8, GROUPS, LANES)).swapaxes(-3, -2)
    return tiled.reshape(lead + (2 * GROUPS * 8, LANES))


def from_rows(field):
    lead = field.shape[:-2]
    tiled = field.reshape(lead + (2, GROUPS, 8, LANES)).swapaxes(-3, -2)
    return tiled.reshape(lead + (COLS, GROUPS * LANES))


def column_slices(col, half):
    start = half * 128 + col
    return pl.ds(start, 8, 16), pl.ds(start + 8, 8, 16)


def column_tile(load, col, half):
    even, odd = column_slices(col, half)
    return jnp.concatenate([load(even), load(odd)], axis=0)


def west_slot(step):
    return 48 + STEPS * step - (step * (step - 1)) // 2


def east_slot(step):
    return 45 + (STEPS - 1) * step - (step * (step - 1)) // 2


def pack_kernel(
    state_hbm, strains_hbm, strength_hbm, mass_hbm, mask_hbm, partner_hbm,
    west_out, east_out, strip_out, state_out, zeta_out, mass_out,
    state, strains, strength, mass, mask, partner, rows, sems,
):
    bf16 = jnp.bfloat16
    copies = [
        pltpu.make_async_copy(strength_hbm, strength, sems.at[0]),
        pltpu.make_async_copy(partner_hbm, partner, sems.at[4]),
    ]
    strain_copies = [
        pltpu.make_async_copy(strains_hbm.at[2 * k : 2 * k + 2], strains.at[2 * k : 2 * k + 2], sems.at[5 + k])
        for k in range(STEPS // 2)
    ]
    state_copy = pltpu.make_async_copy(state_hbm, state, sems.at[3])
    cell_copies = [
        pltpu.make_async_copy(mass_hbm, mass, sems.at[1]),
        pltpu.make_async_copy(mask_hbm, mask, sems.at[2]),
    ]
    for copy in [state_copy, *copies, *strain_copies, *cell_copies]:
        copy.start()

    lane = lax.broadcasted_iota(jnp.int32, (COLS, LANES), 1)

    def strip_field(strip, at, tile):
        moved = pltpu.roll(tile, (8 * at + 8) % LANES, 1)
        return jnp.where((lane >= 8 * at) & (lane < 8 * at + 8), moved, strip)

    state_copy.wait()

    @pl.loop(0, 8)
    def _(turn):
        at = 7 - turn
        for field in range(5):
            tile = column_tile(lambda part: state[field, part, :], at, 0)
            state_out[field, HALO + at] = tile
            east_out[EAST_FIELD[field] + at] = tile.astype(bf16)
            tile = column_tile(lambda part: state[field, part, :], at, 1)
            state_out[field, HALO + 8 + at] = tile
            west_out[WEST_FIELD[field] + at] = tile.astype(bf16)

    strip = jnp.zeros((COLS, LANES), jnp.float32)
    for field in range(5):
        last = jnp.concatenate([state[field, 120:128, :], state[field, 248:256, :]], 0)
        strip = strip_field(strip, field, last)

    for copy in copies:
        copy.wait()

    def cycle_zeta(cycle, step, strip, rows):
        for group in range(GROUPS):
            at = slice(128 * group, 128 * group + 128)
            div = strains[cycle, 0, :, at].astype(jnp.float32)
            ten = strains[cycle, 1, :, at].astype(jnp.float32)
            she = strains[cycle, 2, :, at].astype(jnp.float32)
            square = div * div + 0.25 * (ten * ten + she * she)
            zeta = (0.1 * strength[:, at]) * lax.rsqrt(jnp.maximum(square, 0.25))
            rows[8 * group : 8 * group + 8] = zeta[:8]
            rows[128 + 8 * group : 136 + 8 * group] = zeta[8:]
            if group == GROUPS - 1:
                strip = strip_field(strip, 6 + step, zeta)
        for at in range(8):
            tile = column_tile(lambda part: rows[part, :], at, 0)
            zeta_out[step, HALO + at] = tile
            east_out[east_slot(step) + (EAST_WIDTH[0] - 1 - step) - at] = tile.astype(bf16)
            tile = column_tile(lambda part: rows[part, :], at, 1)
            zeta_out[step, HALO + 8 + at] = tile
            west_out[west_slot(step) + at - step] = tile.astype(bf16)
        return strip

    def two_cycles(turn, strip):
        pltpu.make_async_copy(
            strains_hbm.at[pl.ds(2 * turn, 2)], strains.at[pl.ds(2 * turn, 2)], sems.at[5 + turn]
        ).wait()
        for part in range(2):
            cycle = 2 * turn + part
            strip = cycle_zeta(cycle, STEPS - 1 - cycle, strip, rows.at[part])
        return strip

    strip = lax.fori_loop(0, STEPS // 2, two_cycles, strip)

    for copy in cell_copies:
        copy.wait()
    for group in range(GROUPS):
        at = slice(128 * group, 128 * group + 128)
        weight = mask[:, at].astype(jnp.float32) / (6.0 * mass[:, at])
        rows[0, 8 * group : 8 * group + 8] = weight[:8]
        rows[0, 128 + 8 * group : 136 + 8 * group] = weight[8:]
        if group == GROUPS - 1:
            strip = strip_field(strip, 5, weight)
    for at in range(8):
        tile = column_tile(lambda part: rows[0, part, :], at, 0)
        mass_out[HALO + at] = tile
        east_out[EAST_MASS + at] = tile.astype(bf16)
        tile = column_tile(lambda part: rows[0, part, :], at, 1)
        mass_out[HALO + 8 + at] = tile
        west_out[WEST_MASS + at] = tile.astype(bf16)

    row_at = lax.broadcasted_iota(jnp.int32, (COLS, LANES), 0)
    place = jnp.zeros((COLS, LANES), jnp.int32)
    for col in range(COLS):
        place = jnp.where(row_at == col, lax.rem(partner[col], COLS), place)
    strip = jnp.where(lane == 8 * STRIP_FIELDS, place.astype(jnp.float32), strip)
    packed = strip.astype(bf16)
    for device in range(strip_out.shape[0]):
        strip_out[device] = packed


def fold_values(strips, folds):
    total = strips.shape[0]
    count = total // LANES
    lane = lax.broadcasted_iota(jnp.int32, (8, LANES), 1)
    sub = lax.broadcasted_iota(jnp.int32, (8, total), 0)
    turned = [strips[LANES * r : LANES * r + LANES, :].astype(jnp.float32).T for r in range(count)]

    def field(at):
        return jnp.concatenate([part[8 * at : 8 * at + 8] for part in turned], axis=1)

    places = [
        (7 - lane // COLS) * COLS
        + jnp.broadcast_to(part[8 * STRIP_FIELDS : 8 * STRIP_FIELDS + 1], (8, LANES)).astype(jnp.int32)
        for part in turned
    ]

    def by_partner(value):
        parts = [
            jnp.take_along_axis(
                value[:, LANES * (count - 1 - r) : LANES * (count - r)], places[r], axis=1,
                mode="promise_in_bounds",
            )
            for r in range(count)
        ]
        return jnp.concatenate(parts, axis=1)

    def next_col(value):
        return pltpu.roll(value, total - 1, 1)

    def prev_col(value):
        return pltpu.roll(value, 1, 1)

    def row_above(value):
        return jnp.where(sub == 7, 0.0, pltpu.roll(value, 7, 0))

    def row_below(value):
        return pltpu.roll(value, 1, 0)

    vel_u, vel_v, one, two, shear, weight = (field(at) for at in range(6))
    wet = weight != 0.0
    fold_p = jnp.zeros((8, total), jnp.float32)
    fold_q = jnp.zeros((8, total), jnp.float32)
    for step in range(STEPS):
        p = weight * vel_u
        q = weight * vel_v
        far_p = by_partner(p)
        far_q = by_partner(q)
        turn = (step + 1) % 8
        fold_p = jnp.where(sub == step, pltpu.roll(far_p, turn, 0) if turn else far_p, fold_p)
        fold_q = jnp.where(sub == step, pltpu.roll(far_q, turn, 0) if turn else far_q, fold_q)
        if step == STEPS - 1:
            break
        far_p = jnp.where(sub == 7, far_p, 0.0)
        far_q = jnp.where(sub == 7, far_q, 0.0)
        along = 0.5 * (p - next_col(p))
        across = 0.5 * (row_below(q) - q + far_q)
        one = one + (along + across)
        two = two + (along - across)
        shear = shear + (row_below(p) - p - far_p) + (q - next_col(q))
        zeta = field(6 + step)
        first = zeta * one
        second = (0.25 * zeta) * two
        third = (0.25 * zeta) * shear
        x = first + second
        y = first - second
        wet_u = jnp.where(wet, vel_u, 0.0)
        wet_v = jnp.where(wet, vel_v, 0.0)
        vel_u = (wet_u - 0.1 * wet_v) + (prev_col(x) - x) + (third - row_above(third))
        vel_v = (wet_v + 0.1 * wet_u) + (prev_col(third) - third) + (y - row_above(y))

    me = lax.axis_index("lon")
    shift = lax.rem(2 * total + HALO - COLS * me, total)
    both = jnp.concatenate(
        [pltpu.roll(fold_p, shift, 1)[:, :LANES], pltpu.roll(fold_q, shift, 1)[:, :LANES]], axis=0
    )
    tall = jnp.concatenate([both, jnp.zeros((LANES - 16, LANES), jnp.float32)], axis=0).T
    for at in range(16):
        folds[at] = pltpu.roll(tall[:EXT], LANES - 1 - at, 1)


def main_kernel(west, east, strips, state_in, zeta_in, mass_in, out, state, zeta, weight, folds):
    vel_u, vel_v, one, two, shear = (state.at[field] for field in range(5))
    fold_values(strips, folds)

    @pl.loop(0, 8)
    def _(at):
        for field in range(5):
            state[field, at] = west[WEST_FIELD[field] + at].astype(jnp.float32)
            state[field, HALO + COLS + at] = east[EAST_FIELD[field] + at].astype(jnp.float32)
        weight[at] = west[WEST_MASS + at].astype(jnp.float32)
        weight[HALO + COLS + at] = east[EAST_MASS + at].astype(jnp.float32)

    @pl.loop(0, STEPS)
    def _(step):
        for at in range(8):
            zeta[step, at] = west[west_slot(step) + at - step].astype(jnp.float32)
            zeta[step, HALO + COLS + at] = east[
                east_slot(step) + (EAST_WIDTH[0] - 1 - step) - at
            ].astype(jnp.float32)

    lane = lax.broadcasted_iota(jnp.int32, (8, LANES), 1)
    sub = lax.broadcasted_iota(jnp.int32, (8, LANES), 0)
    first_lane = lane == 0
    last_lane = lane == LANES - 1
    top = sub == 0
    bottom = sub == 7
    corner = last_lane & bottom

    def row_above(value):
        turned = pltpu.roll(value, LANES - 1, 1)
        even, odd = turned[:8], turned[8:]
        carried = jnp.where(bottom, 0.0, pltpu.roll(even, 7, 0))
        return jnp.concatenate([jnp.where(last_lane, odd, even), jnp.where(last_lane, carried, odd)], 0)

    def row_below(value):
        turned = pltpu.roll(value, 1, 1)
        even, odd = turned[:8], turned[8:]
        carried = jnp.where(top, 0.0, pltpu.roll(odd, 1, 0))
        return jnp.concatenate([jnp.where(first_lane, carried, even), jnp.where(first_lane, even, odd)], 0)

    def at_fold(value, add):
        return jnp.concatenate([value[:8], value[8:] + jnp.where(corner, add, 0.0)], 0)

    def forces(col):
        u, v, w = vel_u[col], vel_v[col], weight[col]
        wet = w != 0.0
        wet_u = jnp.where(wet, u, 0.0)
        wet_v = jnp.where(wet, v, 0.0)
        return w * u, w * v, wet_u - 0.1 * wet_v, wet_v + 0.1 * wet_u

    blank = jnp.zeros((TILE, LANES), jnp.float32)

    @pl.loop(0, STEPS)
    def _(step):
        begin = step
        groups = (2 * STEPS + COLS - 1 - 2 * step + UNROLL - 1) // UNROLL

        def body(group, carry):
            p, q, keep_u, keep_v, west_x, west_c = carry
            for part in range(UNROLL):
                col = begin + group * UNROLL + part
                next_p, next_q, next_u, next_v = forces(col + 1)
                along = 0.5 * (p - next_p)
                across = 0.5 * at_fold(row_below(q) - q, folds[8 + step, pl.ds(col, 1), :])
                turn = at_fold(row_below(p) - p, -folds[step, pl.ds(col, 1), :])
                new_one = one[col] + (along + across)
                new_two = two[col] + (along - across)
                new_shear = shear[col] + turn + (q - next_q)
                one[col] = new_one
                two[col] = new_two
                shear[col] = new_shear
                z = zeta[step, col]
                first = z * new_one
                quarter = 0.25 * z
                second = quarter * new_two
                c = quarter * new_shear
                x = first + second
                y = first - second
                vel_u[col] = keep_u + (west_x - x) + (c - row_above(c))
                vel_v[col] = keep_v + (west_c - c) + (y - row_above(y))
                p, q, keep_u, keep_v, west_x, west_c = next_p, next_q, next_u, next_v, x, c
            return p, q, keep_u, keep_v, west_x, west_c

        lax.fori_loop(0, groups, body, forces(begin) + (blank, blank))

    @pl.loop(0, 8)
    def _(at):
        for field in range(5):
            for half in range(2):
                tile = SHRINK * state[field, HALO + 8 * half + at]
                even, odd = column_slices(at, half)
                out[field, even, :] = tile[:8]
                out[field, odd, :] = tile[8:]


def on_device(final_cot, strains, strength, mass, ice_mask, partner):
    count = lax.axis_size("lon")
    state = as_rows(final_cot)
    whole = pl.BlockSpec(memory_space=pltpu.VMEM)
    hbm = pl.BlockSpec(memory_space=pltpu.HBM)
    f32 = jnp.float32
    bf16 = jnp.bfloat16
    params = pltpu.CompilerParams(vmem_limit_bytes=32 * 1024 * 1024)
    extended = (
        jax.ShapeDtypeStruct((5, EXT, TILE, LANES), f32),
        jax.ShapeDtypeStruct((STEPS, EXT, TILE, LANES), f32),
        jax.ShapeDtypeStruct((EXT, TILE, LANES), f32),
    )
    west_send, east_send, strip_send, state_ext, zeta_ext, mass_ext = pl.pallas_call(
        pack_kernel,
        out_shape=(
            jax.ShapeDtypeStruct((WEST_SIZE, TILE, LANES), bf16),
            jax.ShapeDtypeStruct((EAST_SIZE, TILE, LANES), bf16),
            jax.ShapeDtypeStruct((count, COLS, LANES), bf16),
            *extended,
        ),
        in_specs=[hbm] * 6,
        out_specs=(whole,) * 6,
        scratch_shapes=[
            pltpu.VMEM(state.shape, f32),
            pltpu.VMEM(strains.shape, bf16),
            pltpu.VMEM(strength.shape, f32),
            pltpu.VMEM(mass.shape, f32),
            pltpu.VMEM(ice_mask.shape, jnp.int32),
            pltpu.SMEM(partner.shape, jnp.int32),
            pltpu.VMEM((2, 256, LANES), f32),
            pltpu.SemaphoreType.DMA((5 + STEPS // 2,)),
        ],
        compiler_params=params,
    )(*(pltpu.with_memory_space_constraint(x, pltpu.HBM) for x in (state, strains, strength, mass, ice_mask, partner)))

    west = lax.ppermute(west_send, "lon", [(i, (i + 1) % count) for i in range(count)])
    east = lax.ppermute(east_send, "lon", [(i, (i - 1) % count) for i in range(count)])
    strips = lax.all_to_all(strip_send, "lon", 0, 0, tiled=True).reshape(count * COLS, LANES)

    out = pl.pallas_call(
        main_kernel,
        out_shape=(jax.ShapeDtypeStruct(state.shape, f32), *extended),
        in_specs=[whole] * 6,
        out_specs=(whole,) * 4,
        input_output_aliases={3: 1, 4: 2, 5: 3},
        scratch_shapes=[pltpu.VMEM((16, EXT, LANES), f32)],
        compiler_params=params,
    )(west, east, strips, state_ext, zeta_ext, mass_ext)
    return from_rows(out[0])


def solution(mesh):
    return jax.shard_map(
        on_device,
        mesh=mesh,
        in_specs=(
            P("ens", "lon", None),
            P("ens", None, "lon", None),
            P("lon", None),
            P("lon", None),
            P("lon", None),
            P("lon"),
        ),
        out_specs=P("ens", "lon", None),
        check_vma=False,
    )
```

time: 35.8 us -> 26.7 us (0.75)
  local copies, waits for them, and re-layouts: 5.86 us -> 0 us
  Pallas kernels: 13.8 us -> 10.7 us
    unnamed x12 -> x0, local copies, waits for them, and re-layouts: 5.86 us -> none
    pallas_call x1, Pallas kernels: 12.3 us -> 8.18 us  [on_device(): pl.pallas_call(main_kernel, out_shape=(jax.ShapeDtypeStruct(state.shape,...]
    pallas_call x1, Pallas kernels: 1.49 us -> 2.48 us  [on_device(): pl.pallas_call(pack_kernel, out_shape=(jax.ShapeDtypeStruct((WEST_SIZE, T...]
where the time goes in v2:
time: 26.7 us; the launch traced here: 26.5 us
  Pallas kernels  10.7 us (40%)
  blocking collectives  10.3 us (39%)
  starting transfers between devices  5.53 us (21%)
    all_to_all x1, blocking collectives, on_device(): lax.all_to_all(strip_send, 'lon', 0, 0, tiled=True)  10.3 us
    pallas_call x1, Pallas kernels, on_device(): pl.pallas_call(main_kernel, out_shape=(jax.ShapeDtypeStruct(state.shape,...  8.18 us
    ppermute x1, starting transfers between devices, on_device(): lax.ppermute(east_send, 'lon', [(i, (i - 1) % count) for i in range(count)])  5.03 us
    pallas_call x1, Pallas kernels, on_device(): pl.pallas_call(pack_kernel, out_shape=(jax.ShapeDtypeStruct((WEST_SIZE, T...  2.48 us
  transfers between devices with their start and end apart: 2, of which 0 were waited for; matrix products, arithmetic and copies ran while one was open for 0% of the time, Pallas kernels for 0%

profile of v2, /device:TPU:0, one launch (start us, length us, event | category | flops | bytes accessed | tf_op | source)
XLA Modules:
  0.0 26.5 jit_solution(1081551803061143357)
XLA Ops:
  0.0 2.5 %shard_map.64 = (bf16[84,16,128]{2,1,0:T(8,128)(2,1)S(1)}, bf16[73,16,128]{2,1,0:T(8,128)(2,1)S(1)}, bf16[16,16,128]{2,1,0:T(8,128)(2,1)S(1)}, f32[5,40,16,128]{...) custom-call(f32[5,256,128]{2,1,0:T(8,128)} %bitcast.12, ...), custom_call_target="tpu_custom_call" | custom-call | tf_op jit(solution)/shard_map/pallas_call | solution.py:361
  2.5 0.5 %collective-permute-start = (bf16[84,16,128]{2,1,0:T(8,128)(2,1)S(1)}, bf16[84,16,128]{2,1,0:T(8,128)(2,1)S(1)}, u32[]{:S(2)}, u32[]{:S(2)}) collective-permute-start(bf16[84,16,128]{2,1,0:T(8,128)(2,1)S(1)} %get-tuple-element.12), channel_id=1, source_target_pairs={{0,1},{1,2},{2,3},{3,4},{4,5},{5,6},{6,7},{7,8},{8,9},{9,10},{10,1... | collective-permute-start | bytes 1032200 | tf_op jit(solution)/shard_map/ppermute | solution.py:384
  3.0 5.0 %collective-permute-start.1 = (bf16[73,16,128]{2,1,0:T(8,128)(2,1)S(1)}, bf16[73,16,128]{2,1,0:T(8,128)(2,1)S(1)}, u32[]{:S(2)}, u32[]{:S(2)}) collective-permute-start(bf16[73,16,128]{2,1,0:T(8,128)(2,1)S(1)} %get-tuple-element.13), channel_id=1, source_target_pairs={{0,15},{1,0},{2,1},{3,2},{4,3},{5,4},{6,5},{7,6},{8,7},{9,8},{10,9... | collective-permute-start | bytes 897032 | tf_op jit(solution)/shard_map/ppermute | solution.py:385
  8.0 10.3 %all_to_all.5 = bf16[16,16,128]{2,1,0:T(8,128)(2,1)S(1)} all-to-all(bf16[16,16,128]{2,1,0:T(8,128)(2,1)S(1)} %get-tuple-element.14), channel_id=1, replica_groups=mesh['ens'=2,'lon'=16] {'lon'}, dimensions={0} | all-to-all | bytes 131072 | tf_op jit(solution)/shard_map/all_to_all | solution.py:386
  18.3 0.0 collective-permute-done.1.east
  18.3 0.0 collective-permute-done.west
  18.3 8.2 %shard_map.65 = (f32[5,256,128]{2,1,0:T(8,128)}, f32[5,40,16,128]{3,2,1,0:T(8,128)S(1)}, f32[8,40,16,128]{3,2,1,0:T(8,128)S(1)}, f32[40,16,128]{2,1,0:T(8,128)S(1)}) custom-call(bf16[84,16,128]{2,1,0:T(8,128)(2,1)S(1)} %collective-permute-done.west, ...), custom_call_target="tpu_custom_call", output_to_operand_aliasing={{1}: (3, {}), {2}: (4, {}), {3}: (5, {})} | custom-call | tf_op jit(solution)/shard_map/pallas_call | solution.py:388
Async XLA Ops:
  2.5 15.8 %collective-permute-start = (bf16[84,16,128]{2,1,0:T(8,128)(2,1)S(1)}, bf16[84,16,128]{2,1,0:T(8,128)(2,1)S(1)}, u32[]{:S(2)}, u32[]{:S(2)}) collective-permute-start(bf16[84,16,128]{2,1,0:T(8,128)(2,1)S(1)} %get-tuple-element.12), channel_id=1, source_target_pairs={{0,1},{1,2},{2,3},{3,4},{4,5},{5,6},{6,7},{7,8},{8,9},{9,10},{10,1... | collective-permute-start | bytes 1032200 | tf_op jit(solution)/shard_map/ppermute | solution.py:384
  3.0 15.3 %collective-permute-start.1 = (bf16[73,16,128]{2,1,0:T(8,128)(2,1)S(1)}, bf16[73,16,128]{2,1,0:T(8,128)(2,1)S(1)}, u32[]{:S(2)}, u32[]{:S(2)}) collective-permute-start(bf16[73,16,128]{2,1,0:T(8,128)(2,1)S(1)} %get-tuple-element.13), channel_id=1, source_target_pairs={{0,15},{1,0},{2,1},{3,2},{4,3},{5,4},{6,5},{7,6},{8,7},{9,8},{10,9... | collective-permute-start | bytes 897032 | tf_op jit(solution)/shard_map/ppermute | solution.py:385

commit v3 on v2

v3 whole, which is shorter than its diff:
```python
import functools

import jax
import jax.numpy as jnp
from jax import lax
from jax.experimental import pallas as pl
from jax.experimental.pallas import tpu as pltpu
from jax.sharding import PartitionSpec as P

COLS = 16
STEPS = 8
HALO = 8
TILE = 16
LANES = 128
GROUPS = 16
EXT = 40
UNROLL = 8

WEST_WIDTH = [STEPS + 1 - step for step in range(1, STEPS + 1)]
EAST_WIDTH = [STEPS - step for step in range(1, STEPS + 1)]
WEST_FIELD = [0, 8, 16, 24, 32]
WEST_COUNT = [8, 8, 8, 8, 8]
WEST_MASS = 40
WEST_ZETA = [48 + sum(WEST_WIDTH[:k]) for k in range(STEPS)]
WEST_SIZE = 48 + sum(WEST_WIDTH)
EAST_FIELD = [0, 8, 16, 23, 30]
EAST_COUNT = [8, 8, 7, 7, 7]
EAST_MASS = 37
EAST_ZETA = [45 + sum(EAST_WIDTH[:k]) for k in range(STEPS)]
EAST_SIZE = 45 + sum(EAST_WIDTH)
STRIP = 24
STRIP_FIELDS = 5
STRIP_PARTS = 3
EAST_END = EXT + 7
SHRINK = (5.0 / 6.0) ** STEPS


def as_rows(field):
    lead = field.shape[:-2]
    tiled = field.reshape(lead + (2, 8, GROUPS, LANES)).swapaxes(-3, -2)
    return tiled.reshape(lead + (2 * GROUPS * 8, LANES))


def from_rows(field):
    lead = field.shape[:-2]
    tiled = field.reshape(lead + (2, GROUPS, 8, LANES)).swapaxes(-3, -2)
    return tiled.reshape(lead + (COLS, GROUPS * LANES))


def column_slices(col, half):
    start = half * 128 + col
    return pl.ds(start, 8, 16), pl.ds(start + 8, 8, 16)


def column_tile(load, col, half):
    even, odd = column_slices(col, half)
    return jnp.concatenate([load(even), load(odd)], axis=0)


def west_slot(step):
    return 48 + STEPS * step - (step * (step - 1)) // 2


def east_slot(step):
    return 45 + (STEPS - 1) * step - (step * (step - 1)) // 2


def viscosity(rates, strength):
    square = rates[0] * rates[0] + 0.25 * (rates[1] * rates[1] + rates[2] * rates[2])
    return (0.1 * strength) * lax.rsqrt(jnp.maximum(square, 0.25))


def pack_kernel(
    state_hbm, strains_hbm, strength_hbm, mass_hbm, mask_hbm, partner_hbm,
    west_out, east_out, strip_out, own_out, state_out, zeta_out, mass_out,
    state, strains, strength, mass, mask, partner, rows, top, sems,
):
    bf16 = jnp.bfloat16
    cell_copies = [
        pltpu.make_async_copy(mass_hbm, mass, sems.at[0]),
        pltpu.make_async_copy(mask_hbm, mask, sems.at[1]),
    ]
    state_copy = pltpu.make_async_copy(state_hbm, state, sems.at[2])
    late_copies = [
        pltpu.make_async_copy(strength_hbm, strength, sems.at[3]),
        pltpu.make_async_copy(partner_hbm, partner, sems.at[4]),
    ]
    strain_copies = [
        pltpu.make_async_copy(strains_hbm.at[2 * k : 2 * k + 2], strains.at[2 * k : 2 * k + 2], sems.at[5 + k])
        for k in range(STEPS // 2)
    ]
    for copy in [*cell_copies, state_copy, *late_copies, *strain_copies]:
        copy.start()

    for copy in cell_copies:
        copy.wait()
    for group in range(GROUPS):
        at = slice(LANES * group, LANES * group + LANES)
        weight = mask[:, at].astype(jnp.float32) / (6.0 * mass[:, at])
        rows[0, 8 * group : 8 * group + 8] = weight[:8]
        rows[0, 128 + 8 * group : 136 + 8 * group] = weight[8:]
    top[5] = weight
    for at in range(8):
        tile = column_tile(lambda part: rows[0, part, :], at, 0)
        mass_out[HALO + at] = tile
        east_out[EAST_MASS + at] = tile.astype(bf16)
        tile = column_tile(lambda part: rows[0, part, :], at, 1)
        mass_out[HALO + 8 + at] = tile
        west_out[WEST_MASS + at] = tile.astype(bf16)
    spared = mass_out[HALO + 7].astype(bf16)
    east_first = mass_out[HALO].astype(bf16)

    state_copy.wait()

    @pl.loop(0, 8)
    def _(turn):
        at = 7 - turn
        for field in range(5):
            tile = column_tile(lambda part: state[field, part, :], at, 0)
            state_out[field, HALO + at] = tile
            east_out[EAST_FIELD[field] + at] = tile.astype(bf16)
            tile = column_tile(lambda part: state[field, part, :], at, 1)
            state_out[field, HALO + 8 + at] = tile
            west_out[WEST_FIELD[field] + at] = tile.astype(bf16)

    for field in range(5):
        top[field, :8] = state[field, 120:128, :]
        top[field, 8:] = state[field, 248:256, :]
    for copy in late_copies:
        copy.wait()

    def cycle_zeta(cycle, step, rows):
        for group in range(GROUPS):
            at = slice(LANES * group, LANES * group + LANES)
            rates = [strains[cycle, k, :, at].astype(jnp.float32) for k in range(3)]
            zeta = viscosity(rates, strength[:, at])
            rows[8 * group : 8 * group + 8] = zeta[:8]
            rows[128 + 8 * group : 136 + 8 * group] = zeta[8:]
        top[6 + step] = zeta
        for at in range(8):
            tile = column_tile(lambda part: rows[part, :], at, 0)
            zeta_out[step, HALO + at] = tile
            east_out[east_slot(step) + (EAST_WIDTH[0] - 1 - step) - at] = tile.astype(bf16)
            tile = column_tile(lambda part: rows[part, :], at, 1)
            zeta_out[step, HALO + 8 + at] = tile
            west_out[west_slot(step) + at - step] = tile.astype(bf16)

    @pl.loop(0, STEPS // 2)
    def _(turn):
        pltpu.make_async_copy(
            strains_hbm.at[pl.ds(2 * turn, 2)], strains.at[pl.ds(2 * turn, 2)], sems.at[5 + turn]
        ).wait()
        for part in range(2):
            cycle = 2 * turn + part
            cycle_zeta(cycle, STEPS - 1 - cycle, rows.at[part])

    east_out[EAST_MASS] = east_first
    east_out[EAST_MASS + 7] = spared

    lane = lax.broadcasted_iota(jnp.int32, (COLS, LANES), 1)
    row_at = lax.broadcasted_iota(jnp.int32, (COLS, LANES), 0)
    place = jnp.zeros((COLS, LANES), jnp.int32)
    for col in range(COLS):
        place = jnp.where(row_at == col, lax.rem(partner[col], COLS), place)
    strips = [place.astype(jnp.float32)] + [jnp.zeros((COLS, LANES), jnp.float32)] * (STRIP_PARTS - 1)
    for at in range(6 + STEPS):
        part, begin = at // STRIP_FIELDS, STRIP * (at % STRIP_FIELDS)
        moved = pltpu.roll(top[at], (begin + STRIP) % LANES, 1)
        strips[part] = jnp.where((lane >= begin) & (lane < begin + STRIP), moved, strips[part])
    for part in range(STRIP_PARTS):
        own_out[0, part] = strips[part]
        strip_out[0, part] = strips[part].astype(bf16)


def join_kernel(count, *refs):
    out = refs[(len(refs) + count - 1) // 2]
    at = 0
    for part in refs[:count]:
        size = part.shape[0]
        out[at : at + size] = part[...]
        at += size


def fold_kernel(offsets, *refs):
    *parts, own, last_tiles, _, out, strips, tiles, sems = refs
    me = lax.axis_index("lon")
    blocks = strips.shape[0]
    total = blocks * COLS
    count = total // LANES
    order = iter(offsets)
    for part in parts:
        for k in range(part.shape[0]):
            strips[next(order)] = part[k].astype(jnp.float32)
    strips[0] = own[0]
    lane = lax.broadcasted_iota(jnp.int32, (STRIP, LANES), 1)
    sub = lax.broadcasted_iota(jnp.int32, (STRIP, total), 0)
    last = sub == STRIP - 1
    turned = [
        [
            jnp.concatenate([strips[lax.bitwise_xor(me, 8 * r + k), part] for k in range(8)], axis=0).T
            for r in range(count)
        ]
        for part in range(STRIP_PARTS)
    ]

    def field(at):
        part, begin = at // STRIP_FIELDS, STRIP * (at % STRIP_FIELDS)
        return jnp.concatenate([tile[begin : begin + STRIP] for tile in turned[part]], axis=1)

    begin = STRIP * STRIP_FIELDS
    places = [
        (7 - lane[:8] // COLS) * COLS + jnp.broadcast_to(tile[begin : begin + 1], (8, LANES)).astype(jnp.int32)
        for tile in turned[0]
    ]

    def at_fold(value):
        rows = [
            jnp.take_along_axis(
                value[STRIP - 8 :, LANES * (count - 1 - r) : LANES * (count - r)], places[r], axis=1,
                mode="promise_in_bounds",
            )
            for r in range(count)
        ]
        far = jnp.where(last[:8] | last[STRIP - 8 :], jnp.concatenate(rows, axis=1), 0.0)
        return jnp.concatenate([jnp.zeros((STRIP - 8, total), jnp.float32), far], axis=0)

    def next_col(value):
        return pltpu.roll(value, total - 1, 1)

    def prev_col(value):
        return pltpu.roll(value, 1, 1)

    def row_above(value):
        return jnp.where(last, 0.0, pltpu.roll(value, STRIP - 1, 0))

    def row_below(value):
        return pltpu.roll(value, 1, 0)

    vel_u, vel_v, one, two, shear, weight = (field(at) for at in range(6))
    wet = weight != 0.0
    for step in range(STEPS):
        p = weight * vel_u
        q = weight * vel_v
        along = 0.5 * (p - next_col(p))
        across = 0.5 * (row_below(q) - q + at_fold(q))
        one = one + (along + across)
        two = two + (along - across)
        shear = shear + (row_below(p) - p - at_fold(p)) + (q - next_col(q))
        zeta = field(6 + step)
        first = zeta * one
        quarter = 0.25 * zeta
        second = quarter * two
        third = quarter * shear
        x = first + second
        y = first - second
        wet_u = jnp.where(wet, vel_u, 0.0)
        wet_v = jnp.where(wet, vel_v, 0.0)
        vel_u = (wet_u - 0.1 * wet_v) + (prev_col(x) - x) + (third - row_above(third))
        vel_v = (wet_v + 0.1 * wet_u) + (prev_col(third) - third) + (y - row_above(y))

    shift = lax.rem(total - COLS * me, total)
    rows = [pltpu.roll(value, shift, 1)[:, :LANES] for value in (vel_u, vel_v, one, two, shear)]
    rows.append(jnp.zeros((LANES - STRIP * STRIP_FIELDS, LANES), jnp.float32))
    top = SHRINK * jnp.concatenate(rows, axis=0).T[:COLS]
    reached = lane[:COLS] >= LANES - STEPS - 1
    for field in range(5):
        moved = pltpu.roll(top, (LANES - STRIP - STRIP * field) % LANES, 1)
        tiles[field] = jnp.where(reached, moved, last_tiles[field])
    copies = [
        pltpu.make_async_copy(tiles.at[:, 8 * half : 8 * half + 8, :], out.at[:, pl.ds(128 * half + 120, 8), :], sems.at[half])
        for half in range(2)
    ]
    for copy in copies:
        copy.start()
    for copy in copies:
        copy.wait()


def stepper(state, zeta, weight):
    vel_u, vel_v, one, two, shear = (state.at[field] for field in range(5))
    lane = lax.broadcasted_iota(jnp.int32, (8, LANES), 1)
    sub = lax.broadcasted_iota(jnp.int32, (8, LANES), 0)
    first_lane = lane == 0
    last_lane = lane == LANES - 1
    top = sub == 0
    bottom = sub == 7

    def row_above(value):
        turned = pltpu.roll(value, LANES - 1, 1)
        even, odd = turned[:8], turned[8:]
        carried = jnp.where(bottom, 0.0, pltpu.roll(even, 7, 0))
        return jnp.concatenate([jnp.where(last_lane, odd, even), jnp.where(last_lane, carried, odd)], 0)

    def row_below(value):
        turned = pltpu.roll(value, 1, 1)
        even, odd = turned[:8], turned[8:]
        carried = jnp.where(top, 0.0, pltpu.roll(odd, 1, 0))
        return jnp.concatenate([jnp.where(first_lane, carried, even), jnp.where(first_lane, even, odd)], 0)

    def forces(place, col):
        u, v, w = vel_u[place], vel_v[place], weight[col]
        wet = w != 0.0
        wet_u = jnp.where(wet, u, 0.0)
        wet_v = jnp.where(wet, v, 0.0)
        return w * u, w * v, wet_u - 0.1 * wet_v, wet_v + 0.1 * wet_u

    def strains_of(step, col, one_at, two_at, shear_at):
        z = zeta[step, col]
        first = z * one_at
        quarter = 0.25 * z
        second = quarter * two_at
        return first + second, quarter * shear_at, first - second

    def stored_strains(step, place, col):
        return strains_of(step, col, one[place], two[place], shear[place])

    def velocities(keep_u, keep_v, west_x, west_c, x, c, y):
        return keep_u + (west_x - x) + (c - row_above(c)), keep_v + (west_c - c) + (y - row_above(y))

    def advance(step, place, next_place, col, carry):
        p, q, keep_u, keep_v, west_x, west_c = carry
        next_p, next_q, next_u, next_v = forces(next_place, col + 1)
        along = 0.5 * (p - next_p)
        across = 0.5 * (row_below(q) - q)
        turn = row_below(p) - p
        new_one = one[place] + (along + across)
        new_two = two[place] + (along - across)
        new_shear = shear[place] + turn + (q - next_q)
        x, c, y = strains_of(step, col, new_one, new_two, new_shear)
        new_u, new_v = velocities(keep_u, keep_v, west_x, west_c, x, c, y)
        return (new_u, new_v, new_one, new_two, new_shear), (next_p, next_q, next_u, next_v, x, c)

    return forces, stored_strains, velocities, advance


def inner_kernel(state_in, zeta, weight, sides, state):
    forces, _, _, advance = stepper(state, zeta, weight)
    blank = jnp.zeros((TILE, LANES), jnp.float32)

    @pl.loop(0, STEPS)
    def _(step):
        begin = HALO + step
        last = HALO + COLS - 2 - step

        def body(group, carry):
            for part in range(UNROLL):
                col = begin + group * UNROLL + part
                new, carry = advance(step, col, col + 1, col, carry)
                for field in range(5):
                    valid = (col <= last) & (col > begin) if field < 2 else col <= last
                    state[field, col] = jnp.where(valid, new[field], state[field, col])
            return carry

        lax.fori_loop(0, (last - begin + UNROLL) // UNROLL, body, forces(begin, begin) + (blank, blank))

    @pl.loop(0, 9)
    def _(at):
        for field in range(5):
            sides[field, HALO + at] = state[field, HALO + at]
            sides[field, EAST_END - HALO - 7 - at] = state[field, HALO + 7 + at]


def edge_kernel(west, east, state_in, zeta_in, mass_in, out, last, state, zeta, weight):
    @pl.loop(0, 8)
    def _(at):
        for field in range(5):
            state[field, at] = west[WEST_FIELD[field] + at].astype(jnp.float32)
            state[field, EAST_END - HALO - COLS - at] = east[EAST_FIELD[field] + at].astype(jnp.float32)
        weight[at] = west[WEST_MASS + at].astype(jnp.float32)
        weight[HALO + COLS + at] = east[EAST_MASS + at].astype(jnp.float32)

    @pl.loop(0, STEPS)
    def _(step):
        for at in range(8):
            zeta[step, at] = west[west_slot(step) + at - step].astype(jnp.float32)
            zeta[step, HALO + COLS + at] = east[
                east_slot(step) + (EAST_WIDTH[0] - 1 - step) - at
            ].astype(jnp.float32)

    forces, stored_strains, velocities, advance = stepper(state, zeta, weight)
    blank = jnp.zeros((TILE, LANES), jnp.float32)

    start = EAST_END - (HALO + COLS - 1)

    @pl.loop(0, STEPS)
    def _(step):
        begin = HALO + COLS - 1 - step
        x, c, _ = stored_strains(step, step + (start + 1), begin - 1)
        carry = forces(step + start, begin) + (x, c)
        west_carry = forces(step, step) + (blank, blank)
        for part in range(8):
            new, carry = advance(step, step + (start - part), step + (start - part - 1), begin + part, carry)
            west_new, west_carry = advance(step, step + part, step + part + 1, step + part, west_carry)
            for field in range(5):
                state[field, step + (start - part)] = new[field]
                state[field, step + part] = west_new[field]
        u, v = velocities(*west_carry[2:], *stored_strains(step, step + 8, step + 8))
        state[0, step + 8] = u
        state[1, step + 8] = v

    @pl.loop(0, 8)
    def _(at):
        for field in range(5):
            for half in range(2):
                tile = SHRINK * state[field, (HALO + at, EAST_END - HALO - 8 - at)[half]]
                even, odd = column_slices(at, half)
                out[field, even, :] = tile[:8]
                out[field, odd, :] = tile[8:]

    for field in range(5):
        last[field, :8] = out[field, 120:128, :]
        last[field, 8:] = out[field, 248:256, :]


def join(parts, passed):
    whole = pl.BlockSpec(memory_space=pltpu.VMEM)
    size = sum(part.shape[0] for part in parts)
    held, *passed = pl.pallas_call(
        functools.partial(join_kernel, len(parts)),
        out_shape=(
            jax.ShapeDtypeStruct((size, *parts[0].shape[1:]), parts[0].dtype),
            *(jax.ShapeDtypeStruct(x.shape, x.dtype) for x in passed),
        ),
        in_specs=[whole] * (len(parts) + len(passed)),
        out_specs=(whole,) * (1 + len(passed)),
        input_output_aliases={len(parts) + k: 1 + k for k in range(len(passed))},
        compiler_params=pltpu.CompilerParams(vmem_limit_bytes=16 * 1024 * 1024),
    )(*parts, *passed)
    return held, passed


def gather_stages(count):
    stages = []
    bit = 4
    while bit < count:
        stages.append((bit, 2 * bit, 3 * bit) if 2 * bit < count else (bit,))
        bit *= 4
    return stages + [(1,), (2,)]


def exchange(held, steps, count):
    return [held] + [lax.ppermute(held, "lon", [(i, i ^ step) for i in range(count)]) for step in steps]


def on_device(final_cot, strains, strength, mass, ice_mask, partner):
    count = lax.axis_size("lon")
    whole = pl.BlockSpec(memory_space=pltpu.VMEM)
    hbm = pl.BlockSpec(memory_space=pltpu.HBM)
    f32 = jnp.float32
    bf16 = jnp.bfloat16
    params = pltpu.CompilerParams(vmem_limit_bytes=16 * 1024 * 1024)
    cells = [
        pltpu.with_memory_space_constraint(x, pltpu.HBM)
        for x in (as_rows(final_cot), strains, strength, mass, ice_mask, partner)
    ]
    state_shape = cells[0].shape
    extended = (
        jax.ShapeDtypeStruct((5, EXT, TILE, LANES), f32),
        jax.ShapeDtypeStruct((STEPS, EXT, TILE, LANES), f32),
        jax.ShapeDtypeStruct((EXT, TILE, LANES), f32),
    )
    sends = (
        jax.ShapeDtypeStruct((WEST_SIZE, TILE, LANES), bf16),
        jax.ShapeDtypeStruct((EAST_SIZE, TILE, LANES), bf16),
    )
    west_send, east_send, strip, own_strip, state, zeta, weight = pl.pallas_call(
        pack_kernel,
        out_shape=(
            *sends,
            jax.ShapeDtypeStruct((1, STRIP_PARTS, COLS, LANES), bf16),
            jax.ShapeDtypeStruct((1, STRIP_PARTS, COLS, LANES), f32),
            *extended,
        ),
        in_specs=[hbm] * 6,
        out_specs=(whole,) * 7,
        scratch_shapes=[
            pltpu.VMEM(state_shape, f32),
            pltpu.VMEM(strains.shape, bf16),
            pltpu.VMEM(strength.shape, f32),
            pltpu.VMEM(mass.shape, f32),
            pltpu.VMEM(ice_mask.shape, jnp.int32),
            pltpu.SMEM(partner.shape, jnp.int32),
            pltpu.VMEM((2, 256, LANES), f32),
            pltpu.VMEM((6 + STEPS, COLS, LANES), f32),
            pltpu.SemaphoreType.DMA((5 + STEPS // 2,)),
        ],
        compiler_params=params,
    )(*cells)
    west = lax.ppermute(west_send, "lon", [(i, (i + 1) % count) for i in range(count)])
    east = lax.ppermute(east_send, "lon", [(i, (i - 1) % count) for i in range(count)])
    state, _ = pl.pallas_call(
        inner_kernel,
        out_shape=(extended[0], extended[0]),
        in_specs=[whole] * 3,
        out_specs=(whole,) * 2,
        input_output_aliases={0: 1},
        compiler_params=params,
    )(state, zeta, weight)
    offsets = [0]
    parts = [strip]
    for steps in gather_stages(count):
        held = parts[0]
        if len(parts) > 1:
            held, (state,) = join(parts, (state,))
        parts = exchange(held, steps, count)
        offsets = [offset ^ step for step in (0, *steps) for offset in offsets]
    out, last, *_ = pl.pallas_call(
        edge_kernel,
        out_shape=(
            jax.ShapeDtypeStruct(state_shape, f32),
            jax.ShapeDtypeStruct((5, COLS, LANES), f32),
            *extended,
        ),
        in_specs=[whole] * 5,
        out_specs=(whole,) * 5,
        input_output_aliases={2: 2, 3: 3, 4: 4},
        compiler_params=params,
    )(west, east, state, zeta, weight)
    out = pl.pallas_call(
        functools.partial(fold_kernel, offsets),
        out_shape=jax.ShapeDtypeStruct(state_shape, f32),
        in_specs=[whole] * (len(parts) + 2) + [hbm],
        out_specs=hbm,
        input_output_aliases={len(parts) + 2: 0},
        scratch_shapes=[
            pltpu.VMEM((count, STRIP_PARTS, COLS, LANES), f32),
            pltpu.VMEM((5, COLS, LANES), f32),
            pltpu.SemaphoreType.DMA((2,)),
        ],
        compiler_params=params,
    )(*parts, own_strip, last, pltpu.with_memory_space_constraint(out, pltpu.HBM))
    return from_rows(out)


def solution(mesh):
    return jax.shard_map(
        on_device,
        mesh=mesh,
        in_specs=(
            P("ens", "lon", None),
            P("ens", None, "lon", None),
            P("lon", None),
            P("lon", None),
            P("lon", None),
            P("lon"),
        ),
        out_specs=P("ens", "lon", None),
        check_vma=False,
    )
```

time: 26.7 us -> 24.1 us (0.903)
  blocking collectives: 10.3 us -> 0 us
  starting transfers between devices: 5.53 us -> 10.1 us
  waiting for transfers between devices: 0.01 us -> 1.81 us
  Pallas kernels: 10.7 us -> 12 us
    all_to_all x1 -> x0, blocking collectives: 10.3 us -> none  [on_device(): lax.all_to_all(strip_send, 'lon', 0, 0, tiled=True)]
    ppermute x0 -> x5, starting transfers between devices: none -> 4.54 us  [exchange(): lax.ppermute(held, 'lon', [(i, i ^ step) for i in range(count)])]
    ppermute x0 -> x5, waiting for transfers between devices: none -> 1.8 us  [exchange(): lax.ppermute(held, 'lon', [(i, i ^ step) for i in range(count)])]
    pallas_call x2 -> x6, Pallas kernels: 10.7 us -> 12 us  [the longest x1 4.2 us: on_device(): pl.pallas_call(edge_kernel, out_shape=(jax.ShapeDtypeStruct(state_shape,...]
  transfers between devices with their start and end apart: 2 -> 7, of which waited for: 0 -> 2; matrix products, arithmetic and copies ran while one was open for 0% -> 0% of each run, Pallas kernels for 0% -> 30%
where the time goes in v3:
time: 24.1 us; the launch traced here: 23.9 us
  Pallas kernels  12 us (50%)
  starting transfers between devices  10.1 us (42%)
  waiting for transfers between devices  1.81 us (8%)
    ppermute x1, starting transfers between devices, on_device(): lax.ppermute(east_send, 'lon', [(i, (i - 1) % count) for i in range(count)])  5.03 us
    ppermute x5, starting transfers between devices, exchange(): lax.ppermute(held, 'lon', [(i, i ^ step) for i in range(count)])  4.54 us
    pallas_call x1, Pallas kernels, on_device(): pl.pallas_call(edge_kernel, out_shape=(jax.ShapeDtypeStruct(state_shape,...  4.2 us
    pallas_call x1, Pallas kernels, on_device(): pl.pallas_call(inner_kernel, out_shape=(extended[0], extended[0]), in_spe...  2.95 us
    pallas_call x1, Pallas kernels, on_device(): pl.pallas_call(pack_kernel, out_shape=(*sends, jax.ShapeDtypeStruct((1, S...  2.51 us
    pallas_call x1, Pallas kernels, on_device(): pl.pallas_call(functools.partial(fold_kernel, offsets), out_shape=jax.Sha...  2.31 us
    ppermute x5, waiting for transfers between devices, exchange(): lax.ppermute(held, 'lon', [(i, i ^ step) for i in range(count)])  1.8 us
    ppermute x1, starting transfers between devices, on_device(): lax.ppermute(west_send, 'lon', [(i, (i + 1) % count) for i in range(count)])  0.5 us
  transfers between devices with their start and end apart: 7, of which 2 were waited for; matrix products, arithmetic and copies ran while one was open for 0% of the time, Pallas kernels for 30%

profile of v3, /device:TPU:0, one launch (start us, length us, event | category | flops | bytes accessed | tf_op | source)
XLA Modules:
  0.0 23.9 jit_solution(15024699396040740010)
XLA Ops:
  0.0 2.5 %shard_map.64 = (bf16[84,16,128]{2,1,0:T(8,128)(2,1)S(1)}, bf16[73,16,128]{2,1,0:T(8,128)(2,1)S(1)}, bf16[1,3,16,128]{3,2,1,0:T(8,128)(2,1)S(1)}, f32[1,3,16,128...) custom-call(f32[5,256,128]{2,1,0:T(8,128)} %bitcast.10, ...), custom_call_target="tpu_custom_call" | custom-call | tf_op jit(solution)/shard_map/pallas_call | solution.py:466
  2.5 0.5 %collective-permute-start.5 = (bf16[84,16,128]{2,1,0:T(8,128)(2,1)S(1)}, bf16[84,16,128]{2,1,0:T(8,128)(2,1)S(1)}, u32[]{:S(2)}, u32[]{:S(2)}) collective-permute-start(bf16[84,16,128]{2,1,0:T(8,128)(2,1)S(1)} %get-tuple-element.28), channel_id=1, source_target_pairs={{0,1},{1,2},{2,3},{3,4},{4,5},{5,6},{6,7},{7,8},{8,9},{9,10},{10,1... | collective-permute-start | bytes 1032200 | tf_op jit(solution)/shard_map/ppermute | solution.py:489
  3.0 5.0 %collective-permute-start.6 = (bf16[73,16,128]{2,1,0:T(8,128)(2,1)S(1)}, bf16[73,16,128]{2,1,0:T(8,128)(2,1)S(1)}, u32[]{:S(2)}, u32[]{:S(2)}) collective-permute-start(bf16[73,16,128]{2,1,0:T(8,128)(2,1)S(1)} %get-tuple-element.29), channel_id=1, source_target_pairs={{0,15},{1,0},{2,1},{3,2},{4,3},{5,4},{6,5},{7,6},{8,7},{9,8},{10,9... | collective-permute-start | bytes 897032 | tf_op jit(solution)/shard_map/ppermute | solution.py:490
  8.1 2.2 %collective-permute-start.2 = (bf16[1,3,16,128]{3,2,1,0:T(8,128)(2,1)S(1)}, bf16[1,3,16,128]{3,2,1,0:T(8,128)(2,1)S(1)}, u32[]{:S(2)}, u32[]{:S(2)}) collective-permute-start(bf16[1,3,16,128]{3,2,1,0:T(8,128)(2,1)S(1)} %get-tuple-element.19.refs_0_), channel_id=1, source_target_pairs={{0,12},{1,13},{2,14},{3,15},{4,8},{5,9},{6,10},{7,11},{8,4},{9,5},... | collective-permute-start | bytes 36872 | tf_op jit(solution)/shard_map/ppermute | solution.py:442
  10.3 0.0 collective-permute-start.1
  10.3 2.2 %collective-permute-start = (bf16[1,3,16,128]{3,2,1,0:T(8,128)(2,1)S(1)}, bf16[1,3,16,128]{3,2,1,0:T(8,128)(2,1)S(1)}, u32[]{:S(2)}, u32[]{:S(2)}) collective-permute-start(bf16[1,3,16,128]{3,2,1,0:T(8,128)(2,1)S(1)} %get-tuple-element.19.refs_0_), channel_id=1, source_target_pairs={{0,4},{1,5},{2,6},{3,7},{4,0},{5,1},{6,2},{7,3},{8,12},{9,13},{10,... | collective-permute-start | bytes 36872 | tf_op jit(solution)/shard_map/ppermute | solution.py:442
  12.4 2.9 %shard_map.65 = (f32[5,40,16,128]{3,2,1,0:T(8,128)S(1)}, f32[5,40,16,128]{3,2,1,0:T(8,128)S(1)}) custom-call(f32[5,40,16,128]{3,2,1,0:T(8,128)S(1)} %get-tuple-element.20.state_in, f32[8,40,16,128]{3,2,1,0:T(8,128)S(1)} %get-tuple-element.21.zeta.zeta_in, f32[40,16,128]{2,1,0:T(8,128)S(1)} %get-tuple-element.22.weight.mass_in), custom_call_target="tpu_custom_call", output_to_operand_aliasing={{1}: (0, {})} | custom-call | tf_op jit(solution)/shard_map/pallas_call | solution.py:491
  15.4 0.0 collective-permute-done.2.refs_3_
  15.4 0.0 collective-permute-done.1.refs_2_
  15.4 0.0 collective-permute-done.refs_1_
  15.4 0.1 collective-permute-start.3
  15.5 1.2 %collective-permute-done.3.refs_1_ = bf16[4,3,16,128]{3,2,1,0:T(8,128)(2,1)S(1)} collective-permute-done((bf16[4,3,16,128]{3,2,1,0:T(8,128)(2,1)S(1)}, bf16[4,3,16,128]{3,2,1,0:T(8,128)(2,1)S(1)}, u32[]{:S(2)}, u32[]{:S(2)}) %collective-permute-start.3) | collective-permute-done | bytes 49184 | tf_op jit(solution)/shard_map/ppermute | solution.py:442
  16.8 0.1 collective-permute-start.4
  16.8 0.0 collective-permute-done.6.east
  16.8 0.0 collective-permute-done.5.west
  16.9 4.2 %shard_map.68 = (f32[5,256,128]{2,1,0:T(8,128)}, f32[5,16,128]{2,1,0:T(8,128)S(1)}, f32[5,40,16,128]{3,2,1,0:T(8,128)S(1)}, f32[8,40,16,128]{3,2,1,0:T(8,128)S(1)}, f32[40,16,128]{2,1,0:T(8,128)S(1)}) custom-call(bf16[84,16,128]{2,1,0:T(8,128)(2,1)S(1)} %collective-permute-done.5.west, ...), custom_call_target="tpu_custom_call", output_to_operand_aliasing={{2}: (2, {}), {3}: (3, {}), {4}: (4, {})} | custom-call | tf_op jit(solution)/shard_map/pallas_call | solution.py:507
  21.1 0.6 %collective-permute-done.4.refs_1_ = bf16[8,3,16,128]{3,2,1,0:T(8,128)(2,1)S(1)} collective-permute-done((bf16[8,3,16,128]{3,2,1,0:T(8,128)(2,1)S(1)}, bf16[8,3,16,128]{3,2,1,0:T(8,128)(2,1)S(1)}, u32[]{:S(2)}, u32[]{:S(2)}) %collective-permute-start.4) | collective-permute-done | bytes 98336 | tf_op jit(solution)/shard_map/ppermute | solution.py:442
  21.6 2.3 %shard_map.69 = f32[5,256,128]{2,1,0:T(8,128)} custom-call(bf16[8,3,16,128]{3,2,1,0:T(8,128)(2,1)S(1)} %get-tuple-element.26.refs_0_, bf16[8,3,16,128]{3,2,1,0:T(8,128)(2,1)S(1)} %collective-permute-done.4.refs_1_, f32[1,3,16,128]{3,2,1,0:T(8,128)S(1)} %get-tuple-element.27.refs_2_, ...), custom_call_target="tpu_custom_call", output_to_operand_aliasing={{}: (4, {})} | custom-call | tf_op jit(solution)/shard_map/pallas_call | solution.py:519
  (2 shorter events, 0.0 us)
Async XLA Ops:
  2.5 14.3 %collective-permute-start.5 = (bf16[84,16,128]{2,1,0:T(8,128)(2,1)S(1)}, bf16[84,16,128]{2,1,0:T(8,128)(2,1)S(1)}, u32[]{:S(2)}, u32[]{:S(2)}) collective-permute-start(bf16[84,16,128]{2,1,0:T(8,128)(2,1)S(1)} %get-tuple-element.28), channel_id=1, source_target_pairs={{0,1},{1,2},{2,3},{3,4},{4,5},{5,6},{6,7},{7,8},{8,9},{9,10},{10,1... | collective-permute-start | bytes 1032200 | tf_op jit(solution)/shard_map/ppermute | solution.py:489
  3.0 13.8 %collective-permute-start.6 = (bf16[73,16,128]{2,1,0:T(8,128)(2,1)S(1)}, bf16[73,16,128]{2,1,0:T(8,128)(2,1)S(1)}, u32[]{:S(2)}, u32[]{:S(2)}) collective-permute-start(bf16[73,16,128]{2,1,0:T(8,128)(2,1)S(1)} %get-tuple-element.29), channel_id=1, source_target_pairs={{0,15},{1,0},{2,1},{3,2},{4,3},{5,4},{6,5},{7,6},{8,7},{9,8},{10,9... | collective-permute-start | bytes 897032 | tf_op jit(solution)/shard_map/ppermute | solution.py:490
  8.1 7.3 %collective-permute-start.2 = (bf16[1,3,16,128]{3,2,1,0:T(8,128)(2,1)S(1)}, bf16[1,3,16,128]{3,2,1,0:T(8,128)(2,1)S(1)}, u32[]{:S(2)}, u32[]{:S(2)}) collective-permute-start(bf16[1,3,16,128]{3,2,1,0:T(8,128)(2,1)S(1)} %get-tuple-element.19.refs_0_), channel_id=1, source_target_pairs={{0,12},{1,13},{2,14},{3,15},{4,8},{5,9},{6,10},{7,11},{8,4},{9,5},... | collective-permute-start | bytes 36872 | tf_op jit(solution)/shard_map/ppermute | solution.py:442
  10.3 5.1 %collective-permute-start.1 = (bf16[1,3,16,128]{3,2,1,0:T(8,128)(2,1)S(1)}, bf16[1,3,16,128]{3,2,1,0:T(8,128)(2,1)S(1)}, u32[]{:S(2)}, u32[]{:S(2)}) collective-permute-start(bf16[1,3,16,128]{3,2,1,0:T(8,128)(2,1)S(1)} %get-tuple-element.19.refs_0_), channel_id=1, source_target_pairs={{0,8},{1,9},{2,10},{3,11},{4,12},{5,13},{6,14},{7,15},{8,0},{9,1},... | collective-permute-start | bytes 36872 | tf_op jit(solution)/shard_map/ppermute | solution.py:442
  10.3 5.2 %collective-permute-start = (bf16[1,3,16,128]{3,2,1,0:T(8,128)(2,1)S(1)}, bf16[1,3,16,128]{3,2,1,0:T(8,128)(2,1)S(1)}, u32[]{:S(2)}, u32[]{:S(2)}) collective-permute-start(bf16[1,3,16,128]{3,2,1,0:T(8,128)(2,1)S(1)} %get-tuple-element.19.refs_0_), channel_id=1, source_target_pairs={{0,4},{1,5},{2,6},{3,7},{4,0},{5,1},{6,2},{7,3},{8,12},{9,13},{10,... | collective-permute-start | bytes 36872 | tf_op jit(solution)/shard_map/ppermute | solution.py:442
  15.4 1.3 %collective-permute-start.3 = (bf16[4,3,16,128]{3,2,1,0:T(8,128)(2,1)S(1)}, bf16[4,3,16,128]{3,2,1,0:T(8,128)(2,1)S(1)}, u32[]{:S(2)}, u32[]{:S(2)}) collective-permute-start(bf16[4,3,16,128]{3,2,1,0:T(8,128)(2,1)S(1)} %get-tuple-element.24.refs_0_), channel_id=1, source_target_pairs={{0,1},{1,0},{2,3},{3,2},{4,5},{5,4},{6,7},{7,6},{8,9},{9,8},{10,11... | collective-permute-start | bytes 147464 | tf_op jit(solution)/shard_map/ppermute | solution.py:442
  16.8 4.9 %collective-permute-start.4 = (bf16[8,3,16,128]{3,2,1,0:T(8,128)(2,1)S(1)}, bf16[8,3,16,128]{3,2,1,0:T(8,128)(2,1)S(1)}, u32[]{:S(2)}, u32[]{:S(2)}) collective-permute-start(bf16[8,3,16,128]{3,2,1,0:T(8,128)(2,1)S(1)} %get-tuple-element.26.refs_0_), channel_id=1, source_target_pairs={{0,2},{1,3},{2,0},{3,1},{4,6},{5,7},{6,4},{7,5},{8,10},{9,11},{10,... | collective-permute-start | bytes 294920 | tf_op jit(solution)/shard_map/ppermute | solution.py:442

commit v4 on v3

--- a/solution.py
+++ b/solution.py
@@ -16,22 +16,40 @@
 EXT = 40
 UNROLL = 8
 
-WEST_WIDTH = [STEPS + 1 - step for step in range(1, STEPS + 1)]
-EAST_WIDTH = [STEPS - step for step in range(1, STEPS + 1)]
-WEST_FIELD = [0, 8, 16, 24, 32]
-WEST_COUNT = [8, 8, 8, 8, 8]
-WEST_MASS = 40
-WEST_ZETA = [48 + sum(WEST_WIDTH[:k]) for k in range(STEPS)]
-WEST_SIZE = 48 + sum(WEST_WIDTH)
-EAST_FIELD = [0, 8, 16, 23, 30]
-EAST_COUNT = [8, 8, 7, 7, 7]
-EAST_MASS = 37
-EAST_ZETA = [45 + sum(EAST_WIDTH[:k]) for k in range(STEPS)]
-EAST_SIZE = 45 + sum(EAST_WIDTH)
+WEST_COLS = [4, 5, 6, 7]
+EAST_COLS = [24, 25, 26, 27]
+
+
+def numbered(entries):
+    return {entry: at for at, entry in enumerate(entries)}
+
+
+WEST_PLACES = numbered(
+    [("state", field, col) for field in range(5) for col in WEST_COLS]
+    + [("state", field, 3) for field in range(2, 5)]
+    + [("mass", 0, col) for col in WEST_COLS]
+    + [
+        ("zeta", step, col)
+        for step in range(STEPS)
+        for col in range(6 - step if step < 4 else step, 8)
+    ]
+)
+EAST_PLACES = numbered(
+    [("state", field, col) for field in range(5) for col in EAST_COLS]
+    + [("mass", 0, col) for col in EAST_COLS]
+    + [
+        ("zeta", step, col)
+        for step in range(STEPS)
+        for col in range(24, 25 + step if step < 4 else 31 - step)
+    ]
+)
+WEST_SIZE = len(WEST_PLACES)
+EAST_SIZE = len(EAST_PLACES)
 STRIP = 24
 STRIP_FIELDS = 5
 STRIP_PARTS = 3
 EAST_END = EXT + 7
+EDGE_SPLIT = 4
 SHRINK = (5.0 / 6.0) ** STEPS
 
 
@@ -57,14 +75,6 @@
     return jnp.concatenate([load(even), load(odd)], axis=0)
 
 
-def west_slot(step):
-    return 48 + STEPS * step - (step * (step - 1)) // 2
-
-
-def east_slot(step):
-    return 45 + (STEPS - 1) * step - (step * (step - 1)) // 2
-
-
 def viscosity(rates, strength):
     square = rates[0] * rates[0] + 0.25 * (rates[1] * rates[1] + rates[2] * rates[2])
     return (0.1 * strength) * lax.rsqrt(jnp.maximum(square, 0.25))
@@ -72,7 +82,7 @@
 
 def pack_kernel(
     state_hbm, strains_hbm, strength_hbm, mass_hbm, mask_hbm, partner_hbm,
-    west_out, east_out, strip_out, own_out, state_out, zeta_out, mass_out,
+    strip_out, own_out, state_out, zeta_out, mass_out,
     state, strains, strength, mass, mask, partner, rows, top, sems,
 ):
     bf16 = jnp.bfloat16
@@ -103,25 +113,15 @@
     for at in range(8):
         tile = column_tile(lambda part: rows[0, part, :], at, 0)
         mass_out[HALO + at] = tile
-        east_out[EAST_MASS + at] = tile.astype(bf16)
         tile = column_tile(lambda part: rows[0, part, :], at, 1)
         mass_out[HALO + 8 + at] = tile
-        west_out[WEST_MASS + at] = tile.astype(bf16)
-    spared = mass_out[HALO + 7].astype(bf16)
-    east_first = mass_out[HALO].astype(bf16)
-
     state_copy.wait()
 
     @pl.loop(0, 8)
-    def _(turn):
-        at = 7 - turn
+    def _(at):
         for field in range(5):
-            tile = column_tile(lambda part: state[field, part, :], at, 0)
-            state_out[field, HALO + at] = tile
-            east_out[EAST_FIELD[field] + at] = tile.astype(bf16)
-            tile = column_tile(lambda part: state[field, part, :], at, 1)
-            state_out[field, HALO + 8 + at] = tile
-            west_out[WEST_FIELD[field] + at] = tile.astype(bf16)
+            state_out[field, HALO + at] = column_tile(lambda part: state[field, part, :], at, 0)
+            state_out[field, HALO + 8 + at] = column_tile(lambda part: state[field, part, :], at, 1)
 
     for field in range(5):
         top[field, :8] = state[field, 120:128, :]
@@ -138,12 +138,8 @@
             rows[128 + 8 * group : 136 + 8 * group] = zeta[8:]
         top[6 + step] = zeta
         for at in range(8):
-            tile = column_tile(lambda part: rows[part, :], at, 0)
-            zeta_out[step, HALO + at] = tile
-            east_out[east_slot(step) + (EAST_WIDTH[0] - 1 - step) - at] = tile.astype(bf16)
-            tile = column_tile(lambda part: rows[part, :], at, 1)
-            zeta_out[step, HALO + 8 + at] = tile
-            west_out[west_slot(step) + at - step] = tile.astype(bf16)
+            zeta_out[step, HALO + at] = column_tile(lambda part: rows[part, :], at, 0)
+            zeta_out[step, HALO + 8 + at] = column_tile(lambda part: rows[part, :], at, 1)
 
     @pl.loop(0, STEPS // 2)
     def _(turn):
@@ -153,9 +149,6 @@
         for part in range(2):
             cycle = 2 * turn + part
             cycle_zeta(cycle, STEPS - 1 - cycle, rows.at[part])
-
-    east_out[EAST_MASS] = east_first
-    east_out[EAST_MASS + 7] = spared
 
     lane = lax.broadcasted_iota(jnp.int32, (COLS, LANES), 1)
     row_at = lax.broadcasted_iota(jnp.int32, (COLS, LANES), 0)
@@ -182,7 +175,13 @@
 
 
 def fold_kernel(offsets, *refs):
-    *parts, own, last_tiles, _, out, strips, tiles, sems = refs
+    *parts, own, result, out, strips, tiles, sems = refs
+    copies = [
+        pltpu.make_async_copy(result.at[:, pl.ds(at, 120), :], out.at[:, pl.ds(at, 120), :], sems.at[at // 128])
+        for at in (0, 128)
+    ]
+    for copy in copies:
+        copy.start()
     me = lax.axis_index("lon")
     blocks = strips.shape[0]
     total = blocks * COLS
@@ -265,13 +264,17 @@
     reached = lane[:COLS] >= LANES - STEPS - 1
     for field in range(5):
         moved = pltpu.roll(top, (LANES - STRIP - STRIP * field) % LANES, 1)
-        tiles[field] = jnp.where(reached, moved, last_tiles[field])
-    copies = [
-        pltpu.make_async_copy(tiles.at[:, 8 * half : 8 * half + 8, :], out.at[:, pl.ds(128 * half + 120, 8), :], sems.at[half])
+        before = jnp.concatenate([result[field, 120:128, :], result[field, 248:256, :]], axis=0)
+        tiles[field] = jnp.where(reached, moved, before)
+    last_copies = [
+        pltpu.make_async_copy(
+            tiles.at[:, 8 * half : 8 * half + 8, :], out.at[:, pl.ds(128 * half + 120, 8), :], sems.at[2 + half]
+        )
         for half in range(2)
     ]
-    for copy in copies:
+    for copy in last_copies:
         copy.start()
+    copies.extend(last_copies)
     for copy in copies:
         copy.wait()
 
@@ -317,7 +320,7 @@
     def velocities(keep_u, keep_v, west_x, west_c, x, c, y):
         return keep_u + (west_x - x) + (c - row_above(c)), keep_v + (west_c - c) + (y - row_above(y))
 
-    def advance(step, place, next_place, col, carry):
+    def advance(step, place, next_place, col, carry, moves=None):
         p, q, keep_u, keep_v, west_x, west_c = carry
         next_p, next_q, next_u, next_v = forces(next_place, col + 1)
         along = 0.5 * (p - next_p)
@@ -326,6 +329,10 @@
         new_one = one[place] + (along + across)
         new_two = two[place] + (along - across)
         new_shear = shear[place] + turn + (q - next_q)
+        if moves is not None:
+            new_one = jnp.where(moves, new_one, one[place])
+            new_two = jnp.where(moves, new_two, two[place])
+            new_shear = jnp.where(moves, new_shear, shear[place])
         x, c, y = strains_of(step, col, new_one, new_two, new_shear)
         new_u, new_v = velocities(keep_u, keep_v, west_x, west_c, x, c, y)
         return (new_u, new_v, new_one, new_two, new_shear), (next_p, next_q, next_u, next_v, x, c)
@@ -333,25 +340,33 @@
     return forces, stored_strains, velocities, advance
 
 
-def inner_kernel(state_in, zeta, weight, sides, state):
+def inner_steps(state, zeta, weight, steps, width):
     forces, _, _, advance = stepper(state, zeta, weight)
     blank = jnp.zeros((TILE, LANES), jnp.float32)
 
-    @pl.loop(0, STEPS)
+    @pl.loop(*steps)
     def _(step):
         begin = HALO + step
         last = HALO + COLS - 2 - step
-
-        def body(group, carry):
-            for part in range(UNROLL):
-                col = begin + group * UNROLL + part
-                new, carry = advance(step, col, col + 1, col, carry)
-                for field in range(5):
-                    valid = (col <= last) & (col > begin) if field < 2 else col <= last
-                    state[field, col] = jnp.where(valid, new[field], state[field, col])
-            return carry
-
-        lax.fori_loop(0, (last - begin + UNROLL) // UNROLL, body, forces(begin, begin) + (blank, blank))
+        carry = forces(begin, begin) + (blank, blank)
+        for part in range(width):
+            col = begin + part
+            new, carry = advance(step, col, col + 1, col, carry)
+            for field in range(5):
+                valid = (col <= last) & (part > 0) if field < 2 else col <= last
+                state[field, col] = jnp.where(valid, new[field], state[field, col])
+
+
+def first_inner_kernel(state_in, zeta, weight, state, west, east):
+    inner_steps(state, zeta, weight, (0, EDGE_SPLIT), COLS - 1)
+    for out, places, shift in ((west, WEST_PLACES, COLS), (east, EAST_PLACES, -COLS)):
+        for (kind, which, col), place in places.items():
+            source = {"state": state, "zeta": zeta}[kind].at[which] if kind != "mass" else weight
+            out[place] = source[col + shift].astype(jnp.bfloat16)
+
+
+def second_inner_kernel(state_in, zeta, weight, sides, state):
+    inner_steps(state, zeta, weight, (EDGE_SPLIT, STEPS), COLS - 1 - 2 * EDGE_SPLIT)
 
     @pl.loop(0, 9)
     def _(at):
@@ -360,29 +375,44 @@
             sides[field, EAST_END - HALO - 7 - at] = state[field, HALO + 7 + at]
 
 
-def edge_kernel(west, east, state_in, zeta_in, mass_in, out, last, state, zeta, weight):
-    @pl.loop(0, 8)
-    def _(at):
-        for field in range(5):
-            state[field, at] = west[WEST_FIELD[field] + at].astype(jnp.float32)
-            state[field, EAST_END - HALO - COLS - at] = east[EAST_FIELD[field] + at].astype(jnp.float32)
-        weight[at] = west[WEST_MASS + at].astype(jnp.float32)
-        weight[HALO + COLS + at] = east[EAST_MASS + at].astype(jnp.float32)
-
-    @pl.loop(0, STEPS)
-    def _(step):
-        for at in range(8):
-            zeta[step, at] = west[west_slot(step) + at - step].astype(jnp.float32)
-            zeta[step, HALO + COLS + at] = east[
-                east_slot(step) + (EAST_WIDTH[0] - 1 - step) - at
-            ].astype(jnp.float32)
+def edge_kernel(west, east, state_in, zeta_in, mass_in, out, state, zeta, weight):
+    for source, places in ((west, WEST_PLACES), (east, EAST_PLACES)):
+        for (kind, which, col), place in places.items():
+            tile = source[place].astype(jnp.float32)
+            if kind == "state":
+                state[which, EAST_END - col if col >= HALO + COLS else col] = tile
+            elif kind == "mass":
+                weight[col] = tile
+            else:
+                zeta[which, col] = tile
 
     forces, stored_strains, velocities, advance = stepper(state, zeta, weight)
     blank = jnp.zeros((TILE, LANES), jnp.float32)
 
+    def growing(steps, reach):
+        @pl.loop(*steps)
+        def _(step):
+            for middle in (HALO - 1, HALO + COLS - 1):
+                cols = range(middle - reach, middle + reach + 2)
+                at = [col if middle < HALO else EAST_END - col for col in range(cols[0], cols[-1] + 2)]
+                carry = forces(at[0], cols[0]) + (blank, blank)
+                for part, col in enumerate(cols):
+                    old = [state[field, at[part]] for field in range(5)]
+                    left = abs(col - middle) <= step
+                    new, carry = advance(step, at[part], at[part + 1], col, carry, left)
+                    moves = left | (step + middle + 1 == col)
+                    for field in range(5):
+                        if field >= 2:
+                            state[field, at[part]] = new[field]
+                        elif part:
+                            state[field, at[part]] = jnp.where(moves, new[field], old[field])
+
+    growing((0, 2), 2)
+    growing((2, EDGE_SPLIT), 4)
+
     start = EAST_END - (HALO + COLS - 1)
 
-    @pl.loop(0, STEPS)
+    @pl.loop(EDGE_SPLIT, STEPS)
     def _(step):
         begin = HALO + COLS - 1 - step
         x, c, _ = stored_strains(step, step + (start + 1), begin - 1)
@@ -406,10 +436,6 @@
                 even, odd = column_slices(at, half)
                 out[field, even, :] = tile[:8]
                 out[field, odd, :] = tile[8:]
-
-    for field in range(5):
-        last[field, :8] = out[field, 120:128, :]
-        last[field, 8:] = out[field, 248:256, :]
 
 
 def join(parts, passed):
@@ -430,12 +456,12 @@
 
 
 def gather_stages(count):
-    stages = []
+    stages = [(1,)]
     bit = 4
     while bit < count:
-        stages.append((bit, 2 * bit, 3 * bit) if 2 * bit < count else (bit,))
+        stages.append((3 * bit, 2 * bit, bit) if 2 * bit < count else (bit,))
         bit *= 4
-    return stages + [(1,), (2,)]
+    return stages + [(2,)]
 
 
 def exchange(held, steps, count):
@@ -463,16 +489,15 @@
         jax.ShapeDtypeStruct((WEST_SIZE, TILE, LANES), bf16),
         jax.ShapeDtypeStruct((EAST_SIZE, TILE, LANES), bf16),
     )
-    west_send, east_send, strip, own_strip, state, zeta, weight = pl.pallas_call(
+    strip, own_strip, state, zeta, weight = pl.pallas_call(
         pack_kernel,
         out_shape=(
-            *sends,
             jax.ShapeDtypeStruct((1, STRIP_PARTS, COLS, LANES), bf16),
             jax.ShapeDtypeStruct((1, STRIP_PARTS, COLS, LANES), f32),
             *extended,
         ),
         in_specs=[hbm] * 6,
-        out_specs=(whole,) * 7,
+        out_specs=(whole,) * 5,
         scratch_shapes=[
             pltpu.VMEM(state_shape, f32),
             pltpu.VMEM(strains.shape, bf16),
@@ -486,49 +511,55 @@
         ],
         compiler_params=params,
     )(*cells)
+    stages = gather_stages(count)
+    offsets = [0]
+    for steps in stages:
+        offsets = [offset ^ step for step in (0, *steps) for offset in offsets]
+    parts = exchange(strip, stages[0], count)
+    state, west_send, east_send = pl.pallas_call(
+        first_inner_kernel,
+        out_shape=(extended[0], *sends),
+        in_specs=[whole] * 3,
+        out_specs=(whole,) * 3,
+        input_output_aliases={0: 0},
+        compiler_params=params,
+    )(state, zeta, weight)
+    held, (west_send, east_send) = join(parts, (west_send, east_send))
     west = lax.ppermute(west_send, "lon", [(i, (i + 1) % count) for i in range(count)])
     east = lax.ppermute(east_send, "lon", [(i, (i - 1) % count) for i in range(count)])
     state, _ = pl.pallas_call(
-        inner_kernel,
+        second_inner_kernel,
         out_shape=(extended[0], extended[0]),
         in_specs=[whole] * 3,
         out_specs=(whole,) * 2,
         input_output_aliases={0: 1},
         compiler_params=params,
+        cost_estimate=pl.CostEstimate(flops=1000000000, bytes_accessed=1000000000, transcendentals=0),
     )(state, zeta, weight)
-    offsets = [0]
-    parts = [strip]
-    for steps in gather_stages(count):
-        held = parts[0]
-        if len(parts) > 1:
+    for steps in stages[1:]:
+        parts = exchange(held, steps, count)
+        if steps != stages[-1]:
             held, (state,) = join(parts, (state,))
-        parts = exchange(held, steps, count)
-        offsets = [offset ^ step for step in (0, *steps) for offset in offsets]
-    out, last, *_ = pl.pallas_call(
+    out, *_ = pl.pallas_call(
         edge_kernel,
-        out_shape=(
-            jax.ShapeDtypeStruct(state_shape, f32),
-            jax.ShapeDtypeStruct((5, COLS, LANES), f32),
-            *extended,
-        ),
+        out_shape=(jax.ShapeDtypeStruct(state_shape, f32), *extended),
         in_specs=[whole] * 5,
-        out_specs=(whole,) * 5,
-        input_output_aliases={2: 2, 3: 3, 4: 4},
+        out_specs=(whole,) * 4,
+        input_output_aliases={2: 1, 3: 2, 4: 3},
         compiler_params=params,
     )(west, east, state, zeta, weight)
     out = pl.pallas_call(
         functools.partial(fold_kernel, offsets),
         out_shape=jax.ShapeDtypeStruct(state_shape, f32),
-        in_specs=[whole] * (len(parts) + 2) + [hbm],
+        in_specs=[whole] * (len(parts) + 2),
         out_specs=hbm,
-        input_output_aliases={len(parts) + 2: 0},
         scratch_shapes=[
             pltpu.VMEM((count, STRIP_PARTS, COLS, LANES), f32),
             pltpu.VMEM((5, COLS, LANES), f32),
-            pltpu.SemaphoreType.DMA((2,)),
+            pltpu.SemaphoreType.DMA((4,)),
         ],
         compiler_params=params,
-    )(*parts, own_strip, last, pltpu.with_memory_space_constraint(out, pltpu.HBM))
+    )(*parts, own_strip, out)
     return from_rows(out)
 
 

time: 24.1 us -> 21.7 us (0.900)
  Pallas kernels: 12 us -> 9.72 us
  waiting for transfers between devices: 1.81 us -> 0.26 us
  starting transfers between devices: 10.1 us -> 11.5 us
    ppermute x5, starting transfers between devices: 4.54 us -> 7.76 us  [exchange(): lax.ppermute(held, 'lon', [(i, i ^ step) for i in range(count)])]
    ppermute x5, waiting for transfers between devices: 1.8 us -> 0.01 us  [exchange(): lax.ppermute(held, 'lon', [(i, i ^ step) for i in range(count)])]
    ppermute x1, starting transfers between devices: 5.03 us -> 3.59 us  [on_device(): lax.ppermute(east_send, 'lon', [(i, (i - 1) % count) for i in range(count)])]
    pallas_call x1, Pallas kernels: 4.2 us -> 2.94 us  [on_device(): pl.pallas_call(edge_kernel, out_shape=(jax.ShapeDtypeStruct(state_shape,...]
    pallas_call x2 -> x3, Pallas kernels: 5.46 us -> 4.43 us  [the longest x1 2.34 us: on_device(): pl.pallas_call(pack_kernel, out_shape=(jax.ShapeDtypeStruct((1, STRIP_PAR...]
    ppermute x1, starting transfers between devices: 0.5 us -> 0.11 us  [on_device(): lax.ppermute(west_send, 'lon', [(i, (i + 1) % count) for i in range(count)])]
  transfers between devices with their start and end apart: 7 -> 7, of which waited for: 2 -> 1; matrix products, arithmetic and copies ran while one was open for 0% -> 0% of each run, Pallas kernels for 30% -> 23%
where the time goes in v4:
time: 21.7 us; the launch traced here: 21.5 us
  starting transfers between devices  11.5 us (53%)
  Pallas kernels  9.72 us (45%)
  waiting for transfers between devices  0.26 us (1%)
    ppermute x5, starting transfers between devices, exchange(): lax.ppermute(held, 'lon', [(i, i ^ step) for i in range(count)])  7.76 us
    ppermute x1, starting transfers between devices, on_device(): lax.ppermute(east_send, 'lon', [(i, (i - 1) % count) for i in range(count)])  3.59 us
    pallas_call x1, Pallas kernels, on_device(): pl.pallas_call(edge_kernel, out_shape=(jax.ShapeDtypeStruct(state_shape,...  2.94 us
    pallas_call x1, Pallas kernels, on_device(): pl.pallas_call(pack_kernel, out_shape=(jax.ShapeDtypeStruct((1, STRIP_PAR...  2.34 us
    pallas_call x1, Pallas kernels, on_device(): pl.pallas_call(functools.partial(fold_kernel, offsets), out_shape=jax.Sha...  2.33 us
    pallas_call x1, Pallas kernels, on_device(): pl.pallas_call(first_inner_kernel, out_shape=(extended[0], *sends), in_sp...  1.18 us
    pallas_call x1, Pallas kernels, on_device(): pl.pallas_call(second_inner_kernel, out_shape=(extended[0], extended[0]),...  0.91 us
  transfers between devices with their start and end apart: 7, of which 1 were waited for; matrix products, arithmetic and copies ran while one was open for 0% of the time, Pallas kernels for 23%

profile of v4, /device:TPU:0, one launch (start us, length us, event | category | flops | bytes accessed | tf_op | source)
XLA Modules:
  0.0 21.5 jit_solution(18332673515800635819)
XLA Ops:
  0.0 2.3 %shard_map.64 = (bf16[1,3,16,128]{3,2,1,0:T(8,128)(2,1)S(1)}, f32[1,3,16,128]{3,2,1,0:T(8,128)S(1)}, f32[5,40,16,128]{3,2,1,0:T(8,128)S(1)}, f32[8,40,16,128]{3,2,1,0:T(8,128)S(1)}, f32[40,16,128]{2,1,0:T(8,128)S(1)}) custom-call(f32[5,256,128]{2,1,0:T(8,128)} %bitcast.10, bf16[8,3,16,2048]{3,2,1,0:T(8,128)(2,1)} %strains_hbm.1, f32[16,2048]{1,0:T(8,128)} %strength_hbm.1, ...), custom_call_target="tpu_custom_call" | custom-call | tf_op jit(solution)/shard_map/pallas_call | solution.py:492
  2.4 0.5 %collective-permute-start = (bf16[1,3,16,128]{3,2,1,0:T(8,128)(2,1)S(1)}, bf16[1,3,16,128]{3,2,1,0:T(8,128)(2,1)S(1)}, u32[]{:S(2)}, u32[]{:S(2)}) collective-permute-start(bf16[1,3,16,128]{3,2,1,0:T(8,128)(2,1)S(1)} %get-tuple-element.20.refs_0_), channel_id=1, source_target_pairs={{0,1},{1,0},{2,3},{3,2},{4,5},{5,4},{6,7},{7,6},{8,9},{9,8},{10,11... | collective-permute-start | bytes 36872 | tf_op jit(solution)/shard_map/ppermute | solution.py:468
  2.9 1.2 %shard_map.65 = (f32[5,40,16,128]{3,2,1,0:T(8,128)S(1)}, bf16[51,16,128]{2,1,0:T(8,128)(2,1)S(1)}, bf16[40,16,128]{2,1,0:T(8,128)(2,1)S(1)}) custom-call(f32[5,40,16,128]{3,2,1,0:T(8,128)S(1)} %get-tuple-element.21.state_in, f32[8,40,16,128]{3,2,1,0:T(8,128)S(1)} %get-tuple-element.22.zeta.zeta_in, ...), custom_call_target="tpu_custom_call", output_to_operand_aliasing={{0}: (0, {})} | custom-call | tf_op jit(solution)/shard_map/pallas_call | solution.py:519
  4.1 0.0 collective-permute-done.refs_1_
  4.1 0.1 collective-permute-start.5
  4.2 5.0 %collective-permute-start.1 = (bf16[2,3,16,128]{3,2,1,0:T(8,128)(2,1)S(1)}, bf16[2,3,16,128]{3,2,1,0:T(8,128)(2,1)S(1)}, u32[]{:S(2)}, u32[]{:S(2)}) collective-permute-start(bf16[2,3,16,128]{3,2,1,0:T(8,128)(2,1)S(1)} %get-tuple-element.26.refs_0_), channel_id=1, source_target_pairs={{0,12},{1,13},{2,14},{3,15},{4,8},{5,9},{6,10},{7,11},{8,4},{9,5},... | collective-permute-start | bytes 73736 | tf_op jit(solution)/shard_map/ppermute | solution.py:468
  9.2 0.0 collective-permute-start.2
  9.2 0.6 %collective-permute-start.3 = (bf16[2,3,16,128]{3,2,1,0:T(8,128)(2,1)S(1)}, bf16[2,3,16,128]{3,2,1,0:T(8,128)(2,1)S(1)}, u32[]{:S(2)}, u32[]{:S(2)}) collective-permute-start(bf16[2,3,16,128]{3,2,1,0:T(8,128)(2,1)S(1)} %get-tuple-element.26.refs_0_), channel_id=1, source_target_pairs={{0,4},{1,5},{2,6},{3,7},{4,0},{5,1},{6,2},{7,3},{8,12},{9,13},{10,... | collective-permute-start | bytes 73736 | tf_op jit(solution)/shard_map/ppermute | solution.py:468
  9.8 3.6 %collective-permute-start.6 = (bf16[40,16,128]{2,1,0:T(8,128)(2,1)S(1)}, bf16[40,16,128]{2,1,0:T(8,128)(2,1)S(1)}, u32[]{:S(2)}, u32[]{:S(2)}) collective-permute-start(bf16[40,16,128]{2,1,0:T(8,128)(2,1)S(1)} %get-tuple-element.32), channel_id=1, source_target_pairs={{0,15},{1,0},{2,1},{3,2},{4,3},{5,4},{6,5},{7,6},{8,7},{9,8},{10,9... | collective-permute-start | bytes 491528 | tf_op jit(solution)/shard_map/ppermute | solution.py:529
  13.4 0.9 %shard_map.67 = (f32[5,40,16,128]{3,2,1,0:T(8,128)S(1)}, f32[5,40,16,128]{3,2,1,0:T(8,128)S(1)}) custom-call(f32[5,40,16,128]{3,2,1,0:T(8,128)S(1)} %get-tuple-element.27.state_in, f32[8,40,16,128]{3,2,1,0:T(8,128)S(1)} %get-tuple-element.22.zeta.zeta_in, f32[40,16,128]{2,1,0:T(8,128)S(1)} %get-tuple-element.23.weight.mass_in), custom_call_target="tpu_custom_call", output_to_operand_aliasing={{1}: (0, {})} | custom-call | flops 1000000000 | bytes 1000000000 | tf_op jit(solution)/shard_map/pallas_call | solution.py:530
  14.3 0.0 collective-permute-done.1.refs_1_
  14.3 0.0 collective-permute-done.2.refs_2_
  14.3 0.0 collective-permute-done.3.refs_3_
  14.4 1.6 %collective-permute-start.4 = (bf16[8,3,16,128]{3,2,1,0:T(8,128)(2,1)S(1)}, bf16[8,3,16,128]{3,2,1,0:T(8,128)(2,1)S(1)}, u32[]{:S(2)}, u32[]{:S(2)}) collective-permute-start(bf16[8,3,16,128]{3,2,1,0:T(8,128)(2,1)S(1)} %get-tuple-element.29.refs_0_), channel_id=1, source_target_pairs={{0,2},{1,3},{2,0},{3,1},{4,6},{5,7},{6,4},{7,5},{8,10},{9,11},{10,... | collective-permute-start | bytes 294920 | tf_op jit(solution)/shard_map/ppermute | solution.py:468
  16.0 0.2 %collective-permute-done.6.east = bf16[40,16,128]{2,1,0:T(8,128)(2,1)S(1)} collective-permute-done((bf16[40,16,128]{2,1,0:T(8,128)(2,1)S(1)}, bf16[40,16,128]{2,1,0:T(8,128)(2,1)S(1)}, u32[]{:S(2)}, u32[]{:S(2)}) %collective-permute-start.6) | collective-permute-done | bytes 163872 | tf_op jit(solution)/shard_map/ppermute | solution.py:529
  16.2 0.0 collective-permute-done.5.west
  16.2 2.9 %shard_map.69 = (f32[5,256,128]{2,1,0:T(8,128)S(1)}, f32[5,40,16,128]{3,2,1,0:T(8,128)S(1)}, f32[8,40,16,128]{3,2,1,0:T(8,128)S(1)}, f32[40,16,128]{2,1,0:T(8,128)S(1)}) custom-call(bf16[51,16,128]{2,1,0:T(8,128)(2,1)S(1)} %collective-permute-done.5.west, ...), custom_call_target="tpu_custom_call", output_to_operand_aliasing={{1}: (2, {}), {2}: (3, {}), {3}: (4, {})} | custom-call | tf_op jit(solution)/shard_map/pallas_call | solution.py:543
  19.2 0.0 collective-permute-done.4.refs_1_
  19.2 2.3 %shard_map.70 = f32[5,256,128]{2,1,0:T(8,128)} custom-call(bf16[8,3,16,128]{3,2,1,0:T(8,128)(2,1)S(1)} %get-tuple-element.29.refs_0_, bf16[8,3,16,128]{3,2,1,0:T(8,128)(2,1)S(1)} %collective-permute-done.4.refs_1_, f32[1,3,16,128]{3,2,1,0:T(8,128)S(1)} %get-tuple-element.30.refs_2_, f32[5,256,128]{2,1,0:T(8,128)S(1)} %get-tuple-element.34.refs_3_), custom_call_target="tpu_custom_call" | custom-call | tf_op jit(solution)/shard_map/pallas_call | solution.py:551
  (2 shorter events, 0.0 us)
Async XLA Ops:
  2.4 1.7 %collective-permute-start = (bf16[1,3,16,128]{3,2,1,0:T(8,128)(2,1)S(1)}, bf16[1,3,16,128]{3,2,1,0:T(8,128)(2,1)S(1)}, u32[]{:S(2)}, u32[]{:S(2)}) collective-permute-start(bf16[1,3,16,128]{3,2,1,0:T(8,128)(2,1)S(1)} %get-tuple-element.20.refs_0_), channel_id=1, source_target_pairs={{0,1},{1,0},{2,3},{3,2},{4,5},{5,4},{6,7},{7,6},{8,9},{9,8},{10,11... | collective-permute-start | bytes 36872 | tf_op jit(solution)/shard_map/ppermute | solution.py:468
  4.1 12.2 %collective-permute-start.5 = (bf16[51,16,128]{2,1,0:T(8,128)(2,1)S(1)}, bf16[51,16,128]{2,1,0:T(8,128)(2,1)S(1)}, u32[]{:S(2)}, u32[]{:S(2)}) collective-permute-start(bf16[51,16,128]{2,1,0:T(8,128)(2,1)S(1)} %get-tuple-element.31), channel_id=1, source_target_pairs={{0,1},{1,2},{2,3},{3,4},{4,5},{5,6},{6,7},{7,8},{8,9},{9,10},{10,1... | collective-permute-start | bytes 626696 | tf_op jit(solution)/shard_map/ppermute | solution.py:528
  4.2 10.1 %collective-permute-start.1 = (bf16[2,3,16,128]{3,2,1,0:T(8,128)(2,1)S(1)}, bf16[2,3,16,128]{3,2,1,0:T(8,128)(2,1)S(1)}, u32[]{:S(2)}, u32[]{:S(2)}) collective-permute-start(bf16[2,3,16,128]{3,2,1,0:T(8,128)(2,1)S(1)} %get-tuple-element.26.refs_0_), channel_id=1, source_target_pairs={{0,12},{1,13},{2,14},{3,15},{4,8},{5,9},{6,10},{7,11},{8,4},{9,5},... | collective-permute-start | bytes 73736 | tf_op jit(solution)/shard_map/ppermute | solution.py:468
  9.2 5.1 %collective-permute-start.2 = (bf16[2,3,16,128]{3,2,1,0:T(8,128)(2,1)S(1)}, bf16[2,3,16,128]{3,2,1,0:T(8,128)(2,1)S(1)}, u32[]{:S(2)}, u32[]{:S(2)}) collective-permute-start(bf16[2,3,16,128]{3,2,1,0:T(8,128)(2,1)S(1)} %get-tuple-element.26.refs_0_), channel_id=1, source_target_pairs={{0,8},{1,9},{2,10},{3,11},{4,12},{5,13},{6,14},{7,15},{8,0},{9,1},... | collective-permute-start | bytes 73736 | tf_op jit(solution)/shard_map/ppermute | solution.py:468
  9.2 5.1 %collective-permute-start.3 = (bf16[2,3,16,128]{3,2,1,0:T(8,128)(2,1)S(1)}, bf16[2,3,16,128]{3,2,1,0:T(8,128)(2,1)S(1)}, u32[]{:S(2)}, u32[]{:S(2)}) collective-permute-start(bf16[2,3,16,128]{3,2,1,0:T(8,128)(2,1)S(1)} %get-tuple-element.26.refs_0_), channel_id=1, source_target_pairs={{0,4},{1,5},{2,6},{3,7},{4,0},{5,1},{6,2},{7,3},{8,12},{9,13},{10,... | collective-permute-start | bytes 73736 | tf_op jit(solution)/shard_map/ppermute | solution.py:468
  9.8 6.4 %collective-permute-start.6 = (bf16[40,16,128]{2,1,0:T(8,128)(2,1)S(1)}, bf16[40,16,128]{2,1,0:T(8,128)(2,1)S(1)}, u32[]{:S(2)}, u32[]{:S(2)}) collective-permute-start(bf16[40,16,128]{2,1,0:T(8,128)(2,1)S(1)} %get-tuple-element.32), channel_id=1, source_target_pairs={{0,15},{1,0},{2,1},{3,2},{4,3},{5,4},{6,5},{7,6},{8,7},{9,8},{10,9... | collective-permute-start | bytes 491528 | tf_op jit(solution)/shard_map/ppermute | solution.py:529
  14.4 4.8 %collective-permute-start.4 = (bf16[8,3,16,128]{3,2,1,0:T(8,128)(2,1)S(1)}, bf16[8,3,16,128]{3,2,1,0:T(8,128)(2,1)S(1)}, u32[]{:S(2)}, u32[]{:S(2)}) collective-permute-start(bf16[8,3,16,128]{3,2,1,0:T(8,128)(2,1)S(1)} %get-tuple-element.29.refs_0_), channel_id=1, source_target_pairs={{0,2},{1,3},{2,0},{3,1},{4,6},{5,7},{6,4},{7,5},{8,10},{9,11},{10,... | collective-permute-start | bytes 294920 | tf_op jit(solution)/shard_map/ppermute | solution.py:468

commit v5 on v4

--- a/solution.py
+++ b/solution.py
@@ -43,11 +43,14 @@
         for col in range(24, 25 + step if step < 4 else 31 - step)
     ]
 )
-WEST_SIZE = len(WEST_PLACES)
-EAST_SIZE = len(EAST_PLACES)
-STRIP = 24
-STRIP_FIELDS = 5
-STRIP_PARTS = 3
+WEST_RESTS = [("state", field, 7) for field in range(2, 5)] + [("zeta", step, 7) for step in range(2)]
+EAST_RESTS = [("state", 0, 24), ("state", 1, 24), ("mass", 0, 24)]
+WEST_SIZE = len(WEST_PLACES) + len(WEST_RESTS)
+EAST_SIZE = len(EAST_PLACES) + len(EAST_RESTS)
+STRIP = 16
+STRIP_PARTS = 2
+STRIP_BEFORE = 6 * STRIP
+STRIP_PLACE = STRIP_BEFORE + 8
 EAST_END = EXT + 7
 EDGE_SPLIT = 4
 SHRINK = (5.0 / 6.0) ** STEPS
@@ -155,11 +158,14 @@
     place = jnp.zeros((COLS, LANES), jnp.int32)
     for col in range(COLS):
         place = jnp.where(row_at == col, lax.rem(partner[col], COLS), place)
-    strips = [place.astype(jnp.float32)] + [jnp.zeros((COLS, LANES), jnp.float32)] * (STRIP_PARTS - 1)
+    strips = [jnp.where(lane == STRIP_PLACE, place.astype(jnp.float32), 0.0)] + [jnp.zeros((COLS, LANES), jnp.float32)] * (STRIP_PARTS - 1)
     for at in range(6 + STEPS):
-        part, begin = at // STRIP_FIELDS, STRIP * (at % STRIP_FIELDS)
+        part, begin = (0, STRIP * at) if at < 6 else (1, STRIP * (at - 6))
         moved = pltpu.roll(top[at], (begin + STRIP) % LANES, 1)
         strips[part] = jnp.where((lane >= begin) & (lane < begin + STRIP), moved, strips[part])
+    for k, at in enumerate((0, 1, 5)):
+        moved = pltpu.roll(top[at], (STRIP_BEFORE + k + STRIP + 1) % LANES, 1)
+        strips[0] = jnp.where(lane == STRIP_BEFORE + k, moved, strips[0])
     for part in range(STRIP_PARTS):
         own_out[0, part] = strips[part]
         strip_out[0, part] = strips[part].astype(bf16)
@@ -175,7 +181,7 @@
 
 
 def fold_kernel(offsets, *refs):
-    *parts, own, result, out, strips, tiles, sems = refs
+    *parts, own, result, out, strips, turned, tiles, sems = refs
     copies = [
         pltpu.make_async_copy(result.at[:, pl.ds(at, 120), :], out.at[:, pl.ds(at, 120), :], sems.at[at // 128])
         for at in (0, 128)
@@ -191,37 +197,37 @@
         for k in range(part.shape[0]):
             strips[next(order)] = part[k].astype(jnp.float32)
     strips[0] = own[0]
-    lane = lax.broadcasted_iota(jnp.int32, (STRIP, LANES), 1)
-    sub = lax.broadcasted_iota(jnp.int32, (STRIP, total), 0)
-    last = sub == STRIP - 1
-    turned = [
-        [
-            jnp.concatenate([strips[lax.bitwise_xor(me, 8 * r + k), part] for k in range(8)], axis=0).T
-            for r in range(count)
-        ]
-        for part in range(STRIP_PARTS)
-    ]
+    for part in range(STRIP_PARTS):
+        for r in range(count):
+            group = [strips[lax.bitwise_xor(me, 8 * r + k), part] for k in range(8)]
+            turned[part, :, LANES * r : LANES * r + LANES] = jnp.concatenate(group, axis=0).T
 
     def field(at):
-        part, begin = at // STRIP_FIELDS, STRIP * (at % STRIP_FIELDS)
-        return jnp.concatenate([tile[begin : begin + STRIP] for tile in turned[part]], axis=1)
-
-    begin = STRIP * STRIP_FIELDS
+        part, begin = (0, STRIP * at) if at < 6 else (1, STRIP * (at - 6))
+        return turned[part, begin : begin + STRIP, :]
+
+    lane = lax.broadcasted_iota(jnp.int32, (8, LANES), 1)
+    row = lax.broadcasted_iota(jnp.int32, (STRIP, total), 0)
+    last = row == STRIP - 1
+    far_row = lax.broadcasted_iota(jnp.int32, (8, total), 0) == 7
     places = [
-        (7 - lane[:8] // COLS) * COLS + jnp.broadcast_to(tile[begin : begin + 1], (8, LANES)).astype(jnp.int32)
-        for tile in turned[0]
+        (7 - lane // COLS) * COLS
+        + jnp.broadcast_to(
+            turned[0, STRIP_PLACE : STRIP_PLACE + 1, LANES * r : LANES * r + LANES], (8, LANES)
+        ).astype(jnp.int32)
+        for r in range(count)
     ]
 
     def at_fold(value):
         rows = [
             jnp.take_along_axis(
-                value[STRIP - 8 :, LANES * (count - 1 - r) : LANES * (count - r)], places[r], axis=1,
+                value[8:, LANES * (count - 1 - r) : LANES * (count - r)], places[r], axis=1,
                 mode="promise_in_bounds",
             )
             for r in range(count)
         ]
-        far = jnp.where(last[:8] | last[STRIP - 8 :], jnp.concatenate(rows, axis=1), 0.0)
-        return jnp.concatenate([jnp.zeros((STRIP - 8, total), jnp.float32), far], axis=0)
+        far = jnp.where(far_row, jnp.concatenate(rows, axis=1), 0.0)
+        return jnp.concatenate([jnp.zeros((8, total), jnp.float32), far], axis=0)
 
     def next_col(value):
         return pltpu.roll(value, total - 1, 1)
@@ -236,15 +242,21 @@
         return pltpu.roll(value, 1, 0)
 
     vel_u, vel_v, one, two, shear, weight = (field(at) for at in range(6))
+    before = turned[0, STRIP_BEFORE : STRIP_BEFORE + 8, :]
     wet = weight != 0.0
     for step in range(STEPS):
         p = weight * vel_u
         q = weight * vel_v
+        low_p = row_below(p)
+        low_q = row_below(q)
+        if step == 0:
+            low_p = jnp.where(row == 0, before[2:3] * before[0:1], low_p)
+            low_q = jnp.where(row == 0, before[2:3] * before[1:2], low_q)
         along = 0.5 * (p - next_col(p))
-        across = 0.5 * (row_below(q) - q + at_fold(q))
+        across = 0.5 * (low_q - q + at_fold(q))
         one = one + (along + across)
         two = two + (along - across)
-        shear = shear + (row_below(p) - p - at_fold(p)) + (q - next_col(q))
+        shear = shear + (low_p - p - at_fold(p)) + (q - next_col(q))
         zeta = field(6 + step)
         first = zeta * one
         quarter = 0.25 * zeta
@@ -259,11 +271,11 @@
 
     shift = lax.rem(total - COLS * me, total)
     rows = [pltpu.roll(value, shift, 1)[:, :LANES] for value in (vel_u, vel_v, one, two, shear)]
-    rows.append(jnp.zeros((LANES - STRIP * STRIP_FIELDS, LANES), jnp.float32))
+    rows.append(jnp.zeros((LANES - 80, LANES), jnp.float32))
     top = SHRINK * jnp.concatenate(rows, axis=0).T[:COLS]
-    reached = lane[:COLS] >= LANES - STEPS - 1
+    reached = lax.broadcasted_iota(jnp.int32, (COLS, LANES), 1) >= LANES - STEPS - 1
     for field in range(5):
-        moved = pltpu.roll(top, (LANES - STRIP - STRIP * field) % LANES, 1)
+        moved = pltpu.roll(top, LANES - 16 - 16 * field, 1)
         before = jnp.concatenate([result[field, 120:128, :], result[field, 248:256, :]], axis=0)
         tiles[field] = jnp.where(reached, moved, before)
     last_copies = [
@@ -359,10 +371,18 @@
 
 def first_inner_kernel(state_in, zeta, weight, state, west, east):
     inner_steps(state, zeta, weight, (0, EDGE_SPLIT), COLS - 1)
-    for out, places, shift in ((west, WEST_PLACES, COLS), (east, EAST_PLACES, -COLS)):
-        for (kind, which, col), place in places.items():
+    for out, places, rests, shift in (
+        (west, WEST_PLACES, WEST_RESTS, COLS),
+        (east, EAST_PLACES, EAST_RESTS, -COLS),
+    ):
+        for entry, place in places.items():
+            kind, which, col = entry
             source = {"state": state, "zeta": zeta}[kind].at[which] if kind != "mass" else weight
-            out[place] = source[col + shift].astype(jnp.bfloat16)
+            tile = source[col + shift]
+            sent = tile.astype(jnp.bfloat16)
+            out[place] = sent
+            if entry in rests:
+                out[len(places) + rests.index(entry)] = (tile - sent.astype(jnp.float32)).astype(jnp.bfloat16)
 
 
 def second_inner_kernel(state_in, zeta, weight, sides, state):
@@ -376,9 +396,12 @@
 
 
 def edge_kernel(west, east, state_in, zeta_in, mass_in, out, state, zeta, weight):
-    for source, places in ((west, WEST_PLACES), (east, EAST_PLACES)):
-        for (kind, which, col), place in places.items():
+    for source, places, rests in ((west, WEST_PLACES, WEST_RESTS), (east, EAST_PLACES, EAST_RESTS)):
+        for entry, place in places.items():
+            kind, which, col = entry
             tile = source[place].astype(jnp.float32)
+            if entry in rests:
+                tile = tile + source[len(places) + rests.index(entry)].astype(jnp.float32)
             if kind == "state":
                 state[which, EAST_END - col if col >= HALO + COLS else col] = tile
             elif kind == "mass":
@@ -459,7 +482,7 @@
     stages = [(1,)]
     bit = 4
     while bit < count:
-        stages.append((3 * bit, 2 * bit, bit) if 2 * bit < count else (bit,))
+        stages.append((2 * bit, 3 * bit, bit) if 2 * bit < count else (bit,))
         bit *= 4
     return stages + [(2,)]
 
@@ -534,7 +557,7 @@
         out_specs=(whole,) * 2,
         input_output_aliases={0: 1},
         compiler_params=params,
-        cost_estimate=pl.CostEstimate(flops=1000000000, bytes_accessed=1000000000, transcendentals=0),
+        cost_estimate=pl.CostEstimate(flops=1500000000, bytes_accessed=0, transcendentals=0),
     )(state, zeta, weight)
     for steps in stages[1:]:
         parts = exchange(held, steps, count)
@@ -555,6 +578,7 @@
         out_specs=hbm,
         scratch_shapes=[
             pltpu.VMEM((count, STRIP_PARTS, COLS, LANES), f32),
+            pltpu.VMEM((STRIP_PARTS, LANES, count * COLS), f32),
             pltpu.VMEM((5, COLS, LANES), f32),
             pltpu.SemaphoreType.DMA((4,)),
         ],

time: 21.7 us -> 21.5 us (level)
  starting transfers between devices: 11.5 us -> 11 us
  waiting for transfers between devices: 0.26 us -> 0.66 us
    ppermute x1, waiting for transfers between devices: 0.24 us -> 0.64 us  [on_device(): lax.ppermute(east_send, 'lon', [(i, (i - 1) % count) for i in range(count)])]
    ppermute x5, starting transfers between devices: 7.76 us -> 7.49 us  [exchange(): lax.ppermute(held, 'lon', [(i, i ^ step) for i in range(count)])]
  transfers between devices with their start and end apart: 7 -> 7, of which waited for: 1 -> 1; matrix products, arithmetic and copies ran while one was open for 0% -> 0% of each run, Pallas kernels for 23% -> 24%
where the time goes in v5:
time: 21.5 us; the launch traced here: 21.4 us
  starting transfers between devices  11 us (51%)
  Pallas kernels  9.66 us (45%)
  waiting for transfers between devices  0.66 us (3%)
    ppermute x5, starting transfers between devices, exchange(): lax.ppermute(held, 'lon', [(i, i ^ step) for i in range(count)])  7.49 us
    ppermute x1, starting transfers between devices, on_device(): lax.ppermute(east_send, 'lon', [(i, (i - 1) % count) for i in range(count)])  3.39 us
    pallas_call x1, Pallas kernels, on_device(): pl.pallas_call(edge_kernel, out_shape=(jax.ShapeDtypeStruct(state_shape,...  2.94 us
    pallas_call x1, Pallas kernels, on_device(): pl.pallas_call(pack_kernel, out_shape=(jax.ShapeDtypeStruct((1, STRIP_PAR...  2.35 us
    pallas_call x1, Pallas kernels, on_device(): pl.pallas_call(functools.partial(fold_kernel, offsets), out_shape=jax.Sha...  2.28 us
    pallas_call x1, Pallas kernels, on_device(): pl.pallas_call(first_inner_kernel, out_shape=(extended[0], *sends), in_sp...  1.18 us
    pallas_call x1, Pallas kernels, on_device(): pl.pallas_call(second_inner_kernel, out_shape=(extended[0], extended[0]),...  0.91 us
    ppermute x1, waiting for transfers between devices, on_device(): lax.ppermute(east_send, 'lon', [(i, (i - 1) % count) for i in range(count)])  0.64 us
  transfers between devices with their start and end apart: 7, of which 1 were waited for; matrix products, arithmetic and copies ran while one was open for 0% of the time, Pallas kernels for 24%

profile of v5, /device:TPU:0, one launch (start us, length us, event | category | flops | bytes accessed | tf_op | source)
XLA Modules:
  0.0 21.4 jit_solution(8843677093662859017)
XLA Ops:
  0.0 2.3 %shard_map.64 = (bf16[1,2,16,128]{3,2,1,0:T(8,128)(2,1)S(1)}, f32[1,2,16,128]{3,2,1,0:T(8,128)S(1)}, f32[5,40,16,128]{3,2,1,0:T(8,128)S(1)}, f32[8,40,16,128]{3,2,1,0:T(8,128)S(1)}, f32[40,16,128]{2,1,0:T(8,128)S(1)}) custom-call(f32[5,256,128]{2,1,0:T(8,128)} %bitcast.10, bf16[8,3,16,2048]{3,2,1,0:T(8,128)(2,1)} %strains_hbm.1, f32[16,2048]{1,0:T(8,128)} %strength_hbm.1, ...), custom_call_target="tpu_custom_call" | custom-call | tf_op jit(solution)/shard_map/pallas_call | solution.py:515
  2.4 0.5 %collective-permute-start = (bf16[1,2,16,128]{3,2,1,0:T(8,128)(2,1)S(1)}, bf16[1,2,16,128]{3,2,1,0:T(8,128)(2,1)S(1)}, u32[]{:S(2)}, u32[]{:S(2)}) collective-permute-start(bf16[1,2,16,128]{3,2,1,0:T(8,128)(2,1)S(1)} %get-tuple-element.20.refs_0_), channel_id=1, source_target_pairs={{0,1},{1,0},{2,3},{3,2},{4,5},{5,4},{6,7},{7,6},{8,9},{9,8},{10,11... | collective-permute-start | bytes 24584 | tf_op jit(solution)/shard_map/ppermute | solution.py:491
  2.9 1.2 %shard_map.65 = (f32[5,40,16,128]{3,2,1,0:T(8,128)S(1)}, bf16[56,16,128]{2,1,0:T(8,128)(2,1)S(1)}, bf16[43,16,128]{2,1,0:T(8,128)(2,1)S(1)}) custom-call(f32[5,40,16,128]{3,2,1,0:T(8,128)S(1)} %get-tuple-element.21.state_in, f32[8,40,16,128]{3,2,1,0:T(8,128)S(1)} %get-tuple-element.22.zeta.zeta_in, ...), custom_call_target="tpu_custom_call", output_to_operand_aliasing={{0}: (0, {})} | custom-call | tf_op jit(solution)/shard_map/pallas_call | solution.py:542
  4.1 0.0 collective-permute-done.refs_1_
  4.1 0.1 collective-permute-start.5
  4.2 4.0 %collective-permute-start.1 = (bf16[2,2,16,128]{3,2,1,0:T(8,128)(2,1)S(1)}, bf16[2,2,16,128]{3,2,1,0:T(8,128)(2,1)S(1)}, u32[]{:S(2)}, u32[]{:S(2)}) collective-permute-start(bf16[2,2,16,128]{3,2,1,0:T(8,128)(2,1)S(1)} %get-tuple-element.26.refs_0_), channel_id=1, source_target_pairs={{0,8},{1,9},{2,10},{3,11},{4,12},{5,13},{6,14},{7,15},{8,0},{9,1},... | collective-permute-start | bytes 49160 | tf_op jit(solution)/shard_map/ppermute | solution.py:491
  8.2 1.3 %collective-permute-start.2 = (bf16[2,2,16,128]{3,2,1,0:T(8,128)(2,1)S(1)}, bf16[2,2,16,128]{3,2,1,0:T(8,128)(2,1)S(1)}, u32[]{:S(2)}, u32[]{:S(2)}) collective-permute-start(bf16[2,2,16,128]{3,2,1,0:T(8,128)(2,1)S(1)} %get-tuple-element.26.refs_0_), channel_id=1, source_target_pairs={{0,12},{1,13},{2,14},{3,15},{4,8},{5,9},{6,10},{7,11},{8,4},{9,5},... | collective-permute-start | bytes 49160 | tf_op jit(solution)/shard_map/ppermute | solution.py:491
  9.6 0.2 %collective-permute-start.3 = (bf16[2,2,16,128]{3,2,1,0:T(8,128)(2,1)S(1)}, bf16[2,2,16,128]{3,2,1,0:T(8,128)(2,1)S(1)}, u32[]{:S(2)}, u32[]{:S(2)}) collective-permute-start(bf16[2,2,16,128]{3,2,1,0:T(8,128)(2,1)S(1)} %get-tuple-element.26.refs_0_), channel_id=1, source_target_pairs={{0,4},{1,5},{2,6},{3,7},{4,0},{5,1},{6,2},{7,3},{8,12},{9,13},{10,... | collective-permute-start | bytes 49160 | tf_op jit(solution)/shard_map/ppermute | solution.py:491
  9.8 3.4 %collective-permute-start.6 = (bf16[43,16,128]{2,1,0:T(8,128)(2,1)S(1)}, bf16[43,16,128]{2,1,0:T(8,128)(2,1)S(1)}, u32[]{:S(2)}, u32[]{:S(2)}) collective-permute-start(bf16[43,16,128]{2,1,0:T(8,128)(2,1)S(1)} %get-tuple-element.32), channel_id=1, source_target_pairs={{0,15},{1,0},{2,1},{3,2},{4,3},{5,4},{6,5},{7,6},{8,7},{9,8},{10,9... | collective-permute-start | bytes 528392 | tf_op jit(solution)/shard_map/ppermute | solution.py:552
  13.2 0.9 %shard_map.67 = (f32[5,40,16,128]{3,2,1,0:T(8,128)S(1)}, f32[5,40,16,128]{3,2,1,0:T(8,128)S(1)}) custom-call(f32[5,40,16,128]{3,2,1,0:T(8,128)S(1)} %get-tuple-element.27.state_in, f32[8,40,16,128]{3,2,1,0:T(8,128)S(1)} %get-tuple-element.22.zeta.zeta_in, f32[40,16,128]{2,1,0:T(8,128)S(1)} %get-tuple-element.23.weight.mass_in), custom_call_target="tpu_custom_call", output_to_operand_aliasing={{1}: (0, {})} | custom-call | flops 1500000000 | tf_op jit(solution)/shard_map/pallas_call | solution.py:553
  14.1 0.0 collective-permute-done.1.refs_1_
  14.1 0.0 collective-permute-done.2.refs_2_
  14.1 0.0 collective-permute-done.3.refs_3_
  14.2 1.4 %collective-permute-start.4 = (bf16[8,2,16,128]{3,2,1,0:T(8,128)(2,1)S(1)}, bf16[8,2,16,128]{3,2,1,0:T(8,128)(2,1)S(1)}, u32[]{:S(2)}, u32[]{:S(2)}) collective-permute-start(bf16[8,2,16,128]{3,2,1,0:T(8,128)(2,1)S(1)} %get-tuple-element.29.refs_0_), channel_id=1, source_target_pairs={{0,2},{1,3},{2,0},{3,1},{4,6},{5,7},{6,4},{7,5},{8,10},{9,11},{10,... | collective-permute-start | bytes 196616 | tf_op jit(solution)/shard_map/ppermute | solution.py:491
  15.5 0.6 %collective-permute-done.6.east = bf16[43,16,128]{2,1,0:T(8,128)(2,1)S(1)} collective-permute-done((bf16[43,16,128]{2,1,0:T(8,128)(2,1)S(1)}, bf16[43,16,128]{2,1,0:T(8,128)(2,1)S(1)}, u32[]{:S(2)}, u32[]{:S(2)}) %collective-permute-start.6) | collective-permute-done | bytes 176160 | tf_op jit(solution)/shard_map/ppermute | solution.py:552
  16.2 0.0 collective-permute-done.5.west
  16.2 2.9 %shard_map.69 = (f32[5,256,128]{2,1,0:T(8,128)S(1)}, f32[5,40,16,128]{3,2,1,0:T(8,128)S(1)}, f32[8,40,16,128]{3,2,1,0:T(8,128)S(1)}, f32[40,16,128]{2,1,0:T(8,128)S(1)}) custom-call(bf16[56,16,128]{2,1,0:T(8,128)(2,1)S(1)} %collective-permute-done.5.west, ...), custom_call_target="tpu_custom_call", output_to_operand_aliasing={{1}: (2, {}), {2}: (3, {}), {3}: (4, {})} | custom-call | tf_op jit(solution)/shard_map/pallas_call | solution.py:566
  19.1 0.0 collective-permute-done.4.refs_1_
  19.1 2.3 %shard_map.70 = f32[5,256,128]{2,1,0:T(8,128)} custom-call(bf16[8,2,16,128]{3,2,1,0:T(8,128)(2,1)S(1)} %get-tuple-element.29.refs_0_, bf16[8,2,16,128]{3,2,1,0:T(8,128)(2,1)S(1)} %collective-permute-done.4.refs_1_, f32[1,2,16,128]{3,2,1,0:T(8,128)S(1)} %get-tuple-element.30.refs_2_, f32[5,256,128]{2,1,0:T(8,128)S(1)} %get-tuple-element.34.refs_3_), custom_call_target="tpu_custom_call" | custom-call | tf_op jit(solution)/shard_map/pallas_call | solution.py:574
  (2 shorter events, 0.0 us)
Async XLA Ops:
  2.4 1.7 %collective-permute-start = (bf16[1,2,16,128]{3,2,1,0:T(8,128)(2,1)S(1)}, bf16[1,2,16,128]{3,2,1,0:T(8,128)(2,1)S(1)}, u32[]{:S(2)}, u32[]{:S(2)}) collective-permute-start(bf16[1,2,16,128]{3,2,1,0:T(8,128)(2,1)S(1)} %get-tuple-element.20.refs_0_), channel_id=1, source_target_pairs={{0,1},{1,0},{2,3},{3,2},{4,5},{5,4},{6,7},{7,6},{8,9},{9,8},{10,11... | collective-permute-start | bytes 24584 | tf_op jit(solution)/shard_map/ppermute | solution.py:491
  4.1 12.1 %collective-permute-start.5 = (bf16[56,16,128]{2,1,0:T(8,128)(2,1)S(1)}, bf16[56,16,128]{2,1,0:T(8,128)(2,1)S(1)}, u32[]{:S(2)}, u32[]{:S(2)}) collective-permute-start(bf16[56,16,128]{2,1,0:T(8,128)(2,1)S(1)} %get-tuple-element.31), channel_id=1, source_target_pairs={{0,1},{1,2},{2,3},{3,4},{4,5},{5,6},{6,7},{7,8},{8,9},{9,10},{10,1... | collective-permute-start | bytes 688136 | tf_op jit(solution)/shard_map/ppermute | solution.py:551
  4.2 9.9 %collective-permute-start.1 = (bf16[2,2,16,128]{3,2,1,0:T(8,128)(2,1)S(1)}, bf16[2,2,16,128]{3,2,1,0:T(8,128)(2,1)S(1)}, u32[]{:S(2)}, u32[]{:S(2)}) collective-permute-start(bf16[2,2,16,128]{3,2,1,0:T(8,128)(2,1)S(1)} %get-tuple-element.26.refs_0_), channel_id=1, source_target_pairs={{0,8},{1,9},{2,10},{3,11},{4,12},{5,13},{6,14},{7,15},{8,0},{9,1},... | collective-permute-start | bytes 49160 | tf_op jit(solution)/shard_map/ppermute | solution.py:491
  8.2 5.9 %collective-permute-start.2 = (bf16[2,2,16,128]{3,2,1,0:T(8,128)(2,1)S(1)}, bf16[2,2,16,128]{3,2,1,0:T(8,128)(2,1)S(1)}, u32[]{:S(2)}, u32[]{:S(2)}) collective-permute-start(bf16[2,2,16,128]{3,2,1,0:T(8,128)(2,1)S(1)} %get-tuple-element.26.refs_0_), channel_id=1, source_target_pairs={{0,12},{1,13},{2,14},{3,15},{4,8},{5,9},{6,10},{7,11},{8,4},{9,5},... | collective-permute-start | bytes 49160 | tf_op jit(solution)/shard_map/ppermute | solution.py:491
  9.6 4.6 %collective-permute-start.3 = (bf16[2,2,16,128]{3,2,1,0:T(8,128)(2,1)S(1)}, bf16[2,2,16,128]{3,2,1,0:T(8,128)(2,1)S(1)}, u32[]{:S(2)}, u32[]{:S(2)}) collective-permute-start(bf16[2,2,16,128]{3,2,1,0:T(8,128)(2,1)S(1)} %get-tuple-element.26.refs_0_), channel_id=1, source_target_pairs={{0,4},{1,5},{2,6},{3,7},{4,0},{5,1},{6,2},{7,3},{8,12},{9,13},{10,... | collective-permute-start | bytes 49160 | tf_op jit(solution)/shard_map/ppermute | solution.py:491
  9.8 6.4 %collective-permute-start.6 = (bf16[43,16,128]{2,1,0:T(8,128)(2,1)S(1)}, bf16[43,16,128]{2,1,0:T(8,128)(2,1)S(1)}, u32[]{:S(2)}, u32[]{:S(2)}) collective-permute-start(bf16[43,16,128]{2,1,0:T(8,128)(2,1)S(1)} %get-tuple-element.32), channel_id=1, source_target_pairs={{0,15},{1,0},{2,1},{3,2},{4,3},{5,4},{6,5},{7,6},{8,7},{9,8},{10,9... | collective-permute-start | bytes 528392 | tf_op jit(solution)/shard_map/ppermute | solution.py:552
  14.2 5.0 %collective-permute-start.4 = (bf16[8,2,16,128]{3,2,1,0:T(8,128)(2,1)S(1)}, bf16[8,2,16,128]{3,2,1,0:T(8,128)(2,1)S(1)}, u32[]{:S(2)}, u32[]{:S(2)}) collective-permute-start(bf16[8,2,16,128]{3,2,1,0:T(8,128)(2,1)S(1)} %get-tuple-element.29.refs_0_), channel_id=1, source_target_pairs={{0,2},{1,3},{2,0},{3,1},{4,6},{5,7},{6,4},{7,5},{8,10},{9,11},{10,... | collective-permute-start | bytes 196616 | tf_op jit(solution)/shard_map/ppermute | solution.py:491

commit v6 on v5

--- a/solution.py
+++ b/solution.py
@@ -332,7 +332,7 @@
     def velocities(keep_u, keep_v, west_x, west_c, x, c, y):
         return keep_u + (west_x - x) + (c - row_above(c)), keep_v + (west_c - c) + (y - row_above(y))
 
-    def advance(step, place, next_place, col, carry, moves=None):
+    def advance(step, place, next_place, col, carry):
         p, q, keep_u, keep_v, west_x, west_c = carry
         next_p, next_q, next_u, next_v = forces(next_place, col + 1)
         along = 0.5 * (p - next_p)
@@ -341,10 +341,6 @@
         new_one = one[place] + (along + across)
         new_two = two[place] + (along - across)
         new_shear = shear[place] + turn + (q - next_q)
-        if moves is not None:
-            new_one = jnp.where(moves, new_one, one[place])
-            new_two = jnp.where(moves, new_two, two[place])
-            new_shear = jnp.where(moves, new_shear, shear[place])
         x, c, y = strains_of(step, col, new_one, new_two, new_shear)
         new_u, new_v = velocities(keep_u, keep_v, west_x, west_c, x, c, y)
         return (new_u, new_v, new_one, new_two, new_shear), (next_p, next_q, next_u, next_v, x, c)
@@ -352,25 +348,20 @@
     return forces, stored_strains, velocities, advance
 
 
-def inner_steps(state, zeta, weight, steps, width):
+def inner_steps(state, zeta, weight, steps):
     forces, _, _, advance = stepper(state, zeta, weight)
     blank = jnp.zeros((TILE, LANES), jnp.float32)
-
-    @pl.loop(*steps)
-    def _(step):
+    for step in steps:
         begin = HALO + step
-        last = HALO + COLS - 2 - step
         carry = forces(begin, begin) + (blank, blank)
-        for part in range(width):
-            col = begin + part
+        for col in range(begin, HALO + COLS - 1 - step):
             new, carry = advance(step, col, col + 1, col, carry)
-            for field in range(5):
-                valid = (col <= last) & (part > 0) if field < 2 else col <= last
-                state[field, col] = jnp.where(valid, new[field], state[field, col])
+            for field in range(2 if col == begin else 0, 5):
+                state[field, col] = new[field]
 
 
 def first_inner_kernel(state_in, zeta, weight, state, west, east):
-    inner_steps(state, zeta, weight, (0, EDGE_SPLIT), COLS - 1)
+    inner_steps(state, zeta, weight, range(EDGE_SPLIT))
     for out, places, rests, shift in (
         (west, WEST_PLACES, WEST_RESTS, COLS),
         (east, EAST_PLACES, EAST_RESTS, -COLS),
@@ -386,7 +377,7 @@
 
 
 def second_inner_kernel(state_in, zeta, weight, sides, state):
-    inner_steps(state, zeta, weight, (EDGE_SPLIT, STEPS), COLS - 1 - 2 * EDGE_SPLIT)
+    inner_steps(state, zeta, weight, range(EDGE_SPLIT, STEPS))
 
     @pl.loop(0, 9)
     def _(at):
@@ -412,26 +403,22 @@
     forces, stored_strains, velocities, advance = stepper(state, zeta, weight)
     blank = jnp.zeros((TILE, LANES), jnp.float32)
 
-    def growing(steps, reach):
-        @pl.loop(*steps)
-        def _(step):
-            for middle in (HALO - 1, HALO + COLS - 1):
-                cols = range(middle - reach, middle + reach + 2)
-                at = [col if middle < HALO else EAST_END - col for col in range(cols[0], cols[-1] + 2)]
-                carry = forces(at[0], cols[0]) + (blank, blank)
-                for part, col in enumerate(cols):
-                    old = [state[field, at[part]] for field in range(5)]
-                    left = abs(col - middle) <= step
-                    new, carry = advance(step, at[part], at[part + 1], col, carry, left)
-                    moves = left | (step + middle + 1 == col)
-                    for field in range(5):
-                        if field >= 2:
-                            state[field, at[part]] = new[field]
-                        elif part:
-                            state[field, at[part]] = jnp.where(moves, new[field], old[field])
-
-    growing((0, 2), 2)
-    growing((2, EDGE_SPLIT), 4)
+    def grow(step):
+        for middle in (HALO - 1, HALO + COLS - 1):
+            cols = range(middle - step, middle + step + 1)
+            at = [col if middle < HALO else EAST_END - col for col in (*cols, middle + step + 1)]
+            behind = middle - step - 1
+            x, c, _ = stored_strains(step, behind if middle < HALO else EAST_END - behind, behind)
+            carry = forces(at[0], cols[0]) + (x, c)
+            for part, col in enumerate(cols):
+                new, carry = advance(step, at[part], at[part + 1], col, carry)
+                for field in range(5):
+                    state[field, at[part]] = new[field]
+            ahead = middle + step + 1
+            state[0, at[-1]], state[1, at[-1]] = velocities(*carry[2:], *stored_strains(step, at[-1], ahead))
+
+    for step in range(EDGE_SPLIT):
+        grow(step)
 
     start = EAST_END - (HALO + COLS - 1)
 

time: 21.5 us -> 20.9 us (0.972)
  Pallas kernels: 9.66 us -> 8.67 us
  starting transfers between devices: 11 us -> 11.3 us
    pallas_call x1, Pallas kernels: 2.94 us -> 2.37 us  [on_device(): pl.pallas_call(edge_kernel, out_shape=(jax.ShapeDtypeStruct(state_shape,...]
    pallas_call x1, Pallas kernels: 0.91 us -> 0.61 us  [on_device(): pl.pallas_call(second_inner_kernel, out_shape=(extended[0], extended[0]),...]
    ppermute x5, starting transfers between devices: 7.49 us -> 7.79 us  [exchange(): lax.ppermute(held, 'lon', [(i, i ^ step) for i in range(count)])]
  transfers between devices with their start and end apart: 7 -> 7, of which waited for: 1 -> 1; matrix products, arithmetic and copies ran while one was open for 0% -> 0% of each run, Pallas kernels for 24% -> 20%
where the time goes in v6:
time: 20.9 us; the launch traced here: 20.7 us
  starting transfers between devices  11.3 us (54%)
  Pallas kernels  8.67 us (41%)
  waiting for transfers between devices  0.67 us (3%)
    ppermute x5, starting transfers between devices, exchange(): lax.ppermute(held, 'lon', [(i, i ^ step) for i in range(count)])  7.79 us
    ppermute x1, starting transfers between devices, on_device(): lax.ppermute(east_send, 'lon', [(i, (i - 1) % count) for i in range(count)])  3.4 us
    pallas_call x1, Pallas kernels, on_device(): pl.pallas_call(edge_kernel, out_shape=(jax.ShapeDtypeStruct(state_shape,...  2.37 us
    pallas_call x1, Pallas kernels, on_device(): pl.pallas_call(pack_kernel, out_shape=(jax.ShapeDtypeStruct((1, STRIP_PAR...  2.35 us
    pallas_call x1, Pallas kernels, on_device(): pl.pallas_call(functools.partial(fold_kernel, offsets), out_shape=jax.Sha...  2.28 us
    pallas_call x1, Pallas kernels, on_device(): pl.pallas_call(first_inner_kernel, out_shape=(extended[0], *sends), in_sp...  1.06 us
    ppermute x1, waiting for transfers between devices, on_device(): lax.ppermute(east_send, 'lon', [(i, (i - 1) % count) for i in range(count)])  0.66 us
    pallas_call x1, Pallas kernels, on_device(): pl.pallas_call(second_inner_kernel, out_shape=(extended[0], extended[0]),...  0.61 us
  transfers between devices with their start and end apart: 7, of which 1 were waited for; matrix products, arithmetic and copies ran while one was open for 0% of the time, Pallas kernels for 20%

profile of v6, /device:TPU:0, one launch (start us, length us, event | category | flops | bytes accessed | tf_op | source)
XLA Modules:
  0.0 20.7 jit_solution(2424714672020184680)
XLA Ops:
  0.0 2.3 %shard_map.64 = (bf16[1,2,16,128]{3,2,1,0:T(8,128)(2,1)S(1)}, f32[1,2,16,128]{3,2,1,0:T(8,128)S(1)}, f32[5,40,16,128]{3,2,1,0:T(8,128)S(1)}, f32[8,40,16,128]{3,2,1,0:T(8,128)S(1)}, f32[40,16,128]{2,1,0:T(8,128)S(1)}) custom-call(f32[5,256,128]{2,1,0:T(8,128)} %bitcast.10, bf16[8,3,16,2048]{3,2,1,0:T(8,128)(2,1)} %strains_hbm.1, f32[16,2048]{1,0:T(8,128)} %strength_hbm.1, ...), custom_call_target="tpu_custom_call" | custom-call | tf_op jit(solution)/shard_map/pallas_call | solution.py:502
  2.4 0.5 %collective-permute-start = (bf16[1,2,16,128]{3,2,1,0:T(8,128)(2,1)S(1)}, bf16[1,2,16,128]{3,2,1,0:T(8,128)(2,1)S(1)}, u32[]{:S(2)}, u32[]{:S(2)}) collective-permute-start(bf16[1,2,16,128]{3,2,1,0:T(8,128)(2,1)S(1)} %get-tuple-element.20.refs_0_), channel_id=1, source_target_pairs={{0,1},{1,0},{2,3},{3,2},{4,5},{5,4},{6,7},{7,6},{8,9},{9,8},{10,11... | collective-permute-start | bytes 24584 | tf_op jit(solution)/shard_map/ppermute | solution.py:478
  2.9 1.1 %shard_map.65 = (f32[5,40,16,128]{3,2,1,0:T(8,128)S(1)}, bf16[56,16,128]{2,1,0:T(8,128)(2,1)S(1)}, bf16[43,16,128]{2,1,0:T(8,128)(2,1)S(1)}) custom-call(f32[5,40,16,128]{3,2,1,0:T(8,128)S(1)} %get-tuple-element.21.state_in, f32[8,40,16,128]{3,2,1,0:T(8,128)S(1)} %get-tuple-element.22.zeta.zeta_in, ...), custom_call_target="tpu_custom_call", output_to_operand_aliasing={{0}: (0, {})} | custom-call | tf_op jit(solution)/shard_map/pallas_call | solution.py:529
  3.9 0.0 collective-permute-done.refs_1_
  4.0 0.1 collective-permute-start.5
  4.1 4.0 %collective-permute-start.1 = (bf16[2,2,16,128]{3,2,1,0:T(8,128)(2,1)S(1)}, bf16[2,2,16,128]{3,2,1,0:T(8,128)(2,1)S(1)}, u32[]{:S(2)}, u32[]{:S(2)}) collective-permute-start(bf16[2,2,16,128]{3,2,1,0:T(8,128)(2,1)S(1)} %get-tuple-element.26.refs_0_), channel_id=1, source_target_pairs={{0,8},{1,9},{2,10},{3,11},{4,12},{5,13},{6,14},{7,15},{8,0},{9,1},... | collective-permute-start | bytes 49160 | tf_op jit(solution)/shard_map/ppermute | solution.py:478
  8.1 1.3 %collective-permute-start.2 = (bf16[2,2,16,128]{3,2,1,0:T(8,128)(2,1)S(1)}, bf16[2,2,16,128]{3,2,1,0:T(8,128)(2,1)S(1)}, u32[]{:S(2)}, u32[]{:S(2)}) collective-permute-start(bf16[2,2,16,128]{3,2,1,0:T(8,128)(2,1)S(1)} %get-tuple-element.26.refs_0_), channel_id=1, source_target_pairs={{0,12},{1,13},{2,14},{3,15},{4,8},{5,9},{6,10},{7,11},{8,4},{9,5},... | collective-permute-start | bytes 49160 | tf_op jit(solution)/shard_map/ppermute | solution.py:478
  9.5 0.2 %collective-permute-start.3 = (bf16[2,2,16,128]{3,2,1,0:T(8,128)(2,1)S(1)}, bf16[2,2,16,128]{3,2,1,0:T(8,128)(2,1)S(1)}, u32[]{:S(2)}, u32[]{:S(2)}) collective-permute-start(bf16[2,2,16,128]{3,2,1,0:T(8,128)(2,1)S(1)} %get-tuple-element.26.refs_0_), channel_id=1, source_target_pairs={{0,4},{1,5},{2,6},{3,7},{4,0},{5,1},{6,2},{7,3},{8,12},{9,13},{10,... | collective-permute-start | bytes 49160 | tf_op jit(solution)/shard_map/ppermute | solution.py:478
  9.7 3.4 %collective-permute-start.6 = (bf16[43,16,128]{2,1,0:T(8,128)(2,1)S(1)}, bf16[43,16,128]{2,1,0:T(8,128)(2,1)S(1)}, u32[]{:S(2)}, u32[]{:S(2)}) collective-permute-start(bf16[43,16,128]{2,1,0:T(8,128)(2,1)S(1)} %get-tuple-element.32), channel_id=1, source_target_pairs={{0,15},{1,0},{2,1},{3,2},{4,3},{5,4},{6,5},{7,6},{8,7},{9,8},{10,9... | collective-permute-start | bytes 528392 | tf_op jit(solution)/shard_map/ppermute | solution.py:539
  13.1 0.6 %shard_map.67 = (f32[5,40,16,128]{3,2,1,0:T(8,128)S(1)}, f32[5,40,16,128]{3,2,1,0:T(8,128)S(1)}) custom-call(f32[5,40,16,128]{3,2,1,0:T(8,128)S(1)} %get-tuple-element.27.state_in, f32[8,40,16,128]{3,2,1,0:T(8,128)S(1)} %get-tuple-element.22.zeta.zeta_in, f32[40,16,128]{2,1,0:T(8,128)S(1)} %get-tuple-element.23.weight.mass_in), custom_call_target="tpu_custom_call", output_to_operand_aliasing={{1}: (0, {})} | custom-call | flops 1500000000 | tf_op jit(solution)/shard_map/pallas_call | solution.py:540
  13.7 0.0 collective-permute-done.1.refs_1_
  13.7 0.0 collective-permute-done.2.refs_2_
  13.7 0.0 collective-permute-done.3.refs_3_
  13.8 1.7 %collective-permute-start.4 = (bf16[8,2,16,128]{3,2,1,0:T(8,128)(2,1)S(1)}, bf16[8,2,16,128]{3,2,1,0:T(8,128)(2,1)S(1)}, u32[]{:S(2)}, u32[]{:S(2)}) collective-permute-start(bf16[8,2,16,128]{3,2,1,0:T(8,128)(2,1)S(1)} %get-tuple-element.29.refs_0_), channel_id=1, source_target_pairs={{0,2},{1,3},{2,0},{3,1},{4,6},{5,7},{6,4},{7,5},{8,10},{9,11},{10,... | collective-permute-start | bytes 196616 | tf_op jit(solution)/shard_map/ppermute | solution.py:478
  15.4 0.7 %collective-permute-done.6.east = bf16[43,16,128]{2,1,0:T(8,128)(2,1)S(1)} collective-permute-done((bf16[43,16,128]{2,1,0:T(8,128)(2,1)S(1)}, bf16[43,16,128]{2,1,0:T(8,128)(2,1)S(1)}, u32[]{:S(2)}, u32[]{:S(2)}) %collective-permute-start.6) | collective-permute-done | bytes 176160 | tf_op jit(solution)/shard_map/ppermute | solution.py:539
  16.1 0.0 collective-permute-done.5.west
  16.1 2.4 %shard_map.69 = (f32[5,256,128]{2,1,0:T(8,128)S(1)}, f32[5,40,16,128]{3,2,1,0:T(8,128)S(1)}, f32[8,40,16,128]{3,2,1,0:T(8,128)S(1)}, f32[40,16,128]{2,1,0:T(8,128)S(1)}) custom-call(bf16[56,16,128]{2,1,0:T(8,128)(2,1)S(1)} %collective-permute-done.5.west, ...), custom_call_target="tpu_custom_call", output_to_operand_aliasing={{1}: (2, {}), {2}: (3, {}), {3}: (4, {})} | custom-call | tf_op jit(solution)/shard_map/pallas_call | solution.py:553
  18.4 0.0 collective-permute-done.4.refs_1_
  18.5 2.3 %shard_map.70 = f32[5,256,128]{2,1,0:T(8,128)} custom-call(bf16[8,2,16,128]{3,2,1,0:T(8,128)(2,1)S(1)} %get-tuple-element.29.refs_0_, bf16[8,2,16,128]{3,2,1,0:T(8,128)(2,1)S(1)} %collective-permute-done.4.refs_1_, f32[1,2,16,128]{3,2,1,0:T(8,128)S(1)} %get-tuple-element.30.refs_2_, f32[5,256,128]{2,1,0:T(8,128)S(1)} %get-tuple-element.34.refs_3_), custom_call_target="tpu_custom_call" | custom-call | tf_op jit(solution)/shard_map/pallas_call | solution.py:561
  (2 shorter events, 0.0 us)
Async XLA Ops:
  2.4 1.6 %collective-permute-start = (bf16[1,2,16,128]{3,2,1,0:T(8,128)(2,1)S(1)}, bf16[1,2,16,128]{3,2,1,0:T(8,128)(2,1)S(1)}, u32[]{:S(2)}, u32[]{:S(2)}) collective-permute-start(bf16[1,2,16,128]{3,2,1,0:T(8,128)(2,1)S(1)} %get-tuple-element.20.refs_0_), channel_id=1, source_target_pairs={{0,1},{1,0},{2,3},{3,2},{4,5},{5,4},{6,7},{7,6},{8,9},{9,8},{10,11... | collective-permute-start | bytes 24584 | tf_op jit(solution)/shard_map/ppermute | solution.py:478
  4.0 12.1 %collective-permute-start.5 = (bf16[56,16,128]{2,1,0:T(8,128)(2,1)S(1)}, bf16[56,16,128]{2,1,0:T(8,128)(2,1)S(1)}, u32[]{:S(2)}, u32[]{:S(2)}) collective-permute-start(bf16[56,16,128]{2,1,0:T(8,128)(2,1)S(1)} %get-tuple-element.31), channel_id=1, source_target_pairs={{0,1},{1,2},{2,3},{3,4},{4,5},{5,6},{6,7},{7,8},{8,9},{9,10},{10,1... | collective-permute-start | bytes 688136 | tf_op jit(solution)/shard_map/ppermute | solution.py:538
  4.1 9.6 %collective-permute-start.1 = (bf16[2,2,16,128]{3,2,1,0:T(8,128)(2,1)S(1)}, bf16[2,2,16,128]{3,2,1,0:T(8,128)(2,1)S(1)}, u32[]{:S(2)}, u32[]{:S(2)}) collective-permute-start(bf16[2,2,16,128]{3,2,1,0:T(8,128)(2,1)S(1)} %get-tuple-element.26.refs_0_), channel_id=1, source_target_pairs={{0,8},{1,9},{2,10},{3,11},{4,12},{5,13},{6,14},{7,15},{8,0},{9,1},... | collective-permute-start | bytes 49160 | tf_op jit(solution)/shard_map/ppermute | solution.py:478
  8.1 5.6 %collective-permute-start.2 = (bf16[2,2,16,128]{3,2,1,0:T(8,128)(2,1)S(1)}, bf16[2,2,16,128]{3,2,1,0:T(8,128)(2,1)S(1)}, u32[]{:S(2)}, u32[]{:S(2)}) collective-permute-start(bf16[2,2,16,128]{3,2,1,0:T(8,128)(2,1)S(1)} %get-tuple-element.26.refs_0_), channel_id=1, source_target_pairs={{0,12},{1,13},{2,14},{3,15},{4,8},{5,9},{6,10},{7,11},{8,4},{9,5},... | collective-permute-start | bytes 49160 | tf_op jit(solution)/shard_map/ppermute | solution.py:478
  9.5 4.3 %collective-permute-start.3 = (bf16[2,2,16,128]{3,2,1,0:T(8,128)(2,1)S(1)}, bf16[2,2,16,128]{3,2,1,0:T(8,128)(2,1)S(1)}, u32[]{:S(2)}, u32[]{:S(2)}) collective-permute-start(bf16[2,2,16,128]{3,2,1,0:T(8,128)(2,1)S(1)} %get-tuple-element.26.refs_0_), channel_id=1, source_target_pairs={{0,4},{1,5},{2,6},{3,7},{4,0},{5,1},{6,2},{7,3},{8,12},{9,13},{10,... | collective-permute-start | bytes 49160 | tf_op jit(solution)/shard_map/ppermute | solution.py:478
  9.7 6.4 %collective-permute-start.6 = (bf16[43,16,128]{2,1,0:T(8,128)(2,1)S(1)}, bf16[43,16,128]{2,1,0:T(8,128)(2,1)S(1)}, u32[]{:S(2)}, u32[]{:S(2)}) collective-permute-start(bf16[43,16,128]{2,1,0:T(8,128)(2,1)S(1)} %get-tuple-element.32), channel_id=1, source_target_pairs={{0,15},{1,0},{2,1},{3,2},{4,3},{5,4},{6,5},{7,6},{8,7},{9,8},{10,9... | collective-permute-start | bytes 528392 | tf_op jit(solution)/shard_map/ppermute | solution.py:539
  13.8 4.7 %collective-permute-start.4 = (bf16[8,2,16,128]{3,2,1,0:T(8,128)(2,1)S(1)}, bf16[8,2,16,128]{3,2,1,0:T(8,128)(2,1)S(1)}, u32[]{:S(2)}, u32[]{:S(2)}) collective-permute-start(bf16[8,2,16,128]{3,2,1,0:T(8,128)(2,1)S(1)} %get-tuple-element.29.refs_0_), channel_id=1, source_target_pairs={{0,2},{1,3},{2,0},{3,1},{4,6},{5,7},{6,4},{7,5},{8,10},{9,11},{10,... | collective-permute-start | bytes 196616 | tf_op jit(solution)/shard_map/ppermute | solution.py:478

commit v7 on v6

--- a/solution.py
+++ b/solution.py
@@ -218,16 +218,30 @@
         for r in range(count)
     ]
 
-    def at_fold(value):
-        rows = [
-            jnp.take_along_axis(
-                value[8:, LANES * (count - 1 - r) : LANES * (count - r)], places[r], axis=1,
-                mode="promise_in_bounds",
-            )
-            for r in range(count)
-        ]
-        far = jnp.where(far_row, jnp.concatenate(rows, axis=1), 0.0)
-        return jnp.concatenate([jnp.zeros((8, total), jnp.float32), far], axis=0)
+    west_places = [jnp.where(place == 0, LANES - 1, place - 1) for place in places]
+
+    def gathered(value, r, place):
+        part = value[STRIP - 8 :, LANES * (r % count) : LANES * (r % count) + LANES]
+        return jnp.take_along_axis(part, place, axis=1, mode="promise_in_bounds")
+
+    def by_partner(value):
+        return jnp.concatenate([gathered(value, count - 1 - r, places[r]) for r in range(count)], axis=1)
+
+    def by_partner_west(value):
+        return jnp.concatenate(
+            [
+                jnp.where(
+                    places[r] == 0,
+                    gathered(value, count - 2 - r, west_places[r]),
+                    gathered(value, count - 1 - r, west_places[r]),
+                )
+                for r in range(count)
+            ],
+            axis=1,
+        )
+
+    def at_fold(far):
+        return jnp.concatenate([jnp.zeros((STRIP - 8, total), jnp.float32), jnp.where(far_row, far, 0.0)], axis=0)
 
     def next_col(value):
         return pltpu.roll(value, total - 1, 1)
@@ -244,19 +258,28 @@
     vel_u, vel_v, one, two, shear, weight = (field(at) for at in range(6))
     before = turned[0, STRIP_BEFORE : STRIP_BEFORE + 8, :]
     wet = weight != 0.0
+    next_weight = next_col(weight)
+    far_weight = by_partner(weight)
     for step in range(STEPS):
         p = weight * vel_u
         q = weight * vel_v
+        if step == 0:
+            next_p, next_q, far_p, far_q = next_col(p), next_col(q), by_partner(p), by_partner(q)
+        else:
+            next_p = next_weight * (next_col(rest_u) + x)
+            next_q = next_weight * (next_col(rest_v) + third)
+            far_p = far_weight * (by_partner(rest_u) + by_partner_west(x))
+            far_q = far_weight * (by_partner(rest_v) + by_partner_west(third))
         low_p = row_below(p)
         low_q = row_below(q)
         if step == 0:
             low_p = jnp.where(row == 0, before[2:3] * before[0:1], low_p)
             low_q = jnp.where(row == 0, before[2:3] * before[1:2], low_q)
-        along = 0.5 * (p - next_col(p))
-        across = 0.5 * (low_q - q + at_fold(q))
+        along = 0.5 * (p - next_p)
+        across = 0.5 * (low_q - q + at_fold(far_q))
         one = one + (along + across)
         two = two + (along - across)
-        shear = shear + (low_p - p - at_fold(p)) + (q - next_col(q))
+        shear = shear + (low_p - p - at_fold(far_p)) + (q - next_q)
         zeta = field(6 + step)
         first = zeta * one
         quarter = 0.25 * zeta
@@ -266,8 +289,10 @@
         y = first - second
         wet_u = jnp.where(wet, vel_u, 0.0)
         wet_v = jnp.where(wet, vel_v, 0.0)
-        vel_u = (wet_u - 0.1 * wet_v) + (prev_col(x) - x) + (third - row_above(third))
-        vel_v = (wet_v + 0.1 * wet_u) + (prev_col(third) - third) + (y - row_above(y))
+        rest_u = (wet_u - 0.1 * wet_v) - x + (third - row_above(third))
+        rest_v = (wet_v + 0.1 * wet_u) - third + (y - row_above(y))
+        vel_u = rest_u + prev_col(x)
+        vel_v = rest_v + prev_col(third)
 
     shift = lax.rem(total - COLS * me, total)
     rows = [pltpu.roll(value, shift, 1)[:, :LANES] for value in (vel_u, vel_v, one, two, shear)]

time: 20.9 us -> 20.6 us (0.986)
  Pallas kernels: 8.67 us -> 8.4 us
    pallas_call x1, Pallas kernels: 2.28 us -> 2 us  [on_device(): pl.pallas_call(functools.partial(fold_kernel, offsets), out_shape=jax.Sha...]
where the time goes in v7:
time: 20.6 us; the launch traced here: 20.5 us
  starting transfers between devices  11.3 us (55%)
  Pallas kernels  8.4 us (41%)
  waiting for transfers between devices  0.67 us (3%)
    ppermute x5, starting transfers between devices, exchange(): lax.ppermute(held, 'lon', [(i, i ^ step) for i in range(count)])  7.79 us
    ppermute x1, starting transfers between devices, on_device(): lax.ppermute(east_send, 'lon', [(i, (i - 1) % count) for i in range(count)])  3.4 us
    pallas_call x1, Pallas kernels, on_device(): pl.pallas_call(edge_kernel, out_shape=(jax.ShapeDtypeStruct(state_shape,...  2.37 us
    pallas_call x1, Pallas kernels, on_device(): pl.pallas_call(pack_kernel, out_shape=(jax.ShapeDtypeStruct((1, STRIP_PAR...  2.35 us
    pallas_call x1, Pallas kernels, on_device(): pl.pallas_call(functools.partial(fold_kernel, offsets), out_shape=jax.Sha...  2 us
    pallas_call x1, Pallas kernels, on_device(): pl.pallas_call(first_inner_kernel, out_shape=(extended[0], *sends), in_sp...  1.06 us
    ppermute x1, waiting for transfers between devices, on_device(): lax.ppermute(east_send, 'lon', [(i, (i - 1) % count) for i in range(count)])  0.66 us
    pallas_call x1, Pallas kernels, on_device(): pl.pallas_call(second_inner_kernel, out_shape=(extended[0], extended[0]),...  0.61 us
  transfers between devices with their start and end apart: 7, of which 1 were waited for; matrix products, arithmetic and copies ran while one was open for 0% of the time, Pallas kernels for 20%

profile of v7, /device:TPU:0, one launch (start us, length us, event | category | flops | bytes accessed | tf_op | source)
XLA Modules:
  0.0 20.5 jit_solution(12409119432541262819)
XLA Ops:
  0.0 2.3 %shard_map.64 = (bf16[1,2,16,128]{3,2,1,0:T(8,128)(2,1)S(1)}, f32[1,2,16,128]{3,2,1,0:T(8,128)S(1)}, f32[5,40,16,128]{3,2,1,0:T(8,128)S(1)}, f32[8,40,16,128]{3,2,1,0:T(8,128)S(1)}, f32[40,16,128]{2,1,0:T(8,128)S(1)}) custom-call(f32[5,256,128]{2,1,0:T(8,128)} %bitcast.10, bf16[8,3,16,2048]{3,2,1,0:T(8,128)(2,1)} %strains_hbm.1, f32[16,2048]{1,0:T(8,128)} %strength_hbm.1, ...), custom_call_target="tpu_custom_call" | custom-call | tf_op jit(solution)/shard_map/pallas_call | solution.py:527
  2.4 0.5 %collective-permute-start = (bf16[1,2,16,128]{3,2,1,0:T(8,128)(2,1)S(1)}, bf16[1,2,16,128]{3,2,1,0:T(8,128)(2,1)S(1)}, u32[]{:S(2)}, u32[]{:S(2)}) collective-permute-start(bf16[1,2,16,128]{3,2,1,0:T(8,128)(2,1)S(1)} %get-tuple-element.20.refs_0_), channel_id=1, source_target_pairs={{0,1},{1,0},{2,3},{3,2},{4,5},{5,4},{6,7},{7,6},{8,9},{9,8},{10,11... | collective-permute-start | bytes 24584 | tf_op jit(solution)/shard_map/ppermute | solution.py:503
  2.9 1.1 %shard_map.65 = (f32[5,40,16,128]{3,2,1,0:T(8,128)S(1)}, bf16[56,16,128]{2,1,0:T(8,128)(2,1)S(1)}, bf16[43,16,128]{2,1,0:T(8,128)(2,1)S(1)}) custom-call(f32[5,40,16,128]{3,2,1,0:T(8,128)S(1)} %get-tuple-element.21.state_in, f32[8,40,16,128]{3,2,1,0:T(8,128)S(1)} %get-tuple-element.22.zeta.zeta_in, ...), custom_call_target="tpu_custom_call", output_to_operand_aliasing={{0}: (0, {})} | custom-call | tf_op jit(solution)/shard_map/pallas_call | solution.py:554
  3.9 0.0 collective-permute-done.refs_1_
  4.0 0.1 collective-permute-start.5
  4.1 4.0 %collective-permute-start.1 = (bf16[2,2,16,128]{3,2,1,0:T(8,128)(2,1)S(1)}, bf16[2,2,16,128]{3,2,1,0:T(8,128)(2,1)S(1)}, u32[]{:S(2)}, u32[]{:S(2)}) collective-permute-start(bf16[2,2,16,128]{3,2,1,0:T(8,128)(2,1)S(1)} %get-tuple-element.26.refs_0_), channel_id=1, source_target_pairs={{0,8},{1,9},{2,10},{3,11},{4,12},{5,13},{6,14},{7,15},{8,0},{9,1},... | collective-permute-start | bytes 49160 | tf_op jit(solution)/shard_map/ppermute | solution.py:503
  8.1 1.3 %collective-permute-start.2 = (bf16[2,2,16,128]{3,2,1,0:T(8,128)(2,1)S(1)}, bf16[2,2,16,128]{3,2,1,0:T(8,128)(2,1)S(1)}, u32[]{:S(2)}, u32[]{:S(2)}) collective-permute-start(bf16[2,2,16,128]{3,2,1,0:T(8,128)(2,1)S(1)} %get-tuple-element.26.refs_0_), channel_id=1, source_target_pairs={{0,12},{1,13},{2,14},{3,15},{4,8},{5,9},{6,10},{7,11},{8,4},{9,5},... | collective-permute-start | bytes 49160 | tf_op jit(solution)/shard_map/ppermute | solution.py:503
  9.5 0.2 %collective-permute-start.3 = (bf16[2,2,16,128]{3,2,1,0:T(8,128)(2,1)S(1)}, bf16[2,2,16,128]{3,2,1,0:T(8,128)(2,1)S(1)}, u32[]{:S(2)}, u32[]{:S(2)}) collective-permute-start(bf16[2,2,16,128]{3,2,1,0:T(8,128)(2,1)S(1)} %get-tuple-element.26.refs_0_), channel_id=1, source_target_pairs={{0,4},{1,5},{2,6},{3,7},{4,0},{5,1},{6,2},{7,3},{8,12},{9,13},{10,... | collective-permute-start | bytes 49160 | tf_op jit(solution)/shard_map/ppermute | solution.py:503
  9.7 3.4 %collective-permute-start.6 = (bf16[43,16,128]{2,1,0:T(8,128)(2,1)S(1)}, bf16[43,16,128]{2,1,0:T(8,128)(2,1)S(1)}, u32[]{:S(2)}, u32[]{:S(2)}) collective-permute-start(bf16[43,16,128]{2,1,0:T(8,128)(2,1)S(1)} %get-tuple-element.32), channel_id=1, source_target_pairs={{0,15},{1,0},{2,1},{3,2},{4,3},{5,4},{6,5},{7,6},{8,7},{9,8},{10,9... | collective-permute-start | bytes 528392 | tf_op jit(solution)/shard_map/ppermute | solution.py:564
  13.1 0.6 %shard_map.67 = (f32[5,40,16,128]{3,2,1,0:T(8,128)S(1)}, f32[5,40,16,128]{3,2,1,0:T(8,128)S(1)}) custom-call(f32[5,40,16,128]{3,2,1,0:T(8,128)S(1)} %get-tuple-element.27.state_in, f32[8,40,16,128]{3,2,1,0:T(8,128)S(1)} %get-tuple-element.22.zeta.zeta_in, f32[40,16,128]{2,1,0:T(8,128)S(1)} %get-tuple-element.23.weight.mass_in), custom_call_target="tpu_custom_call", output_to_operand_aliasing={{1}: (0, {})} | custom-call | flops 1500000000 | tf_op jit(solution)/shard_map/pallas_call | solution.py:565
  13.7 0.0 collective-permute-done.1.refs_1_
  13.7 0.0 collective-permute-done.2.refs_2_
  13.7 0.0 collective-permute-done.3.refs_3_
  13.8 1.7 %collective-permute-start.4 = (bf16[8,2,16,128]{3,2,1,0:T(8,128)(2,1)S(1)}, bf16[8,2,16,128]{3,2,1,0:T(8,128)(2,1)S(1)}, u32[]{:S(2)}, u32[]{:S(2)}) collective-permute-start(bf16[8,2,16,128]{3,2,1,0:T(8,128)(2,1)S(1)} %get-tuple-element.29.refs_0_), channel_id=1, source_target_pairs={{0,2},{1,3},{2,0},{3,1},{4,6},{5,7},{6,4},{7,5},{8,10},{9,11},{10,... | collective-permute-start | bytes 196616 | tf_op jit(solution)/shard_map/ppermute | solution.py:503
  15.4 0.7 %collective-permute-done.6.east = bf16[43,16,128]{2,1,0:T(8,128)(2,1)S(1)} collective-permute-done((bf16[43,16,128]{2,1,0:T(8,128)(2,1)S(1)}, bf16[43,16,128]{2,1,0:T(8,128)(2,1)S(1)}, u32[]{:S(2)}, u32[]{:S(2)}) %collective-permute-start.6) | collective-permute-done | bytes 176160 | tf_op jit(solution)/shard_map/ppermute | solution.py:564
  16.1 0.0 collective-permute-done.5.west
  16.1 2.4 %shard_map.69 = (f32[5,256,128]{2,1,0:T(8,128)S(1)}, f32[5,40,16,128]{3,2,1,0:T(8,128)S(1)}, f32[8,40,16,128]{3,2,1,0:T(8,128)S(1)}, f32[40,16,128]{2,1,0:T(8,128)S(1)}) custom-call(bf16[56,16,128]{2,1,0:T(8,128)(2,1)S(1)} %collective-permute-done.5.west, ...), custom_call_target="tpu_custom_call", output_to_operand_aliasing={{1}: (2, {}), {2}: (3, {}), {3}: (4, {})} | custom-call | tf_op jit(solution)/shard_map/pallas_call | solution.py:578
  18.4 0.0 collective-permute-done.4.refs_1_
  18.5 2.0 %shard_map.70 = f32[5,256,128]{2,1,0:T(8,128)} custom-call(bf16[8,2,16,128]{3,2,1,0:T(8,128)(2,1)S(1)} %get-tuple-element.29.refs_0_, bf16[8,2,16,128]{3,2,1,0:T(8,128)(2,1)S(1)} %collective-permute-done.4.refs_1_, f32[1,2,16,128]{3,2,1,0:T(8,128)S(1)} %get-tuple-element.30.refs_2_, f32[5,256,128]{2,1,0:T(8,128)S(1)} %get-tuple-element.34.refs_3_), custom_call_target="tpu_custom_call" | custom-call | tf_op jit(solution)/shard_map/pallas_call | solution.py:586
  (2 shorter events, 0.0 us)
Async XLA Ops:
  2.4 1.6 %collective-permute-start = (bf16[1,2,16,128]{3,2,1,0:T(8,128)(2,1)S(1)}, bf16[1,2,16,128]{3,2,1,0:T(8,128)(2,1)S(1)}, u32[]{:S(2)}, u32[]{:S(2)}) collective-permute-start(bf16[1,2,16,128]{3,2,1,0:T(8,128)(2,1)S(1)} %get-tuple-element.20.refs_0_), channel_id=1, source_target_pairs={{0,1},{1,0},{2,3},{3,2},{4,5},{5,4},{6,7},{7,6},{8,9},{9,8},{10,11... | collective-permute-start | bytes 24584 | tf_op jit(solution)/shard_map/ppermute | solution.py:503
  4.0 12.1 %collective-permute-start.5 = (bf16[56,16,128]{2,1,0:T(8,128)(2,1)S(1)}, bf16[56,16,128]{2,1,0:T(8,128)(2,1)S(1)}, u32[]{:S(2)}, u32[]{:S(2)}) collective-permute-start(bf16[56,16,128]{2,1,0:T(8,128)(2,1)S(1)} %get-tuple-element.31), channel_id=1, source_target_pairs={{0,1},{1,2},{2,3},{3,4},{4,5},{5,6},{6,7},{7,8},{8,9},{9,10},{10,1... | collective-permute-start | bytes 688136 | tf_op jit(solution)/shard_map/ppermute | solution.py:563
  4.1 9.6 %collective-permute-start.1 = (bf16[2,2,16,128]{3,2,1,0:T(8,128)(2,1)S(1)}, bf16[2,2,16,128]{3,2,1,0:T(8,128)(2,1)S(1)}, u32[]{:S(2)}, u32[]{:S(2)}) collective-permute-start(bf16[2,2,16,128]{3,2,1,0:T(8,128)(2,1)S(1)} %get-tuple-element.26.refs_0_), channel_id=1, source_target_pairs={{0,8},{1,9},{2,10},{3,11},{4,12},{5,13},{6,14},{7,15},{8,0},{9,1},... | collective-permute-start | bytes 49160 | tf_op jit(solution)/shard_map/ppermute | solution.py:503
  8.1 5.6 %collective-permute-start.2 = (bf16[2,2,16,128]{3,2,1,0:T(8,128)(2,1)S(1)}, bf16[2,2,16,128]{3,2,1,0:T(8,128)(2,1)S(1)}, u32[]{:S(2)}, u32[]{:S(2)}) collective-permute-start(bf16[2,2,16,128]{3,2,1,0:T(8,128)(2,1)S(1)} %get-tuple-element.26.refs_0_), channel_id=1, source_target_pairs={{0,12},{1,13},{2,14},{3,15},{4,8},{5,9},{6,10},{7,11},{8,4},{9,5},... | collective-permute-start | bytes 49160 | tf_op jit(solution)/shard_map/ppermute | solution.py:503
  9.5 4.3 %collective-permute-start.3 = (bf16[2,2,16,128]{3,2,1,0:T(8,128)(2,1)S(1)}, bf16[2,2,16,128]{3,2,1,0:T(8,128)(2,1)S(1)}, u32[]{:S(2)}, u32[]{:S(2)}) collective-permute-start(bf16[2,2,16,128]{3,2,1,0:T(8,128)(2,1)S(1)} %get-tuple-element.26.refs_0_), channel_id=1, source_target_pairs={{0,4},{1,5},{2,6},{3,7},{4,0},{5,1},{6,2},{7,3},{8,12},{9,13},{10,... | collective-permute-start | bytes 49160 | tf_op jit(solution)/shard_map/ppermute | solution.py:503
  9.7 6.4 %collective-permute-start.6 = (bf16[43,16,128]{2,1,0:T(8,128)(2,1)S(1)}, bf16[43,16,128]{2,1,0:T(8,128)(2,1)S(1)}, u32[]{:S(2)}, u32[]{:S(2)}) collective-permute-start(bf16[43,16,128]{2,1,0:T(8,128)(2,1)S(1)} %get-tuple-element.32), channel_id=1, source_target_pairs={{0,15},{1,0},{2,1},{3,2},{4,3},{5,4},{6,5},{7,6},{8,7},{9,8},{10,9... | collective-permute-start | bytes 528392 | tf_op jit(solution)/shard_map/ppermute | solution.py:564
  13.8 4.7 %collective-permute-start.4 = (bf16[8,2,16,128]{3,2,1,0:T(8,128)(2,1)S(1)}, bf16[8,2,16,128]{3,2,1,0:T(8,128)(2,1)S(1)}, u32[]{:S(2)}, u32[]{:S(2)}) collective-permute-start(bf16[8,2,16,128]{3,2,1,0:T(8,128)(2,1)S(1)} %get-tuple-element.29.refs_0_), channel_id=1, source_target_pairs={{0,2},{1,3},{2,0},{3,1},{4,6},{5,7},{6,4},{7,5},{8,10},{9,11},{10,... | collective-permute-start | bytes 196616 | tf_op jit(solution)/shard_map/ppermute | solution.py:503

commit v8 on v7

--- a/solution.py
+++ b/solution.py
@@ -94,7 +94,7 @@
         pltpu.make_async_copy(mask_hbm, mask, sems.at[1]),
     ]
     state_copy = pltpu.make_async_copy(state_hbm, state, sems.at[2])
-    late_copies = [
+    first_copies = [
         pltpu.make_async_copy(strength_hbm, strength, sems.at[3]),
         pltpu.make_async_copy(partner_hbm, partner, sems.at[4]),
     ]
@@ -102,8 +102,32 @@
         pltpu.make_async_copy(strains_hbm.at[2 * k : 2 * k + 2], strains.at[2 * k : 2 * k + 2], sems.at[5 + k])
         for k in range(STEPS // 2)
     ]
-    for copy in [*cell_copies, state_copy, *late_copies, *strain_copies]:
+    for copy in [*first_copies, *strain_copies, *cell_copies, state_copy]:
         copy.start()
+
+    for copy in first_copies:
+        copy.wait()
+
+    def cycle_zeta(cycle, step, rows):
+        for group in range(GROUPS):
+            at = slice(LANES * group, LANES * group + LANES)
+            rates = [strains[cycle, k, :, at].astype(jnp.float32) for k in range(3)]
+            zeta = viscosity(rates, strength[:, at])
+            rows[8 * group : 8 * group + 8] = zeta[:8]
+            rows[128 + 8 * group : 136 + 8 * group] = zeta[8:]
+        top[6 + step] = zeta
+        for at in range(8):
+            zeta_out[step, HALO + at] = column_tile(lambda part: rows[part, :], at, 0)
+            zeta_out[step, HALO + 8 + at] = column_tile(lambda part: rows[part, :], at, 1)
+
+    @pl.loop(0, STEPS // 2)
+    def _(turn):
+        pltpu.make_async_copy(
+            strains_hbm.at[pl.ds(2 * turn, 2)], strains.at[pl.ds(2 * turn, 2)], sems.at[5 + turn]
+        ).wait()
+        for part in range(2):
+            cycle = 2 * turn + part
+            cycle_zeta(cycle, STEPS - 1 - cycle, rows.at[part])
 
     for copy in cell_copies:
         copy.wait()
@@ -129,30 +153,6 @@
     for field in range(5):
         top[field, :8] = state[field, 120:128, :]
         top[field, 8:] = state[field, 248:256, :]
-    for copy in late_copies:
-        copy.wait()
-
-    def cycle_zeta(cycle, step, rows):
-        for group in range(GROUPS):
-            at = slice(LANES * group, LANES * group + LANES)
-            rates = [strains[cycle, k, :, at].astype(jnp.float32) for k in range(3)]
-            zeta = viscosity(rates, strength[:, at])
-            rows[8 * group : 8 * group + 8] = zeta[:8]
-            rows[128 + 8 * group : 136 + 8 * group] = zeta[8:]
-        top[6 + step] = zeta
-        for at in range(8):
-            zeta_out[step, HALO + at] = column_tile(lambda part: rows[part, :], at, 0)
-            zeta_out[step, HALO + 8 + at] = column_tile(lambda part: rows[part, :], at, 1)
-
-    @pl.loop(0, STEPS // 2)
-    def _(turn):
-        pltpu.make_async_copy(
-            strains_hbm.at[pl.ds(2 * turn, 2)], strains.at[pl.ds(2 * turn, 2)], sems.at[5 + turn]
-        ).wait()
-        for part in range(2):
-            cycle = 2 * turn + part
-            cycle_zeta(cycle, STEPS - 1 - cycle, rows.at[part])
-
     lane = lax.broadcasted_iota(jnp.int32, (COLS, LANES), 1)
     row_at = lax.broadcasted_iota(jnp.int32, (COLS, LANES), 0)
     place = jnp.zeros((COLS, LANES), jnp.int32)

time: 20.6 us -> 20.5 us (level)
  no operation moved by 1% of the time
where the time goes in v8:
time: 20.5 us; the launch traced here: 20.4 us
  starting transfers between devices  11.3 us (55%)
  Pallas kernels  8.3 us (40%)
  waiting for transfers between devices  0.67 us (3%)
    ppermute x5, starting transfers between devices, exchange(): lax.ppermute(held, 'lon', [(i, i ^ step) for i in range(count)])  7.79 us
    ppermute x1, starting transfers between devices, on_device(): lax.ppermute(east_send, 'lon', [(i, (i - 1) % count) for i in range(count)])  3.4 us
    pallas_call x1, Pallas kernels, on_device(): pl.pallas_call(edge_kernel, out_shape=(jax.ShapeDtypeStruct(state_shape,...  2.37 us
    pallas_call x1, Pallas kernels, on_device(): pl.pallas_call(pack_kernel, out_shape=(jax.ShapeDtypeStruct((1, STRIP_PAR...  2.24 us
    pallas_call x1, Pallas kernels, on_device(): pl.pallas_call(functools.partial(fold_kernel, offsets), out_shape=jax.Sha...  2 us
    pallas_call x1, Pallas kernels, on_device(): pl.pallas_call(first_inner_kernel, out_shape=(extended[0], *sends), in_sp...  1.06 us
    ppermute x1, waiting for transfers between devices, on_device(): lax.ppermute(east_send, 'lon', [(i, (i - 1) % count) for i in range(count)])  0.66 us
    pallas_call x1, Pallas kernels, on_device(): pl.pallas_call(second_inner_kernel, out_shape=(extended[0], extended[0]),...  0.61 us
  transfers between devices with their start and end apart: 7, of which 1 were waited for; matrix products, arithmetic and copies ran while one was open for 0% of the time, Pallas kernels for 20%

profile of v8, /device:TPU:0, one launch (start us, length us, event | category | flops | bytes accessed | tf_op | source)
XLA Modules:
  0.0 20.4 jit_solution(7083892373087517625)
XLA Ops:
  0.0 2.2 %shard_map.64 = (bf16[1,2,16,128]{3,2,1,0:T(8,128)(2,1)S(1)}, f32[1,2,16,128]{3,2,1,0:T(8,128)S(1)}, f32[5,40,16,128]{3,2,1,0:T(8,128)S(1)}, f32[8,40,16,128]{3,2,1,0:T(8,128)S(1)}, f32[40,16,128]{2,1,0:T(8,128)S(1)}) custom-call(f32[5,256,128]{2,1,0:T(8,128)} %bitcast.10, bf16[8,3,16,2048]{3,2,1,0:T(8,128)(2,1)} %strains_hbm.1, f32[16,2048]{1,0:T(8,128)} %strength_hbm.1, ...), custom_call_target="tpu_custom_call" | custom-call | tf_op jit(solution)/shard_map/pallas_call | solution.py:527
  2.3 0.5 %collective-permute-start = (bf16[1,2,16,128]{3,2,1,0:T(8,128)(2,1)S(1)}, bf16[1,2,16,128]{3,2,1,0:T(8,128)(2,1)S(1)}, u32[]{:S(2)}, u32[]{:S(2)}) collective-permute-start(bf16[1,2,16,128]{3,2,1,0:T(8,128)(2,1)S(1)} %get-tuple-element.20.refs_0_), channel_id=1, source_target_pairs={{0,1},{1,0},{2,3},{3,2},{4,5},{5,4},{6,7},{7,6},{8,9},{9,8},{10,11... | collective-permute-start | bytes 24584 | tf_op jit(solution)/shard_map/ppermute | solution.py:503
  2.8 1.1 %shard_map.65 = (f32[5,40,16,128]{3,2,1,0:T(8,128)S(1)}, bf16[56,16,128]{2,1,0:T(8,128)(2,1)S(1)}, bf16[43,16,128]{2,1,0:T(8,128)(2,1)S(1)}) custom-call(f32[5,40,16,128]{3,2,1,0:T(8,128)S(1)} %get-tuple-element.21.state_in, f32[8,40,16,128]{3,2,1,0:T(8,128)S(1)} %get-tuple-element.22.zeta.zeta_in, ...), custom_call_target="tpu_custom_call", output_to_operand_aliasing={{0}: (0, {})} | custom-call | tf_op jit(solution)/shard_map/pallas_call | solution.py:554
  3.8 0.0 collective-permute-done.refs_1_
  3.9 0.1 collective-permute-start.5
  4.0 4.0 %collective-permute-start.1 = (bf16[2,2,16,128]{3,2,1,0:T(8,128)(2,1)S(1)}, bf16[2,2,16,128]{3,2,1,0:T(8,128)(2,1)S(1)}, u32[]{:S(2)}, u32[]{:S(2)}) collective-permute-start(bf16[2,2,16,128]{3,2,1,0:T(8,128)(2,1)S(1)} %get-tuple-element.26.refs_0_), channel_id=1, source_target_pairs={{0,8},{1,9},{2,10},{3,11},{4,12},{5,13},{6,14},{7,15},{8,0},{9,1},... | collective-permute-start | bytes 49160 | tf_op jit(solution)/shard_map/ppermute | solution.py:503
  8.0 1.3 %collective-permute-start.2 = (bf16[2,2,16,128]{3,2,1,0:T(8,128)(2,1)S(1)}, bf16[2,2,16,128]{3,2,1,0:T(8,128)(2,1)S(1)}, u32[]{:S(2)}, u32[]{:S(2)}) collective-permute-start(bf16[2,2,16,128]{3,2,1,0:T(8,128)(2,1)S(1)} %get-tuple-element.26.refs_0_), channel_id=1, source_target_pairs={{0,12},{1,13},{2,14},{3,15},{4,8},{5,9},{6,10},{7,11},{8,4},{9,5},... | collective-permute-start | bytes 49160 | tf_op jit(solution)/shard_map/ppermute | solution.py:503
  9.4 0.2 %collective-permute-start.3 = (bf16[2,2,16,128]{3,2,1,0:T(8,128)(2,1)S(1)}, bf16[2,2,16,128]{3,2,1,0:T(8,128)(2,1)S(1)}, u32[]{:S(2)}, u32[]{:S(2)}) collective-permute-start(bf16[2,2,16,128]{3,2,1,0:T(8,128)(2,1)S(1)} %get-tuple-element.26.refs_0_), channel_id=1, source_target_pairs={{0,4},{1,5},{2,6},{3,7},{4,0},{5,1},{6,2},{7,3},{8,12},{9,13},{10,... | collective-permute-start | bytes 49160 | tf_op jit(solution)/shard_map/ppermute | solution.py:503
  9.6 3.4 %collective-permute-start.6 = (bf16[43,16,128]{2,1,0:T(8,128)(2,1)S(1)}, bf16[43,16,128]{2,1,0:T(8,128)(2,1)S(1)}, u32[]{:S(2)}, u32[]{:S(2)}) collective-permute-start(bf16[43,16,128]{2,1,0:T(8,128)(2,1)S(1)} %get-tuple-element.32), channel_id=1, source_target_pairs={{0,15},{1,0},{2,1},{3,2},{4,3},{5,4},{6,5},{7,6},{8,7},{9,8},{10,9... | collective-permute-start | bytes 528392 | tf_op jit(solution)/shard_map/ppermute | solution.py:564
  13.0 0.6 %shard_map.67 = (f32[5,40,16,128]{3,2,1,0:T(8,128)S(1)}, f32[5,40,16,128]{3,2,1,0:T(8,128)S(1)}) custom-call(f32[5,40,16,128]{3,2,1,0:T(8,128)S(1)} %get-tuple-element.27.state_in, f32[8,40,16,128]{3,2,1,0:T(8,128)S(1)} %get-tuple-element.22.zeta.zeta_in, f32[40,16,128]{2,1,0:T(8,128)S(1)} %get-tuple-element.23.weight.mass_in), custom_call_target="tpu_custom_call", output_to_operand_aliasing={{1}: (0, {})} | custom-call | flops 1500000000 | tf_op jit(solution)/shard_map/pallas_call | solution.py:565
  13.6 0.0 collective-permute-done.1.refs_1_
  13.6 0.0 collective-permute-done.2.refs_2_
  13.6 0.0 collective-permute-done.3.refs_3_
  13.7 1.7 %collective-permute-start.4 = (bf16[8,2,16,128]{3,2,1,0:T(8,128)(2,1)S(1)}, bf16[8,2,16,128]{3,2,1,0:T(8,128)(2,1)S(1)}, u32[]{:S(2)}, u32[]{:S(2)}) collective-permute-start(bf16[8,2,16,128]{3,2,1,0:T(8,128)(2,1)S(1)} %get-tuple-element.29.refs_0_), channel_id=1, source_target_pairs={{0,2},{1,3},{2,0},{3,1},{4,6},{5,7},{6,4},{7,5},{8,10},{9,11},{10,... | collective-permute-start | bytes 196616 | tf_op jit(solution)/shard_map/ppermute | solution.py:503
  15.3 0.7 %collective-permute-done.6.east = bf16[43,16,128]{2,1,0:T(8,128)(2,1)S(1)} collective-permute-done((bf16[43,16,128]{2,1,0:T(8,128)(2,1)S(1)}, bf16[43,16,128]{2,1,0:T(8,128)(2,1)S(1)}, u32[]{:S(2)}, u32[]{:S(2)}) %collective-permute-start.6) | collective-permute-done | bytes 176160 | tf_op jit(solution)/shard_map/ppermute | solution.py:564
  16.0 0.0 collective-permute-done.5.west
  16.0 2.4 %shard_map.69 = (f32[5,256,128]{2,1,0:T(8,128)S(1)}, f32[5,40,16,128]{3,2,1,0:T(8,128)S(1)}, f32[8,40,16,128]{3,2,1,0:T(8,128)S(1)}, f32[40,16,128]{2,1,0:T(8,128)S(1)}) custom-call(bf16[56,16,128]{2,1,0:T(8,128)(2,1)S(1)} %collective-permute-done.5.west, ...), custom_call_target="tpu_custom_call", output_to_operand_aliasing={{1}: (2, {}), {2}: (3, {}), {3}: (4, {})} | custom-call | tf_op jit(solution)/shard_map/pallas_call | solution.py:578
  18.3 0.0 collective-permute-done.4.refs_1_
  18.4 2.0 %shard_map.70 = f32[5,256,128]{2,1,0:T(8,128)} custom-call(bf16[8,2,16,128]{3,2,1,0:T(8,128)(2,1)S(1)} %get-tuple-element.29.refs_0_, bf16[8,2,16,128]{3,2,1,0:T(8,128)(2,1)S(1)} %collective-permute-done.4.refs_1_, f32[1,2,16,128]{3,2,1,0:T(8,128)S(1)} %get-tuple-element.30.refs_2_, f32[5,256,128]{2,1,0:T(8,128)S(1)} %get-tuple-element.34.refs_3_), custom_call_target="tpu_custom_call" | custom-call | tf_op jit(solution)/shard_map/pallas_call | solution.py:586
  (2 shorter events, 0.0 us)
Async XLA Ops:
  2.3 1.6 %collective-permute-start = (bf16[1,2,16,128]{3,2,1,0:T(8,128)(2,1)S(1)}, bf16[1,2,16,128]{3,2,1,0:T(8,128)(2,1)S(1)}, u32[]{:S(2)}, u32[]{:S(2)}) collective-permute-start(bf16[1,2,16,128]{3,2,1,0:T(8,128)(2,1)S(1)} %get-tuple-element.20.refs_0_), channel_id=1, source_target_pairs={{0,1},{1,0},{2,3},{3,2},{4,5},{5,4},{6,7},{7,6},{8,9},{9,8},{10,11... | collective-permute-start | bytes 24584 | tf_op jit(solution)/shard_map/ppermute | solution.py:503
  3.9 12.1 %collective-permute-start.5 = (bf16[56,16,128]{2,1,0:T(8,128)(2,1)S(1)}, bf16[56,16,128]{2,1,0:T(8,128)(2,1)S(1)}, u32[]{:S(2)}, u32[]{:S(2)}) collective-permute-start(bf16[56,16,128]{2,1,0:T(8,128)(2,1)S(1)} %get-tuple-element.31), channel_id=1, source_target_pairs={{0,1},{1,2},{2,3},{3,4},{4,5},{5,6},{6,7},{7,8},{8,9},{9,10},{10,1... | collective-permute-start | bytes 688136 | tf_op jit(solution)/shard_map/ppermute | solution.py:563
  4.0 9.6 %collective-permute-start.1 = (bf16[2,2,16,128]{3,2,1,0:T(8,128)(2,1)S(1)}, bf16[2,2,16,128]{3,2,1,0:T(8,128)(2,1)S(1)}, u32[]{:S(2)}, u32[]{:S(2)}) collective-permute-start(bf16[2,2,16,128]{3,2,1,0:T(8,128)(2,1)S(1)} %get-tuple-element.26.refs_0_), channel_id=1, source_target_pairs={{0,8},{1,9},{2,10},{3,11},{4,12},{5,13},{6,14},{7,15},{8,0},{9,1},... | collective-permute-start | bytes 49160 | tf_op jit(solution)/shard_map/ppermute | solution.py:503
  8.0 5.6 %collective-permute-start.2 = (bf16[2,2,16,128]{3,2,1,0:T(8,128)(2,1)S(1)}, bf16[2,2,16,128]{3,2,1,0:T(8,128)(2,1)S(1)}, u32[]{:S(2)}, u32[]{:S(2)}) collective-permute-start(bf16[2,2,16,128]{3,2,1,0:T(8,128)(2,1)S(1)} %get-tuple-element.26.refs_0_), channel_id=1, source_target_pairs={{0,12},{1,13},{2,14},{3,15},{4,8},{5,9},{6,10},{7,11},{8,4},{9,5},... | collective-permute-start | bytes 49160 | tf_op jit(solution)/shard_map/ppermute | solution.py:503
  9.4 4.3 %collective-permute-start.3 = (bf16[2,2,16,128]{3,2,1,0:T(8,128)(2,1)S(1)}, bf16[2,2,16,128]{3,2,1,0:T(8,128)(2,1)S(1)}, u32[]{:S(2)}, u32[]{:S(2)}) collective-permute-start(bf16[2,2,16,128]{3,2,1,0:T(8,128)(2,1)S(1)} %get-tuple-element.26.refs_0_), channel_id=1, source_target_pairs={{0,4},{1,5},{2,6},{3,7},{4,0},{5,1},{6,2},{7,3},{8,12},{9,13},{10,... | collective-permute-start | bytes 49160 | tf_op jit(solution)/shard_map/ppermute | solution.py:503
  9.6 6.4 %collective-permute-start.6 = (bf16[43,16,128]{2,1,0:T(8,128)(2,1)S(1)}, bf16[43,16,128]{2,1,0:T(8,128)(2,1)S(1)}, u32[]{:S(2)}, u32[]{:S(2)}) collective-permute-start(bf16[43,16,128]{2,1,0:T(8,128)(2,1)S(1)} %get-tuple-element.32), channel_id=1, source_target_pairs={{0,15},{1,0},{2,1},{3,2},{4,3},{5,4},{6,5},{7,6},{8,7},{9,8},{10,9... | collective-permute-start | bytes 528392 | tf_op jit(solution)/shard_map/ppermute | solution.py:564
  13.7 4.7 %collective-permute-start.4 = (bf16[8,2,16,128]{3,2,1,0:T(8,128)(2,1)S(1)}, bf16[8,2,16,128]{3,2,1,0:T(8,128)(2,1)S(1)}, u32[]{:S(2)}, u32[]{:S(2)}) collective-permute-start(bf16[8,2,16,128]{3,2,1,0:T(8,128)(2,1)S(1)} %get-tuple-element.29.refs_0_), channel_id=1, source_target_pairs={{0,2},{1,3},{2,0},{3,1},{4,6},{5,7},{6,4},{7,5},{8,10},{9,11},{10,... | collective-permute-start | bytes 196616 | tf_op jit(solution)/shard_map/ppermute | solution.py:503
